TPU v7x, 512 devices: a whole 4x8x8 slice. The times are simulated.
512 devices in a mesh: dp: 16 (over y, core), ctx: 32 (over x, z).
Axes of the slice: x: 4, y: 8, z: 8, core: 2. Of those that a mesh axis runs over, the one named last changes fastest.
Arguments:
- inputs: bfloat16 [16, 6144, 1536], P('dp', 'ctx'), may hold values from -6 to 6
- cotangent: bfloat16 [16, 6144, 1536], P('dp', 'ctx'), may hold values from -6 to 6
- conv_kernel: float32 [31, 1536], replicated, may hold values from -1 to 1
- norm_gain: float32 [1536], replicated, may hold values from 0.5 to 1.5
- adapt_down: bfloat16 [64, 1536, 128], P('ctx'), may hold values from -0.15625 to 0.15625
- adapt_up: bfloat16 [64, 128, 1536], P('ctx'), may hold values from -0.5 to 0.5
- segment_lengths: int32 [16, 32, 16], P('dp', 'ctx'), may hold values from 1 to 15, 192 in all within a row
- segment_langs: int32 [16, 32, 16], P('dp', 'ctx'), may hold values from 0 to 63, as said below
- lang_slot: int32 [64], replicated, may hold values from 0 to 63, as said below
Outputs:
- output: bfloat16 [16, 6144, 1536], P('dp', 'ctx')
- grad_input: bfloat16 [16, 6144, 1536], P('dp', 'ctx')
- grad_kernel: float32 [31, 1536], replicated
- grad_gain: float32 [1536], replicated
- grad_down: float32 [64, 1536, 128], P('ctx', 'dp')
- grad_up: float32 [64, 128, 1536], P('ctx', None, 'dp')
Inputs may be any that keep to these rules, and one draw needn't show every extreme that they name: On one device, the 16 segments' adapters lie at different ctx indices: the values lang_slot[segment_langs] // 2 differ. `lang_slot`: A permutation; slot s is kept by ctx index s // 2. `segment_lengths`: each row sums to 192; its largest entry is exactly 15.
All inputs are finite; a program needn't handle non-finite values.
Results may differ from a plain program's by a relative error of at most 0.0055.
Values may be sent and summed in bfloat16 or wider, within the bound.
No kernel may reach another device: no remote copies, remote signals or barrier semaphores. Data moves between devices by JAX's collectives and lax.ppermute only.
A program may use at most 64 MiB of HBM per device.

v0:
```python
import math

import jax
import jax.numpy as jnp
from jax import lax
from jax.sharding import PartitionSpec as P


def extended(cells, sides, width):
    for axis, dim in sides:
        count = lax.axis_size(axis)
        ends = count - 1
        head = lax.slice_in_dim(cells, 0, width, axis=dim)
        tail = lax.slice_in_dim(cells, cells.shape[dim] - width, cells.shape[dim], axis=dim)
        cells = jnp.concatenate(
            [
                lax.ppermute(tail, axis, [(i, (i + 1) % count) for i in range(ends)]),
                cells,
                lax.ppermute(head, axis, [((i + 1) % count, i) for i in range(ends)]),
            ],
            axis=dim,
        )
    return cells


def silu_slope(pre_act):
    sigmoid_val = jax.nn.sigmoid(pre_act)
    return sigmoid_val * (1.0 + pre_act * (1.0 - sigmoid_val))


def gather_rows(source, owner_count, seg_cap, owner_starts, owner_lens):
    position = jnp.arange(seg_cap, dtype=jnp.int32)
    indices = jnp.clip(owner_starts[:, None] + position[None, :], 0, source.shape[0] - 1).reshape(
        -1
    )
    picked = jnp.take(source, indices, axis=0).reshape(owner_count, seg_cap, source.shape[1])
    inside = position[None, :] < owner_lens[:, None]
    return jnp.where(inside[:, :, None], picked, jnp.zeros((), source.dtype))


def local(
    inputs,
    cotangent,
    conv_kernel,
    norm_gain,
    adapt_down,
    adapt_up,
    segment_lengths,
    segment_langs,
    lang_slot,
):
    frame_count = inputs.shape[1]
    feat_width = inputs.shape[2]
    tap_count = conv_kernel.shape[0]
    half_width = tap_count // 2
    lang_dev = adapt_down.shape[0]
    bottleneck = adapt_down.shape[2]
    owner_count = lax.axis_size("ctx")
    owner_index = lax.axis_index("ctx")
    seg_count = segment_lengths.shape[2]
    seg_cap = frame_count * 5 // (4 * seg_count)
    padded = extended(inputs, (("ctx", 1),), half_width)[0].astype(jnp.float32)
    frames_in = inputs[0].astype(jnp.float32)
    conv_out = jnp.zeros_like(frames_in)
    for offset in range(tap_count):
        conv_out = conv_out + conv_kernel[offset] * padded[offset : offset + frame_count]
    summed = frames_in + conv_out
    inv_rms = lax.rsqrt(jnp.mean(summed * summed, axis=-1, keepdims=True) + 1e-06)
    normed = (summed * inv_rms * norm_gain).astype(jnp.bfloat16)
    seg_lens = segment_lengths[0, 0]
    seg_ends = jnp.cumsum(seg_lens)
    seg_starts = seg_ends - seg_lens
    lang_ids = jnp.arange(lang_slot.shape[0], dtype=jnp.int32)
    my_slots = jnp.sum(
        jnp.where(segment_langs[0, 0][:, None] == lang_ids[None, :], lang_slot[None, :], 0), axis=1
    )
    my_owners = my_slots // lang_dev
    owner_ids = jnp.arange(owner_count, dtype=jnp.int32)
    owner_hits = (my_owners[None, :] == owner_ids[:, None]).astype(jnp.int32)
    owner_starts = jnp.sum(owner_hits * seg_starts[None, :], axis=1)
    owner_lens = jnp.sum(owner_hits * seg_lens[None, :], axis=1)
    frame_local = jnp.arange(frame_count, dtype=jnp.int32)
    seg_number = jnp.sum((frame_local[:, None] >= seg_ends[None, :]).astype(jnp.int32), axis=1)
    seg_hot = (seg_number[:, None] == jnp.arange(seg_count, dtype=jnp.int32)[None, :]).astype(
        jnp.int32
    )
    frame_owner = jnp.sum(seg_hot * my_owners[None, :], axis=1)
    frame_pos = frame_local - jnp.sum(seg_hot * seg_starts[None, :], axis=1)
    frame_slot = frame_owner * seg_cap + frame_pos
    lang_table = lax.all_gather(segment_langs, "ctx", axis=1, tiled=True)[0, :, :]
    table_slots = jnp.sum(
        jnp.where(lang_table[:, :, None] == lang_ids[None, None, :], lang_slot[None, None, :], 0),
        axis=2,
    )
    is_mine = table_slots // lang_dev == owner_index
    local_in = jnp.sum(jnp.where(is_mine, table_slots % lang_dev, 0), axis=1)
    selectors = [
        (local_in == adapter_id).astype(jnp.float32)[:, None, None]
        for adapter_id in range(lang_dev)
    ]
    masks_bf = [selector.astype(jnp.bfloat16) for selector in selectors]

    def project_down(row_data):
        return sum(
            (
                selectors[adapter_id]
                * jnp.einsum(
                    "scd,dr->scr",
                    row_data,
                    adapt_down[adapter_id],
                    preferred_element_type=jnp.float32,
                )
                for adapter_id in range(lang_dev)
            )
        )

    def project_up(activated):
        return sum(
            (
                selectors[adapter_id]
                * jnp.einsum(
                    "scr,rd->scd",
                    activated,
                    adapt_up[adapter_id],
                    preferred_element_type=jnp.float32,
                )
                for adapter_id in range(lang_dev)
            )
        )

    send_normed = gather_rows(normed, owner_count, seg_cap, owner_starts, owner_lens)
    received = lax.all_to_all(send_normed, "ctx", split_axis=0, concat_axis=0, tiled=True)
    pre_act = project_down(received)
    activated = jax.nn.silu(pre_act).astype(jnp.bfloat16)
    branch = project_up(activated).astype(jnp.bfloat16)
    returned = lax.all_to_all(branch, "ctx", split_axis=0, concat_axis=0, tiled=True)
    returned, pre_act, activated, received = (returned, pre_act, activated, received)
    branch_frames = jnp.take(returned.reshape(-1, feat_width), frame_slot, axis=0)
    output = (summed + branch_frames.astype(jnp.float32)).astype(jnp.bfloat16)

    def owner_backward(grad_rows, pre_values):
        grad_act = sum(
            (
                selectors[adapter_id]
                * jnp.einsum(
                    "scd,rd->scr",
                    grad_rows,
                    adapt_up[adapter_id],
                    preferred_element_type=jnp.float32,
                )
                for adapter_id in range(lang_dev)
            )
        )
        grad_pre = (grad_act * silu_slope(pre_values)).astype(jnp.bfloat16)
        grad_normed = sum(
            (
                selectors[adapter_id]
                * jnp.einsum(
                    "scr,dr->scd",
                    grad_pre,
                    adapt_down[adapter_id],
                    preferred_element_type=jnp.float32,
                )
                for adapter_id in range(lang_dev)
            )
        ).astype(jnp.bfloat16)
        sent_back = lax.all_to_all(grad_normed, "ctx", split_axis=0, concat_axis=0, tiled=True)
        return (sent_back, grad_pre)

    send_grad = gather_rows(cotangent[0], owner_count, seg_cap, owner_starts, owner_lens)
    again_rows = lax.all_to_all(send_normed, "ctx", split_axis=0, concat_axis=0, tiled=True)
    grad_rows = lax.all_to_all(send_grad, "ctx", split_axis=0, concat_axis=0, tiled=True)
    again_pre = project_down(again_rows)
    sent_back, grad_pre = owner_backward(grad_rows, again_pre)
    grad_back, grad_pre, grad_rows, activated, received = (
        sent_back,
        grad_pre,
        grad_rows,
        jax.nn.silu(again_pre).astype(jnp.bfloat16),
        again_rows,
    )
    grad_parts = jnp.stack(
        [
            jnp.concatenate(
                [
                    jnp.einsum(
                        "scd,scr->dr",
                        received * masks_bf[adapter_id],
                        grad_pre,
                        preferred_element_type=jnp.float32,
                    ),
                    jnp.einsum(
                        "scr,scd->dr",
                        activated * masks_bf[adapter_id],
                        grad_rows,
                        preferred_element_type=jnp.float32,
                    ),
                ],
                axis=1,
            )
            for adapter_id in range(lang_dev)
        ]
    )
    owned_grads = lax.psum_scatter(grad_parts, "dp", scatter_dimension=1, tiled=True)
    grad_frames = jnp.take(grad_back.reshape(-1, feat_width), frame_slot, axis=0).astype(
        jnp.float32
    )
    weighted = norm_gain * grad_frames
    inner_sum = jnp.mean(weighted * summed, axis=-1, keepdims=True)
    grad_sum = (
        cotangent[0].astype(jnp.float32)
        + inv_rms * weighted
        - summed * (inv_rms * inv_rms * inv_rms) * inner_sum
    )
    gain_part = jnp.sum(grad_frames * summed * inv_rms, axis=0)
    grad_pad = extended(grad_sum[None], (("ctx", 1),), half_width)[0]
    grad_input = grad_sum
    for offset in range(tap_count):
        grad_input = (
            grad_input
            + conv_kernel[offset]
            * grad_pad[2 * half_width - offset : 2 * half_width - offset + frame_count]
        )
    kernel_part = jnp.stack(
        [
            jnp.sum(grad_sum * padded[offset : offset + frame_count], axis=0)
            for offset in range(tap_count)
        ]
    )
    kernel_total, gain_total = lax.psum((kernel_part, gain_part), ("dp", "ctx"))
    grad_scale = 1.0 / math.sqrt(lax.axis_size("dp") * owner_count * frame_count)
    grad_down = owned_grads[:, :, :bottleneck] * grad_scale
    grad_up = jnp.transpose(owned_grads[:, :, bottleneck:], (0, 2, 1)) * grad_scale
    return (
        output[None],
        grad_input.astype(jnp.bfloat16)[None],
        kernel_total * grad_scale,
        gain_total * grad_scale,
        grad_down,
        grad_up,
    )


def solution(mesh):
    in_specs = (
        P("dp", "ctx", None),
        P("dp", "ctx", None),
        P(),
        P(),
        P("ctx", None, None),
        P("ctx", None, None),
        P("dp", "ctx", None),
        P("dp", "ctx", None),
        P(),
    )
    out_specs = (
        P("dp", "ctx", None),
        P("dp", "ctx", None),
        P(),
        P(),
        P("ctx", "dp", None),
        P("ctx", None, "dp"),
    )
    return jax.shard_map(local, mesh=mesh, in_specs=in_specs, out_specs=out_specs, check_vma=False)
```

profile of v0, /device:TPU:1, one launch (start us, length us, event | category | flops | bytes accessed | tf_op | source)
XLA Modules:
  0.0 662.1 jit_solution(11168787629438946549)
XLA Ops:
  8.9 4.8 collective-permute-start
  13.7 1.3 collective-permute-start.1
  15.0 1.8 slice_reduce_fusion.30
  17.0 1.5 slice_reduce_fusion.29
  22.7 2.9 gather_fusion.2
  26.2 6.2 multiply_reduce_fusion.31
  33.6 2.9 gather_fusion
  36.5 3.8 broadcast_select_fusion.2
  40.3 1.6 reshape.218
  41.9 2.5 reshape.220
  44.4 2.9 broadcast_select_fusion
  47.3 49.6 %all_to_all.21 = bf16[32,15,1536]{2,1,0:T(8,128)(2,1)S(1)} all-to-all(bf16[32,15,1536]{2,1,0:T(8,128)(2,1)S(1)} %get-tuple-element.119), channel_id=1, replica_groups=mesh['dp'=16,'ctx'=32] {'ctx'}, dimensions={0} | all-to-all | bytes 2949120 | tf_op jit(solution)/shard_map/all_to_all | solution.py:132
  96.9 9.1 %all-to-all-start.2 = ((bf16[32,15,1536]{2,1,0:T(8,128)(2,1)}), bf16[32,15,1536]{2,1,0:T(8,128)(2,1)}, u32[]{:S(2)}, u32[]{:S(2)}) async-start(bf16[32,15,1536]{2,1,0:T(8,128)(2,1)} %get-tuple-element.118), calls=%async_computation.2 | async-start | bytes 3145728 | tf_op jit(solution)/shard_map/all_to_all | solution.py:172
  106.0 60.6 %all_gather.3 = s32[1,32,16]{2,0,1:T(1,128)S(1)} all-gather(s32[1,1,16]{2,0,1:T(1,128)} %bitcast.591), channel_id=1, replica_groups=mesh['dp'=16,'ctx'=32] {'ctx'}, dimensions={1}, use_global_device_ids=true | all-gather | bytes 2112 | tf_op jit(solution)/shard_map/all_gather | solution.py:90
  166.6 1.4 select_reduce_fusion
  168.6 2.2 convolution_multiply_fusion.6
  170.8 1.8 multiply_convert_fusion.1
  173.8 2.0 copy.65
  175.8 5.9 all-to-all-start.1
  181.7 2.7 convolution_multiply_fusion.4
  184.5 2.6 fusion.136
  188.2 2.0 copy.68
  190.2 3.5 convolution_bitcast_fusion.2
  193.7 2.0 convolution_bitcast_fusion.3
  195.7 13.5 %all-to-all-done.1 = bf16[32,15,1536]{2,1,0:T(8,128)(2,1)S(1)} async-done(((bf16[32,15,1536]{2,1,0:T(8,128)(2,1)}), bf16[32,15,1536]{2,1,0:T(8,128)(2,1)S(1)}, u32[]{:S(2)}, u32[]{:S(2)}) %all-to-all-start.1) | async-done | bytes 1474592 | tf_op jit(solution)/shard_map/all_to_all | solution.py:136
  209.2 1.2 copy-done.3
  210.4 11.1 %all-to-all-start.3 = ((bf16[32,15,1536]{2,1,0:T(8,128)(2,1)}), bf16[32,15,1536]{2,1,0:T(8,128)(2,1)}, u32[]{:S(2)}, u32[]{:S(2)}) async-start(bf16[32,15,1536]{2,1,0:T(8,128)(2,1)} %copy.68), calls=%async_computation.3 | async-start | bytes 3145728 | tf_op jit(solution)/shard_map/all_to_all | solution.py:167
  221.8 2.7 convolution_bitcast_fusion
  224.5 1.1 convolution_bitcast_fusion.1
  226.1 1.9 pad_maximum_fusion
  228.0 5.8 copy.73
  233.9 1.3 dynamic-slice
  236.0 128.9 %all-reduce.6.cloned.1.call-done = f32[2,1536,256]{2,0,1:T(2,128)} async-done(((f32[2,1536,256]{2,0,1:T(2,128)}), f32[2,1536,256]{2,0,1:T(2,128)}) %all-reduce.6.cloned.1.call-update) | async-done | bytes 3145744
  364.9 1.1 fusion.167
  367.3 1.6 reshape.219
  369.0 1.9 gather_fusion.1
  370.9 1.6 reshape.221
  372.5 1.9 gather_fusion.3
  374.4 3.6 fusion.12
  378.1 3.8 multiply_reduce_fusion
  381.9 2.0 multiply_reduce_fusion.18
  384.7 2.8 stack.136
  387.5 1.3 collective-permute-start.2
  388.8 4.0 collective-permute-start.3
  392.9 102.5 %psum.15 = f32[1536]{0:T(1024)S(1)} all-reduce(f32[1536]{0:T(1024)S(1)} %copy-done.80), channel_id=1, replica_groups=mesh['dp'=16,'ctx'=32] {'dp','ctx'}, use_global_device_ids=true, to_apply=%region_44.47 | all-reduce | flops 1536 | bytes 12288 | tf_op jit(solution)/shard_map/psum | solution.py:230
  496.3 6.0 fusion.148
  502.3 150.7 %all-reduce.4.cloned.1.call-done = f32[31,1536]{1,0:T(8,128)} async-done(((f32[31,1536]{1,0:T(8,128)}), f32[31,1536]{1,0:T(8,128)}) %all-reduce.4.cloned.1.call-update) | async-done | bytes 190480 | tf_op jit(solution)/shard_map/psum | solution.py:230
  653.1 1.6 broadcast_multiply_fusion
  (267 shorter events, 12.8 us)
Async XLA Ops:
  8.0 14.7 %copy-start = (bf16[1,192,1536]{2,1,0:T(8,128)(2,1)S(1)}, bf16[1,192,1536]{2,1,0:T(8,128)(2,1)}, u32[]{:S(2)}) copy-start(bf16[1,192,1536]{2,1,0:T(8,128)(2,1)} %param.14) | copy-start | bytes 1769476
  8.9 16.8 %collective-permute-start = (bf16[1,15,1536]{2,1,0:T(8,128)(2,1)S(1)}, bf16[1,15,1536]{2,1,0:T(8,128)(2,1)S(1)}, u32[]{:S(2)}, u32[]{:S(2)}) collective-permute-start(bf16[1,15,1536]{2,1,0:T(8,128)(2,1)S(1)} %get-tuple-element.116), channel_id=1, source_target_pairs={{0,1},{1,2},{2,3},{3,4},{4,5},{5,6},{6,7},{7,8},{8,9},{9,10},{10,1... | collective-permute-start | bytes 138248 | tf_op jit(solution)/shard_map/ppermute | solution.py:17
  13.7 11.9 %collective-permute-start.1 = (bf16[1,15,1536]{2,1,0:T(8,128)(2,1)S(1)}, bf16[1,15,1536]{2,1,0:T(8,128)(2,1)S(1)}, u32[]{:S(2)}, u32[]{:S(2)}) collective-permute-start(bf16[1,15,1536]{2,1,0:T(8,128)(2,1)S(1)} %get-tuple-element.117), channel_id=1, source_target_pairs={{1,0},{2,1},{3,2},{4,3},{5,4},{6,5},{7,6},{8,7},{9,8},{10,9},{11,1... | collective-permute-start | bytes 138248 | tf_op jit(solution)/shard_map/ppermute | solution.py:19
  16.8 9.0 %copy-start.20 = (f32[1536]{0:T(1024)}, f32[1536]{0:T(1024)S(1)}, u32[]{:S(2)}) copy-start(f32[1536]{0:T(1024)S(1)} %get-tuple-element.72) | copy-start | bytes 18436
  16.8 9.0 %copy-start.22 = (f32[1536]{0:T(1024)}, f32[1536]{0:T(1024)S(1)}, u32[]{:S(2)}) copy-start(f32[1536]{0:T(1024)S(1)} %get-tuple-element.73) | copy-start | bytes 18436
  16.9 9.0 %copy-start.24 = (f32[1536]{0:T(1024)}, f32[1536]{0:T(1024)S(1)}, u32[]{:S(2)}) copy-start(f32[1536]{0:T(1024)S(1)} %get-tuple-element.74) | copy-start | bytes 18436
  16.9 9.0 %copy-start.26 = (f32[1536]{0:T(1024)}, f32[1536]{0:T(1024)S(1)}, u32[]{:S(2)}) copy-start(f32[1536]{0:T(1024)S(1)} %get-tuple-element.75) | copy-start | bytes 18436
  16.9 9.0 %copy-start.28 = (f32[1536]{0:T(1024)}, f32[1536]{0:T(1024)S(1)}, u32[]{:S(2)}) copy-start(f32[1536]{0:T(1024)S(1)} %get-tuple-element.76) | copy-start | bytes 18436
  16.9 9.0 %copy-start.30 = (f32[1536]{0:T(1024)}, f32[1536]{0:T(1024)S(1)}, u32[]{:S(2)}) copy-start(f32[1536]{0:T(1024)S(1)} %get-tuple-element.77) | copy-start | bytes 18436
  16.9 9.0 %copy-start.32 = (f32[1536]{0:T(1024)}, f32[1536]{0:T(1024)S(1)}, u32[]{:S(2)}) copy-start(f32[1536]{0:T(1024)S(1)} %get-tuple-element.78) | copy-start | bytes 18436
  96.9 73.9 %copy-start.6 = (bf16[32,15,1536]{2,1,0:T(8,128)(2,1)}, bf16[32,15,1536]{2,1,0:T(8,128)(2,1)S(1)}, u32[]{:S(2)}) copy-start(bf16[32,15,1536]{2,1,0:T(8,128)(2,1)S(1)} %all_to_all.21) | copy-start | bytes 4423684
  96.9 78.8 %all-to-all-start.2 = ((bf16[32,15,1536]{2,1,0:T(8,128)(2,1)}), bf16[32,15,1536]{2,1,0:T(8,128)(2,1)}, u32[]{:S(2)}, u32[]{:S(2)}) async-start(bf16[32,15,1536]{2,1,0:T(8,128)(2,1)} %get-tuple-element.118), calls=%async_computation.2 | async-start | bytes 3145728 | tf_op jit(solution)/shard_map/all_to_all | solution.py:172
  175.8 33.5 %all-to-all-start.1 = ((bf16[32,15,1536]{2,1,0:T(8,128)(2,1)}), bf16[32,15,1536]{2,1,0:T(8,128)(2,1)S(1)}, u32[]{:S(2)}, u32[]{:S(2)}) async-start(bf16[32,15,1536]{2,1,0:T(8,128)(2,1)} %copy.65), calls=%async_computation.1 | async-start | bytes 3145728 | tf_op jit(solution)/shard_map/all_to_all | solution.py:136
  210.4 160.5 %all-to-all-start.3 = ((bf16[32,15,1536]{2,1,0:T(8,128)(2,1)}), bf16[32,15,1536]{2,1,0:T(8,128)(2,1)}, u32[]{:S(2)}, u32[]{:S(2)}) async-start(bf16[32,15,1536]{2,1,0:T(8,128)(2,1)} %copy.68), calls=%async_computation.3 | async-start | bytes 3145728 | tf_op jit(solution)/shard_map/all_to_all | solution.py:167
  221.5 143.5 %all-reduce.6.cloned.1.call-start = ((), (), s32[]{:S(2)}) async-start(), calls=%async_computation.5 | async-start | bytes 6291456
  233.8 419.3 %all-reduce.4.cloned.1.call-start = ((), (), s32[]{:S(2)}) async-start(), calls=%async_computation.4 | async-start | bytes 393216 | tf_op jit(solution)/shard_map/psum | solution.py:230
  384.0 112.0 %copy-start.21 = (f32[1536]{0:T(1024)S(1)}, f32[1536]{0:T(1024)}, u32[]{:S(2)}) copy-start(f32[1536]{0:T(1024)} %copy-done.20) | copy-start | bytes 18436
  384.0 112.0 %copy-start.23 = (f32[1536]{0:T(1024)S(1)}, f32[1536]{0:T(1024)}, u32[]{:S(2)}) copy-start(f32[1536]{0:T(1024)} %copy-done.22) | copy-start | bytes 18436
  384.0 112.0 %copy-start.25 = (f32[1536]{0:T(1024)S(1)}, f32[1536]{0:T(1024)}, u32[]{:S(2)}) copy-start(f32[1536]{0:T(1024)} %copy-done.24) | copy-start | bytes 18436
  384.0 112.0 %copy-start.27 = (f32[1536]{0:T(1024)S(1)}, f32[1536]{0:T(1024)}, u32[]{:S(2)}) copy-start(f32[1536]{0:T(1024)} %copy-done.26) | copy-start | bytes 18436
  384.0 112.0 %copy-start.29 = (f32[1536]{0:T(1024)S(1)}, f32[1536]{0:T(1024)}, u32[]{:S(2)}) copy-start(f32[1536]{0:T(1024)} %copy-done.28) | copy-start | bytes 18436
  384.0 112.0 %copy-start.31 = (f32[1536]{0:T(1024)S(1)}, f32[1536]{0:T(1024)}, u32[]{:S(2)}) copy-start(f32[1536]{0:T(1024)} %copy-done.30) | copy-start | bytes 18436
  384.1 112.0 %copy-start.33 = (f32[1536]{0:T(1024)S(1)}, f32[1536]{0:T(1024)}, u32[]{:S(2)}) copy-start(f32[1536]{0:T(1024)} %copy-done.32) | copy-start | bytes 18436
  384.1 112.0 %copy-start.35 = (f32[1536]{0:T(1024)S(1)}, f32[1536]{0:T(1024)}, u32[]{:S(2)}) copy-start(f32[1536]{0:T(1024)} %copy-done.34) | copy-start | bytes 18436
  384.1 112.0 %copy-start.37 = (f32[1536]{0:T(1024)S(1)}, f32[1536]{0:T(1024)}, u32[]{:S(2)}) copy-start(f32[1536]{0:T(1024)} %copy-done.36) | copy-start | bytes 18436
  384.1 112.0 %copy-start.39 = (f32[1536]{0:T(1024)S(1)}, f32[1536]{0:T(1024)}, u32[]{:S(2)}) copy-start(f32[1536]{0:T(1024)} %copy-done.38) | copy-start | bytes 18436
  384.1 112.0 %copy-start.41 = (f32[1536]{0:T(1024)S(1)}, f32[1536]{0:T(1024)}, u32[]{:S(2)}) copy-start(f32[1536]{0:T(1024)} %copy-done.40) | copy-start | bytes 18436
  384.1 112.0 %copy-start.43 = (f32[1536]{0:T(1024)S(1)}, f32[1536]{0:T(1024)}, u32[]{:S(2)}) copy-start(f32[1536]{0:T(1024)} %copy-done.42) | copy-start | bytes 18436
  384.1 112.0 %copy-start.45 = (f32[1536]{0:T(1024)S(1)}, f32[1536]{0:T(1024)}, u32[]{:S(2)}) copy-start(f32[1536]{0:T(1024)} %copy-done.44) | copy-start | bytes 18436
  384.1 112.0 %copy-start.47 = (f32[1536]{0:T(1024)S(1)}, f32[1536]{0:T(1024)}, u32[]{:S(2)}) copy-start(f32[1536]{0:T(1024)} %copy-done.46) | copy-start | bytes 18436
  384.1 112.0 %copy-start.49 = (f32[1536]{0:T(1024)S(1)}, f32[1536]{0:T(1024)}, u32[]{:S(2)}) copy-start(f32[1536]{0:T(1024)} %copy-done.48) | copy-start | bytes 18436
  384.1 112.0 %copy-start.51 = (f32[1536]{0:T(1024)S(1)}, f32[1536]{0:T(1024)}, u32[]{:S(2)}) copy-start(f32[1536]{0:T(1024)} %copy-done.50) | copy-start | bytes 18436
  384.2 112.0 %copy-start.53 = (f32[1536]{0:T(1024)S(1)}, f32[1536]{0:T(1024)}, u32[]{:S(2)}) copy-start(f32[1536]{0:T(1024)} %copy-done.52) | copy-start | bytes 18436
  384.2 112.0 %copy-start.55 = (f32[1536]{0:T(1024)S(1)}, f32[1536]{0:T(1024)}, u32[]{:S(2)}) copy-start(f32[1536]{0:T(1024)} %copy-done.54) | copy-start | bytes 18436
  384.2 112.0 %copy-start.57 = (f32[1536]{0:T(1024)S(1)}, f32[1536]{0:T(1024)}, u32[]{:S(2)}) copy-start(f32[1536]{0:T(1024)} %copy-done.56) | copy-start | bytes 18436
  384.2 112.0 %copy-start.59 = (f32[1536]{0:T(1024)S(1)}, f32[1536]{0:T(1024)}, u32[]{:S(2)}) copy-start(f32[1536]{0:T(1024)} %copy-done.58) | copy-start | bytes 18436
  384.2 112.0 %copy-start.61 = (f32[1536]{0:T(1024)S(1)}, f32[1536]{0:T(1024)}, u32[]{:S(2)}) copy-start(f32[1536]{0:T(1024)} %copy-done.60) | copy-start | bytes 18436
  384.2 112.0 %copy-start.63 = (f32[1536]{0:T(1024)S(1)}, f32[1536]{0:T(1024)}, u32[]{:S(2)}) copy-start(f32[1536]{0:T(1024)} %copy-done.62) | copy-start | bytes 18436
  384.2 112.0 %copy-start.65 = (f32[1536]{0:T(1024)S(1)}, f32[1536]{0:T(1024)}, u32[]{:S(2)}) copy-start(f32[1536]{0:T(1024)} %copy-done.64) | copy-start | bytes 18436
  384.2 112.0 %copy-start.67 = (f32[1536]{0:T(1024)S(1)}, f32[1536]{0:T(1024)}, u32[]{:S(2)}) copy-start(f32[1536]{0:T(1024)} %copy-done.66) | copy-start | bytes 18436
  384.2 112.0 %copy-start.69 = (f32[1536]{0:T(1024)S(1)}, f32[1536]{0:T(1024)}, u32[]{:S(2)}) copy-start(f32[1536]{0:T(1024)} %copy-done.68) | copy-start | bytes 18436
  384.2 112.0 %copy-start.71 = (f32[1536]{0:T(1024)S(1)}, f32[1536]{0:T(1024)}, u32[]{:S(2)}) copy-start(f32[1536]{0:T(1024)} %copy-done.70) | copy-start | bytes 18436
  384.3 112.0 %copy-start.73 = (f32[1536]{0:T(1024)S(1)}, f32[1536]{0:T(1024)}, u32[]{:S(2)}) copy-start(f32[1536]{0:T(1024)} %copy-done.72) | copy-start | bytes 18436
  384.3 112.0 %copy-start.75 = (f32[1536]{0:T(1024)S(1)}, f32[1536]{0:T(1024)}, u32[]{:S(2)}) copy-start(f32[1536]{0:T(1024)} %copy-done.74) | copy-start | bytes 18436
  384.3 112.0 %copy-start.77 = (f32[1536]{0:T(1024)S(1)}, f32[1536]{0:T(1024)}, u32[]{:S(2)}) copy-start(f32[1536]{0:T(1024)} %copy-done.76) | copy-start | bytes 18436
  384.3 112.0 %copy-start.79 = (f32[1536]{0:T(1024)S(1)}, f32[1536]{0:T(1024)}, u32[]{:S(2)}) copy-start(f32[1536]{0:T(1024)} %copy-done.78) | copy-start | bytes 18436
  387.5 108.4 %collective-permute-start.2 = (f32[1,15,1536]{2,1,0:T(8,128)S(1)}, f32[1,15,1536]{2,1,0:T(8,128)S(1)}, u32[]{:S(2)}, u32[]{:S(2)}) collective-permute-start(f32[1,15,1536]{2,1,0:T(8,128)S(1)} %get-tuple-element.114), channel_id=1, source_target_pairs={{1,0},{2,1},{3,2},{4,3},{5,4},{6,5},{7,6},{8,7},{9,8},{10,9},{11,1... | collective-permute-start | bytes 276488 | tf_op jit(solution)/shard_map/ppermute | solution.py:19
  388.8 107.1 %collective-permute-start.3 = (f32[1,15,1536]{2,1,0:T(8,128)S(1)}, f32[1,15,1536]{2,1,0:T(8,128)S(1)}, u32[]{:S(2)}, u32[]{:S(2)}) collective-permute-start(f32[1,15,1536]{2,1,0:T(8,128)S(1)} %get-tuple-element.115), channel_id=1, source_target_pairs={{0,1},{1,2},{2,3},{3,4},{4,5},{5,6},{6,7},{7,8},{8,9},{9,10},{10,1... | collective-permute-start | bytes 276488 | tf_op jit(solution)/shard_map/ppermute | solution.py:17
  (58 other events, 289.1 us)
Sparse Core Ops, SparseCore 0:
  233.9 130.9 all-reduce.5
Sparse Core Ops, SparseCore 1:
  387.6 265.4 all-reduce.3
where the time goes:
time: 664 us; the launch traced here: 662 us
  waiting for transfers between devices  293 us (44%)
  blocking collectives  213 us (32%)
  other arithmetic  40.2 us (6%)
  local copies, waits for them, and re-layouts  39.6 us (6%)
  starting transfers between devices  37.8 us (6%)
  matrix products  20.7 us (3%)
  between operations  17.9 us (3%)
    psum x1, waiting for transfers between devices, local(): kernel_total, gain_total = lax.psum((kernel_part, gain_part), ('dp', 'ctx'))  151 us
    unnamed x3, waiting for transfers between devices  129 us
    psum x1, blocking collectives, local(): kernel_total, gain_total = lax.psum((kernel_part, gain_part), ('dp', 'ctx'))  103 us
    all_gather x1, blocking collectives, local(): lax.all_gather(segment_langs, 'ctx', axis=1, tiled=True)[0, :, :]  60.6 us
    all_to_all x1, blocking collectives, local(): lax.all_to_all(send_normed, 'ctx', split_axis=0, concat_axis=0, tiled=True)  49.6 us
    all_to_all x1, waiting for transfers between devices, local(): lax.all_to_all(branch, 'ctx', split_axis=0, concat_axis=0, tiled=True)  13.5 us
  transfers between devices with their start and end apart: 9, of which 3 were waited for; matrix products, arithmetic and copies ran while one was open for 9% of the time, Pallas kernels for 0%

commit v1 on v0

v1 whole, which is shorter than its diff:
```python
import functools
import math

import jax
import jax.numpy as jnp
from jax import lax
from jax.experimental import pallas as pl
from jax.experimental.pallas import tpu as pltpu
from jax.sharding import PartitionSpec as P

BLOCK = 16
SEGMENTS = 16
EDGE = 16
LANES = 128
VMEM = pl.BlockSpec(memory_space=pltpu.VMEM)
SMEM = pl.BlockSpec(memory_space=pltpu.SMEM)
PARAMS = pltpu.CompilerParams(vmem_limit_bytes=40 * 1024 * 1024)
F32 = jnp.float32
BF16 = jnp.bfloat16


def call(body, outs, ins, scratch=()):
    return pl.pallas_call(
        body,
        out_shape=tuple(jax.ShapeDtypeStruct(shape, kind) for shape, kind in outs),
        in_specs=[SMEM if space == "s" else VMEM for space, _ in ins],
        out_specs=tuple(VMEM for _ in outs),
        scratch_shapes=[pltpu.VMEM(shape, kind) for shape, kind in scratch],
        compiler_params=PARAMS,
    )(*[array for _, array in ins])


def segments(numbers):
    start = jnp.int32(0)
    found = []
    for seg in range(SEGMENTS):
        slot = numbers[2 * SEGMENTS + numbers[SEGMENTS + seg]]
        end = start + numbers[seg]
        found.append((start, end, slot // 2, slot % 2))
        start = end
    return found


def frame_slots(found, shape, dim):
    frame = lax.broadcasted_iota(jnp.int32, shape, dim)
    slot = jnp.zeros(shape, jnp.int32)
    for start, end, keeper, _ in found:
        slot = jnp.where((frame >= start) & (frame < end), keeper * BLOCK - start + frame, slot)
    return slot


def scatter_matrix(found, rows, frames):
    slot = frame_slots(found, (1, frames), 1)
    row = lax.broadcasted_iota(jnp.int32, (rows, frames), 0)
    return jnp.where(row == slot, 1.0, 0.0).astype(BF16)


def gather_matrix(found, rows, frames):
    slot = frame_slots(found, (frames, LANES), 0)
    lane = lax.broadcasted_iota(jnp.int32, (frames, LANES), 1)
    parts = [jnp.where(lane + at == slot, 1.0, 0.0) for at in range(0, rows, LANES)]
    return jnp.concatenate(parts, axis=1).astype(BF16)


def shifted(cells, by):
    return cells if by == 0 else pltpu.roll(cells, cells.shape[0] - by, 0)


def send_cotangent(numbers, cot, send):
    found = segments(numbers)
    rows = send.shape[0]
    spread = scatter_matrix(found, rows, cot.shape[0])
    row = lax.broadcasted_iota(jnp.int32, (rows, LANES), 0)
    mark = jnp.zeros((rows, LANES), F32)
    for _, _, keeper, which in found:
        mark = jnp.where(row == keeper * BLOCK + BLOCK - 1, which.astype(F32), mark)
    moved = jnp.dot(spread, cot[...], preferred_element_type=F32)
    send[...] = moved.astype(BF16)
    send[:, :LANES] = (moved[:, :LANES] + mark).astype(BF16)


def conv_and_norm(numbers, left, own, right, taps, gain, send, summed, inv, cells, normed):
    frames, width = own.shape
    cells[:EDGE] = left[...].astype(F32)
    cells[EDGE : EDGE + frames] = own[...].astype(F32)
    cells[EDGE + frames :] = right[...].astype(F32)
    half = frames // 2

    def column(at, squares):
        lanes = pl.ds(pl.multiple_of(at * LANES, LANES), LANES)
        sums = []
        for part in range(2):
            block = cells[part * half : part * half + half + 2 * EDGE, lanes]
            total = block[EDGE : EDGE + half]
            for low in range(8):
                moved = shifted(block, low)
                for high in range(0, 32, 8):
                    if high + low > 0:
                        tap = taps[high + low - 1 : high + low, lanes]
                        total = total + tap * moved[high : high + half]
            summed[part * half : part * half + half, lanes] = total
            sums.append(total * total)
        return squares + jnp.concatenate(sums, axis=0)

    squares = lax.fori_loop(0, width // LANES, column, jnp.zeros((frames, LANES), F32))
    scale = lax.rsqrt(jnp.sum(squares, axis=1, keepdims=True) * (1.0 / width) + 1e-06)
    inv[...] = jnp.broadcast_to(scale, inv.shape)
    normed[...] = (summed[...] * scale * gain[...]).astype(BF16)
    spread = scatter_matrix(segments(numbers), send.shape[0], frames)
    send[...] = jnp.dot(spread, normed[...], preferred_element_type=F32).astype(BF16)


def keeper_back(rows_in, cot_in, down, up, back, pre_grad, act):
    rows, width = rows_in.shape
    units = down.shape[2]
    marks = cot_in[:, :units].astype(F32).reshape(rows // BLOCK, BLOCK, units)
    marks = jnp.broadcast_to(marks[:, BLOCK - 1 :, :], marks.shape).reshape(rows, units)
    keep = jnp.concatenate([1.0 - marks, marks], axis=1)
    both_down = jnp.concatenate([down[0], down[1]], axis=1)
    both_up = up[...].reshape(2 * units, width)
    pre = jnp.dot(rows_in[...], both_down, preferred_element_type=F32)
    slope_of = lax.dot_general(cot_in[...], both_up, (((1,), (1,)), ((), ())), preferred_element_type=F32)
    sig = jax.nn.sigmoid(pre)
    act[...] = (keep * (pre * sig)).astype(BF16)
    grads = (keep * (slope_of * (sig * (1.0 + pre * (1.0 - sig))))).astype(BF16)
    pre_grad[...] = grads
    back[...] = lax.dot_general(grads, both_down, (((1,), (1,)), ((), ())), preferred_element_type=F32).astype(BF16)


def keeper_branch(act, up, branch):
    both_up = up[...].reshape(act.shape[1], branch.shape[1])
    branch[...] = jnp.dot(act[...], both_up, preferred_element_type=F32).astype(BF16)


def keeper_grads(rows_in, cot_in, pre_grad, act, grads):
    parts, twice, units = grads.shape
    part = twice // 2
    down = lax.dot_general(rows_in[...], pre_grad[...], (((0,), (0,)), ((), ())), preferred_element_type=F32)
    up = lax.dot_general(cot_in[...], act[...], (((0,), (0,)), ((), ())), preferred_element_type=F32)
    for place, at in enumerate(turned(parts)):
        grads[place, :part] = down[at * part : at * part + part]
        grads[place, part:] = up[at * part : at * part + part]


def sum_gradients(
    numbers, back, cot, summed, inv, gain, left, own, right, total, edges, sums, cells, frames_grad
):
    frames, width = cot.shape
    gather = gather_matrix(segments(numbers), back.shape[0], frames)
    cells[:EDGE] = left[...].astype(F32)
    cells[EDGE : EDGE + frames] = own[...].astype(F32)
    cells[EDGE + frames :] = right[...].astype(F32)
    frames_grad[...] = jnp.dot(gather, back[...], preferred_element_type=F32)
    scale = inv[:, :1]
    inner = jnp.sum(gain[...] * frames_grad[...] * summed[...], axis=1, keepdims=True) * (1.0 / width)
    pull = scale * scale * scale * inner
    half = frames // 2

    def column(at, carry):
        lanes = pl.ds(pl.multiple_of(at * LANES, LANES), LANES)
        for part in range(2):
            span = slice(part * half, part * half + half)
            grad = frames_grad[span, lanes]
            base = summed[span, lanes]
            inverse = inv[span, :]
            gain_sum = jnp.sum(grad * base * inverse, axis=0, keepdims=True)
            whole = cot[span, lanes].astype(F32) + inverse * (gain[:, lanes] * grad) - base * pull[span]
            total[span, lanes] = whole
            block = cells[part * half : part * half + half + 2 * EDGE, lanes]
            found = [None] * 31
            for low in range(8):
                moved = shifted(block, low)
                for high in range(0, 32, 8):
                    if high + low > 0:
                        product = whole * moved[high : high + half]
                        found[high + low - 1] = jnp.sum(product, axis=0, keepdims=True)
            rows = jnp.concatenate(found + [gain_sum], axis=0)
            if part == 0:
                first = rows
            else:
                sums[:, lanes] = first + rows
        return carry

    lax.fori_loop(0, width // LANES, column, 0)
    edges[0] = total[:EDGE]
    edges[1] = total[frames - EDGE :]


def input_gradient(left, own, right, taps, out, cells):
    frames, width = own.shape
    cells[:EDGE] = left[...]
    cells[EDGE : EDGE + frames] = own[...]
    cells[EDGE + frames :] = right[...]
    half = frames // 2

    def column(at, carry):
        lanes = pl.ds(pl.multiple_of(at * LANES, LANES), LANES)
        for part in range(2):
            block = cells[part * half : part * half + half + 2 * EDGE, lanes]
            total = block[EDGE : EDGE + half]
            for low in range(8):
                moved = shifted(block, low)
                for high in range(0, 32, 8):
                    if high + low > 0:
                        tap = taps[31 - high - low : 32 - high - low, lanes]
                        total = total + tap * moved[high : high + half]
            out[part * half : part * half + half, lanes] = total.astype(BF16)
        return carry

    lax.fori_loop(0, width // LANES, column, 0)


def add_branch(numbers, back, summed, out):
    gather = gather_matrix(segments(numbers), back.shape[0], summed.shape[0])
    out[...] = (summed[...] + jnp.dot(gather, back[...], preferred_element_type=F32)).astype(BF16)


def place_grads(scale, kept, got, down, up):
    share, units = down.shape[1:]
    total = (kept[...] + got[...].astype(F32)) * scale
    for which in range(2):
        lanes = slice(which * units, which * units + units)
        down[which] = total[:share, lanes]
        up[which] = total[share:, lanes].T


def from_sides(head, tail, axis):
    count = lax.axis_size(axis)
    left = lax.ppermute(tail, axis, [(i, i + 1) for i in range(count - 1)])
    right = lax.ppermute(head, axis, [(i + 1, i) for i in range(count - 1)])
    return left, right


def turned(count):
    bits = count.bit_length() - 1
    return [sum(((at >> bit) & 1) << (bits - 1 - bit) for bit in range(bits)) for at in range(count)]


def halved(cells, axis, kind):
    count, me = lax.axis_size(axis), lax.axis_index(axis)
    step = 1
    while True:
        half = cells.shape[0] // 2
        upper = (me // step) % 2 == 1
        given = jnp.where(upper, cells[:half], cells[half:]).astype(kind)
        kept = jnp.where(upper, cells[half:], cells[:half])
        got = lax.ppermute(given, axis, [(i, i ^ step) for i in range(count)])
        step *= 2
        if step == count:
            return kept, got
        cells = kept + got.astype(cells.dtype)


def quartered(cells, axis):
    count, me = lax.axis_size(axis), lax.axis_index(axis)
    unit = count // 4
    while unit > 0:
        part = cells.shape[0] // 4
        blocks = [cells[at * part : at * part + part] for at in range(4)]
        mine = (me // unit) % 4

        def block(turn):
            place = mine ^ turn
            low = jnp.where(place == 0, blocks[0], blocks[1])
            return jnp.where(place < 2, low, jnp.where(place == 2, blocks[2], blocks[3]))

        moved = [lax.ppermute(block(turn), axis, [(i, i ^ (turn * unit)) for i in range(count)]) for turn in (1, 2, 3)]
        cells = (block(0) + moved[0]) + (moved[1] + moved[2])
        unit //= 4
    return cells


def swap(cells, axis):
    return lax.all_to_all(cells, axis, split_axis=0, concat_axis=0, tiled=True)


def spread_rows(rows, axis):
    count = lax.axis_size(axis)
    return swap(jnp.broadcast_to(rows[None], (count,) + rows.shape), axis)


def local(
    inputs, cotangent, conv_kernel, norm_gain, adapt_down, adapt_up, segment_lengths, segment_langs, lang_slot
):
    frames, width = inputs.shape[1:]
    units = adapt_down.shape[2]
    dp, ctx = lax.axis_size("dp"), lax.axis_size("ctx")
    rows = ctx * BLOCK
    own, cot = inputs[0], cotangent[0]
    gain = norm_gain.reshape(1, width)
    numbers = jnp.concatenate([segment_lengths.reshape(-1), segment_langs.reshape(-1), lang_slot])
    where = [("s", numbers)]

    left, right = from_sides(own[:EDGE], own[frames - EDGE :], "ctx")
    (send_cot,) = call(send_cotangent, [((rows, width), BF16)], where + [("v", cot)])
    left, right, send_cot = lax.optimization_barrier((left, right, send_cot))
    got_cot = swap(send_cot, "ctx")
    send_rows, summed, inv = call(
        conv_and_norm,
        [((rows, width), BF16), ((frames, width), F32), ((frames, LANES), F32)],
        where + [("v", left), ("v", own), ("v", right), ("v", conv_kernel), ("v", gain)],
        [((frames + 2 * EDGE, width), F32), ((frames, width), BF16)],
    )
    got_rows = swap(send_rows, "ctx")
    back, pre_grad, act = call(
        keeper_back,
        [((rows, width), BF16), ((rows, 2 * units), BF16), ((rows, 2 * units), BF16)],
        [("v", got_rows), ("v", got_cot), ("v", adapt_down), ("v", adapt_up)],
    )
    grad_back = swap(back, "ctx")
    (branch,) = call(keeper_branch, [((rows, width), BF16)], [("v", act), ("v", adapt_up)])
    (parts,) = call(
        keeper_grads,
        [((dp, 2 * (width // dp), 2 * units), F32)],
        [("v", got_rows), ("v", got_cot), ("v", pre_grad), ("v", act)],
    )
    kept, got = halved(parts, "dp", BF16)
    grad_back, branch = lax.optimization_barrier((grad_back, branch))
    branch_back = swap(branch, "ctx")
    total, edges, sums = call(
        sum_gradients,
        [((frames, width), F32), ((2, EDGE, width), F32), ((32, width), F32)],
        where
        + [("v", grad_back), ("v", cot), ("v", summed), ("v", inv), ("v", gain)]
        + [("v", left), ("v", own), ("v", right)],
        [((frames + 2 * EDGE, width), F32), ((frames, width), F32)],
    )
    grad_left, grad_right = from_sides(edges[0], edges[1], "ctx")
    mine, branch_back = lax.optimization_barrier((quartered(sums, "dp"), branch_back))
    mine = jnp.sum(spread_rows(mine, "ctx"), axis=0)
    grad_scale = 1.0 / math.sqrt(dp * ctx * frames)
    (grad_input,) = call(
        input_gradient,
        [((frames, width), BF16)],
        [("v", grad_left), ("v", total), ("v", grad_right), ("v", conv_kernel)],
        [((frames + 2 * EDGE, width), F32)],
    )
    (output,) = call(add_branch, [((frames, width), BF16)], where + [("v", branch_back), ("v", summed)])
    mine, grad_input, output = lax.optimization_barrier((mine, grad_input, output))
    reduced = spread_rows(mine * grad_scale, "dp").reshape(32, width)
    share = width // dp
    grad_down, grad_up = call(
        functools.partial(place_grads, grad_scale),
        [((2, share, units), F32), ((2, units, share), F32)],
        [("v", kept[0]), ("v", got[0])],
    )
    return output[None], grad_input[None], reduced[:31], reduced[31], grad_down, grad_up


def solution(mesh):
    in_specs = (
        P("dp", "ctx", None),
        P("dp", "ctx", None),
        P(),
        P(),
        P("ctx", None, None),
        P("ctx", None, None),
        P("dp", "ctx", None),
        P("dp", "ctx", None),
        P(),
    )
    out_specs = (
        P("dp", "ctx", None),
        P("dp", "ctx", None),
        P(),
        P(),
        P("ctx", "dp", None),
        P("ctx", None, "dp"),
    )
    return jax.shard_map(local, mesh=mesh, in_specs=in_specs, out_specs=out_specs, check_vma=False)
```

time: 664 us -> 266 us (0.40)
  waiting for transfers between devices: 293 us -> 39.8 us
  blocking collectives: 213 us -> 94.8 us
  starting transfers between devices: 37.8 us -> 80.3 us
  other arithmetic: 40.2 us -> 9.25 us
  local copies, waits for them, and re-layouts: 39.6 us -> 14.5 us
  Pallas kernels: 0 us -> 25 us
  matrix products: 20.7 us -> 0 us
  between operations: 17.9 us -> 1.3 us
    psum x1 -> x0, waiting for transfers between devices: 151 us -> none  [local(): kernel_total, gain_total = lax.psum((kernel_part, gain_part), ('dp', 'ctx'))]
    unnamed x3 -> x0, waiting for transfers between devices: 129 us -> none
    psum x1 -> x0, blocking collectives: 103 us -> none  [local(): kernel_total, gain_total = lax.psum((kernel_part, gain_part), ('dp', 'ctx'))]
    all_gather x1 -> x0, blocking collectives: 60.6 us -> none  [local(): lax.all_gather(segment_langs, 'ctx', axis=1, tiled=True)[0, :, :]]
    all_to_all x1 -> x2, blocking collectives: 49.6 us -> 94.8 us  [swap(): return lax.all_to_all(cells, axis, split_axis=0, concat_axis=0, tiled=True)]
    ppermute x4 -> x14, starting transfers between devices: 11.4 us -> 48.8 us  [the longest x6 22.8 us: quartered(): lax.ppermute(block(turn), axis, [(i, i ^ turn * unit) for i in range(coun...]
    pallas_call x0 -> x9, Pallas kernels: none -> 25 us  [call(): pl.pallas_call(body, out_shape=tuple((jax.ShapeDtypeStruct(shape, kind) f...]
    dot_general x12 -> x0, matrix products: 20.7 us -> none  [the longest x2 6.23 us: local(): jnp.einsum('scr,scd->dr', activated * masks_bf[adapter_id], grad_rows, pr...]
  transfers between devices with their start and end apart: 9 -> 18, of which waited for: 3 -> 6; matrix products, arithmetic and copies ran while one was open for 9% -> 4% of each run, Pallas kernels for 0% -> 7%
where the time goes in v1:
time: 266 us; the launch traced here: 265 us
  blocking collectives  94.8 us (36%)
  starting transfers between devices  80.3 us (30%)
  waiting for transfers between devices  39.8 us (15%)
  Pallas kernels  25 us (9%)
  local copies, waits for them, and re-layouts  14.5 us (5%)
  other arithmetic  9.25 us (3%)
    all_to_all x2, blocking collectives, swap(): return lax.all_to_all(cells, axis, split_axis=0, concat_axis=0, tiled=True)  94.8 us
    all_to_all x4, starting transfers between devices, swap(): return lax.all_to_all(cells, axis, split_axis=0, concat_axis=0, tiled=True)  31.5 us
    pallas_call x9, Pallas kernels, call(): pl.pallas_call(body, out_shape=tuple((jax.ShapeDtypeStruct(shape, kind) f...  25 us
    ppermute x6, starting transfers between devices, quartered(): lax.ppermute(block(turn), axis, [(i, i ^ turn * unit) for i in range(coun...  22.8 us
    all_to_all x4, waiting for transfers between devices, swap(): return lax.all_to_all(cells, axis, split_axis=0, concat_axis=0, tiled=True)  21.9 us
    ppermute x4, starting transfers between devices, halved(): got = lax.ppermute(given, axis, [(i, i ^ step) for i in range(count)])  15.6 us
    ppermute x4, waiting for transfers between devices, halved(): got = lax.ppermute(given, axis, [(i, i ^ step) for i in range(count)])  13.5 us
    unnamed x53, local copies, waits for them, and re-layouts  10.6 us
  transfers between devices with their start and end apart: 18, of which 6 were waited for; matrix products, arithmetic and copies ran while one was open for 4% of the time, Pallas kernels for 7%

profile of v1, /device:TPU:1, one launch (start us, length us, event | category | flops | bytes accessed | tf_op | source)
XLA Modules:
  0.0 265.0 jit_solution(11077582151084645696)
XLA Ops:
  0.6 0.9 slice_bitcast_fusion.2
  1.5 4.8 %collective-permute-start = (bf16[16,1536]{1,0:T(8,128)(2,1)S(1)}, bf16[16,1536]{1,0:T(8,128)(2,1)S(1)}, u32[]{:S(2)}, u32[]{:S(2)}) collective-permute-start(bf16[16,1536]{1,0:T(8,128)(2,1)S(1)} %get-tuple-element.67), channel_id=1, source_target_pairs={{0,1},{1,2},{2,3},{3,4},{4,5},{5,6},{6,7},{7,8},{8,9},{9,10},{10,1... | collective-permute-start | bytes 147464 | tf_op jit(solution)/shard_map/ppermute | solution.py:229
  6.4 1.3 collective-permute-start.1
  7.7 0.8 pad_add_fusion.numbers
  9.1 1.1 copy-done.11
  10.2 1.5 shard_map.136
  11.8 4.9 %shard_map.137 = (bf16[512,1536]{1,0:T(8,128)(2,1)S(1)}, f32[192,1536]{1,0:T(8,128)S(1)}, f32[192,128]{1,0:T(8,128)S(1)}) custom-call(s32[96]{0:T(128)S(1)} %pad_add_fusion.numbers, bf16[16,1536]{1,0:T(8,128)(2,1)S(1)} %collective-permute-done.left, bf16[192,1536]{1,0:T(8,128)(2,1)S(1)} %bitcast.33, bf16[16,1536]{1,0:T(8,128)(2,1)S(1)} %collective-permute-done.1.right, ...), custom_call_target="tpu_custom_call" | custom-call | tf_op jit(solution)/shard_map/pallas_call | solution.py:23
  16.8 49.5 %all_to_all.56 = bf16[32,16,1536]{2,1,0:T(8,128)(2,1)S(1)} all-to-all(bf16[32,16,1536]{2,1,0:T(8,128)(2,1)S(1)} %bitcast.37), channel_id=1, replica_groups=mesh['dp'=16,'ctx'=32] {'ctx'}, dimensions={0} | all-to-all | bytes 3145728 | tf_op jit(solution)/shard_map/all_to_all | solution.py:274
  66.3 45.2 %all_to_all.57 = bf16[32,16,1536]{2,1,0:T(8,128)(2,1)S(1)} all-to-all(bf16[32,16,1536]{2,1,0:T(8,128)(2,1)S(1)} %bitcast.32), channel_id=1, replica_groups=mesh['dp'=16,'ctx'=32] {'ctx'}, dimensions={0} | all-to-all | bytes 3145728 | tf_op jit(solution)/shard_map/all_to_all | solution.py:274
  111.6 2.6 shard_map.138
  115.0 8.5 %all-to-all-start.2 = ((bf16[32,16,1536]{2,1,0:T(8,128)(2,1)}), bf16[32,16,1536]{2,1,0:T(8,128)(2,1)}, u32[]{:S(2)}, u32[]{:S(2)}) async-start(bf16[32,16,1536]{2,1,0:T(8,128)(2,1)} %bitcast.10), calls=%async_computation.2 | async-start | bytes 3145728 | tf_op jit(solution)/shard_map/all_to_all | solution.py:274
  123.5 1.4 copy-done.1
  124.9 1.4 copy-done.3
  126.3 0.9 copy-done.19
  127.2 1.0 shard_map.143
  128.3 1.1 select_convert_fusion
  129.3 3.2 %collective-permute-start.10 = (bf16[8,192,256]{2,1,0:T(8,128)(2,1)}, bf16[8,192,256]{2,1,0:T(8,128)(2,1)}, u32[]{:S(2)}, u32[]{:S(2)}) collective-permute-start(bf16[8,192,256]{2,1,0:T(8,128)(2,1)} %select_convert_fusion), channel_id=1, source_target_pairs={{0,32},{32,0},{64,96},{96,64},{128,160},{160,128},{192,224},{224,1... | collective-permute-start | bytes 2359304 | tf_op jit(solution)/shard_map/ppermute | solution.py:247
  132.7 1.1 copy-done.8
  134.4 1.2 copy-done.4
  135.5 2.6 convert_add_fusion
  138.2 21.9 %all-to-all-done.2 = bf16[32,16,1536]{2,1,0:T(8,128)(2,1)} async-done(((bf16[32,16,1536]{2,1,0:T(8,128)(2,1)}), bf16[32,16,1536]{2,1,0:T(8,128)(2,1)}, u32[]{:S(2)}, u32[]{:S(2)}) %all-to-all-start.2) | async-done | bytes 1572896 | tf_op jit(solution)/shard_map/all_to_all | solution.py:274
  160.1 8.0 %all-to-all-start.3 = ((bf16[32,16,1536]{2,1,0:T(8,128)(2,1)}), bf16[32,16,1536]{2,1,0:T(8,128)(2,1)S(1)}, u32[]{:S(2)}, u32[]{:S(2)}) async-start(bf16[32,16,1536]{2,1,0:T(8,128)(2,1)} %bitcast.31), calls=%async_computation.3 | async-start | bytes 3145728 | tf_op jit(solution)/shard_map/all_to_all | solution.py:274
  168.1 1.1 copy-done.12
  169.1 0.9 copy-done.23
  170.0 7.1 %shard_map.140 = (f32[192,1536]{1,0:T(8,128)S(1)}, f32[2,16,1536]{2,1,0:T(8,128)S(1)}, f32[32,1536]{1,0:T(8,128)S(1)}) custom-call(s32[96]{0:T(128)S(1)} %pad_add_fusion.numbers, bf16[512,1536]{1,0:T(8,128)(2,1)} %bitcast.11.back, bf16[192,1536]{1,0:T(8,128)(2,1)S(1)} %bitcast.36, f32[192,1536]{1,0:T(8,128)S(1)} %copy-done.6, f32[192,128]{1,0:T(8,128)S(1)} %copy-done.23, ...), custom_call_target="tpu_custom_call" | custom-call | tf_op jit(solution)/shard_map/pallas_call | solution.py:23
  177.1 5.9 %collective-permute-start.4 = (f32[8,1536]{1,0:T(8,128)S(1)}, f32[8,1536]{1,0:T(8,128)S(1)}, u32[]{:S(2)}, u32[]{:S(2)}) collective-permute-start(f32[8,1536]{1,0:T(8,128)S(1)} %select_select_fusion), channel_id=1, source_target_pairs={{0,384},{32,416},{64,448},{96,480},{128,256},{160,288},{192,320},{... | collective-permute-start | bytes 147464 | tf_op jit(solution)/shard_map/ppermute | solution.py:267
  183.1 3.8 %collective-permute-start.2 = (f32[8,1536]{1,0:T(8,128)S(1)}, f32[8,1536]{1,0:T(8,128)S(1)}, u32[]{:S(2)}, u32[]{:S(2)}) collective-permute-start(f32[8,1536]{1,0:T(8,128)S(1)} %get-tuple-element.70), channel_id=1, source_target_pairs={{0,128},{32,160},{64,192},{96,224},{128,0},{160,32},{192,64},{224,... | collective-permute-start | bytes 147464 | tf_op jit(solution)/shard_map/ppermute | solution.py:267
  186.8 2.2 collective-permute-start.3
  189.1 2.8 %collective-permute-start.11 = (bf16[4,192,256]{2,1,0:T(8,128)(2,1)S(1)}, bf16[4,192,256]{2,1,0:T(8,128)(2,1)S(1)}, u32[]{:S(2)}, u32[]{:S(2)}) collective-permute-start(bf16[4,192,256]{2,1,0:T(8,128)(2,1)S(1)} %select_convert_fusion.1), channel_id=1, source_target_pairs={{0,64},{32,96},{64,0},{96,32},{128,192},{160,224},{192,128},{224,1... | collective-permute-start | bytes 1179656 | tf_op jit(solution)/shard_map/ppermute | solution.py:247
  191.9 4.0 %collective-permute-done.3 = f32[8,1536]{1,0:T(8,128)S(1)} collective-permute-done((f32[8,1536]{1,0:T(8,128)S(1)}, f32[8,1536]{1,0:T(8,128)S(1)}, u32[]{:S(2)}, u32[]{:S(2)}) %collective-permute-start.3) | collective-permute-done | bytes 49184 | tf_op jit(solution)/shard_map/ppermute | solution.py:267
  195.9 5.7 %collective-permute-start.7 = (f32[2,1536]{1,0:T(2,128)S(1)}, f32[2,1536]{1,0:T(2,128)S(1)}, u32[]{:S(2)}, u32[]{:S(2)}) collective-permute-start(f32[2,1536]{1,0:T(2,128)S(1)} %select_select_fusion.3), channel_id=1, source_target_pairs={{0,96},{32,64},{64,32},{96,0},{128,224},{160,192},{192,160},{224,1... | collective-permute-start | bytes 36872 | tf_op jit(solution)/shard_map/ppermute | solution.py:267
  201.7 2.0 collective-permute-start.5
  203.7 3.3 %collective-permute-start.6 = (f32[2,1536]{1,0:T(2,128)S(1)}, f32[2,1536]{1,0:T(2,128)S(1)}, u32[]{:S(2)}, u32[]{:S(2)}) collective-permute-start(f32[2,1536]{1,0:T(2,128)S(1)} %get-tuple-element.73), channel_id=1, source_target_pairs={{0,64},{32,96},{64,0},{96,32},{128,192},{160,224},{192,128},{224,1... | collective-permute-start | bytes 36872 | tf_op jit(solution)/shard_map/ppermute | solution.py:267
  207.0 1.0 convert_add_fusion.1
  208.2 0.8 broadcast_in_dim.8
  209.0 9.8 %all-to-all-start.4 = ((f32[32,2,1536]{2,1,0:T(2,128)}), f32[32,2,1536]{2,1,0:T(2,128)}, u32[]{:S(2)}, u32[]{:S(2)}) async-start(f32[32,2,1536]{2,1,0:T(2,128)} %broadcast_in_dim.8), calls=%async_computation.4 | async-start | bytes 786432 | tf_op jit(solution)/shard_map/all_to_all | solution.py:274
  218.8 1.2 select_convert_fusion.2
  220.0 2.5 collective-permute-start.12
  222.5 3.1 %collective-permute-start.8 = (f32[16,1536]{1,0:T(8,128)S(1)}, f32[16,1536]{1,0:T(8,128)S(1)}, u32[]{:S(2)}, u32[]{:S(2)}) collective-permute-start(f32[16,1536]{1,0:T(8,128)S(1)} %get-tuple-element.69), channel_id=1, source_target_pairs={{0,1},{1,2},{2,3},{3,4},{4,5},{5,6},{6,7},{7,8},{8,9},{9,10},{10,1... | collective-permute-start | bytes 294920 | tf_op jit(solution)/shard_map/ppermute | solution.py:229
  225.6 1.3 collective-permute-start.9
  226.9 5.9 %collective-permute-done.12 = bf16[2,192,256]{2,1,0:T(8,128)(2,1)S(1)} collective-permute-done((bf16[2,192,256]{2,1,0:T(8,128)(2,1)S(1)}, bf16[2,192,256]{2,1,0:T(8,128)(2,1)S(1)}, u32[]{:S(2)}, u32[]{:S(2)}) %collective-permute-start.12) | collective-permute-done | bytes 196640 | tf_op jit(solution)/shard_map/ppermute | solution.py:247
  232.8 1.2 convert_add_fusion.2
  234.1 4.4 %shard_map.141 = bf16[192,1536]{1,0:T(8,128)(2,1)} custom-call(f32[16,1536]{1,0:T(8,128)S(1)} %collective-permute-done.8.left, f32[192,1536]{1,0:T(8,128)S(1)} %copy-done.14, f32[16,1536]{1,0:T(8,128)S(1)} %collective-permute-done.9.right, f32[31,1536]{1,0:T(8,128)S(1)} %copy-done.17), custom_call_target="tpu_custom_call" | custom-call | tf_op jit(solution)/shard_map/pallas_call | solution.py:23
  238.5 2.3 shard_map.142
  240.7 1.1 reduce_sum.9
  242.6 5.3 %all-to-all-start.5 = ((f32[16,2,1536]{2,1,0:T(2,128)}), f32[16,2,1536]{2,1,0:T(2,128)S(1)}, u32[]{:S(2)}, u32[]{:S(2)}) async-start(f32[16,2,1536]{2,1,0:T(2,128)} %broadcast_in_dim.21), calls=%async_computation.5 | async-start | bytes 393216 | tf_op jit(solution)/shard_map/all_to_all | solution.py:274
  247.9 7.2 %collective-permute-start.13 = (bf16[1,192,256]{2,1,0:T(8,128)(2,1)S(1)}, bf16[1,192,256]{2,1,0:T(8,128)(2,1)S(1)}, u32[]{:S(2)}, u32[]{:S(2)}) collective-permute-start(bf16[1,192,256]{2,1,0:T(8,128)(2,1)S(1)} %select_convert_fusion.3), channel_id=1, source_target_pairs={{0,256},{32,288},{64,320},{96,352},{128,384},{160,416},{192,448},{... | collective-permute-start | bytes 294920 | tf_op jit(solution)/shard_map/ppermute | solution.py:247
  255.1 7.6 %collective-permute-done.13 = bf16[1,192,256]{2,1,0:T(8,128)(2,1)S(1)} collective-permute-done((bf16[1,192,256]{2,1,0:T(8,128)(2,1)S(1)}, bf16[1,192,256]{2,1,0:T(8,128)(2,1)S(1)}, u32[]{:S(2)}, u32[]{:S(2)}) %collective-permute-start.13) | collective-permute-done | bytes 98336 | tf_op jit(solution)/shard_map/ppermute | solution.py:247
  (76 shorter events, 5.6 us)
Async XLA Ops:
  0.6 11.2 %copy-start.9 = (bf16[1,192,1536]{2,1,0:T(8,128)(2,1)S(1)}, bf16[1,192,1536]{2,1,0:T(8,128)(2,1)}, u32[]{:S(2)}) copy-start(bf16[1,192,1536]{2,1,0:T(8,128)(2,1)} %param.9) | copy-start | bytes 1769476
  1.5 10.1 %collective-permute-start = (bf16[16,1536]{1,0:T(8,128)(2,1)S(1)}, bf16[16,1536]{1,0:T(8,128)(2,1)S(1)}, u32[]{:S(2)}, u32[]{:S(2)}) collective-permute-start(bf16[16,1536]{1,0:T(8,128)(2,1)S(1)} %get-tuple-element.67), channel_id=1, source_target_pairs={{0,1},{1,2},{2,3},{3,4},{4,5},{5,6},{6,7},{7,8},{8,9},{9,10},{10,1... | collective-permute-start | bytes 147464 | tf_op jit(solution)/shard_map/ppermute | solution.py:229
  6.4 5.5 %collective-permute-start.1 = (bf16[16,1536]{1,0:T(8,128)(2,1)S(1)}, bf16[16,1536]{1,0:T(8,128)(2,1)S(1)}, u32[]{:S(2)}, u32[]{:S(2)}) collective-permute-start(bf16[16,1536]{1,0:T(8,128)(2,1)S(1)} %get-tuple-element.66), channel_id=1, source_target_pairs={{1,0},{2,1},{3,2},{4,3},{5,4},{6,5},{7,6},{8,7},{9,8},{10,9},{11,1... | collective-permute-start | bytes 147464 | tf_op jit(solution)/shard_map/ppermute | solution.py:230
  9.1 1.1 copy-start.11
  10.2 1.6 copy-start.16
  16.8 49.6 %copy-start.5 = (f32[192,1536]{1,0:T(8,128)}, f32[192,1536]{1,0:T(8,128)S(1)}, u32[]{:S(2)}) copy-start(f32[192,1536]{1,0:T(8,128)S(1)} %get-tuple-element.34.summed) | copy-start | bytes 3538948
  16.8 49.5 %copy-start.22 = (f32[192,128]{1,0:T(8,128)}, f32[192,128]{1,0:T(8,128)S(1)}, u32[]{:S(2)}) copy-start(f32[192,128]{1,0:T(8,128)S(1)} %get-tuple-element.35.inv) | copy-start | bytes 294916
  66.3 45.3 %copy-start = (bf16[32,16,1536]{2,1,0:T(8,128)(2,1)}, bf16[32,16,1536]{2,1,0:T(8,128)(2,1)S(1)}, u32[]{:S(2)}) copy-start(bf16[32,16,1536]{2,1,0:T(8,128)(2,1)S(1)} %all_to_all.56) | copy-start | bytes 4718596
  66.3 45.3 %copy-start.7 = (bf16[2,128,1536]{2,1,0:T(8,128)(2,1)S(1)}, bf16[2,128,1536]{2,1,0:T(8,128)(2,1)}, u32[]{:S(2)}) copy-start(bf16[2,128,1536]{2,1,0:T(8,128)(2,1)} %up.3) | copy-start | bytes 2359300
  66.3 45.3 %copy-start.15 = (bf16[2,1536,128]{2,1,0:T(8,128)(2,1)S(1)}, bf16[2,1536,128]{2,1,0:T(8,128)(2,1)}, u32[]{:S(2)}) copy-start(bf16[2,1536,128]{2,1,0:T(8,128)(2,1)} %down.1) | copy-start | bytes 2359300
  111.6 2.7 %copy-start.2 = (bf16[32,16,1536]{2,1,0:T(8,128)(2,1)}, bf16[32,16,1536]{2,1,0:T(8,128)(2,1)S(1)}, u32[]{:S(2)}) copy-start(bf16[32,16,1536]{2,1,0:T(8,128)(2,1)S(1)} %all_to_all.57) | copy-start | bytes 4718596
  114.2 0.7 copy-start.18
  115.0 45.1 %all-to-all-start.2 = ((bf16[32,16,1536]{2,1,0:T(8,128)(2,1)}), bf16[32,16,1536]{2,1,0:T(8,128)(2,1)}, u32[]{:S(2)}, u32[]{:S(2)}) async-start(bf16[32,16,1536]{2,1,0:T(8,128)(2,1)} %bitcast.10), calls=%async_computation.2 | async-start | bytes 3145728 | tf_op jit(solution)/shard_map/all_to_all | solution.py:274
  123.5 1.4 copy-start.1
  124.9 1.4 copy-start.3
  126.3 0.9 copy-start.19
  129.3 6.2 %collective-permute-start.10 = (bf16[8,192,256]{2,1,0:T(8,128)(2,1)}, bf16[8,192,256]{2,1,0:T(8,128)(2,1)}, u32[]{:S(2)}, u32[]{:S(2)}) collective-permute-start(bf16[8,192,256]{2,1,0:T(8,128)(2,1)} %select_convert_fusion), channel_id=1, source_target_pairs={{0,32},{32,0},{64,96},{96,64},{128,160},{160,128},{192,224},{224,1... | collective-permute-start | bytes 2359304 | tf_op jit(solution)/shard_map/ppermute | solution.py:247
  132.7 1.1 copy-start.8
  134.4 1.2 copy-start.4
  160.1 8.0 %copy-start.6 = (f32[192,1536]{1,0:T(8,128)S(1)}, f32[192,1536]{1,0:T(8,128)}, u32[]{:S(2)}) copy-start(f32[192,1536]{1,0:T(8,128)} %copy-done.5) | copy-start | bytes 3538948
  160.1 8.0 %copy-start.10 = (bf16[1,192,1536]{2,1,0:T(8,128)(2,1)S(1)}, bf16[1,192,1536]{2,1,0:T(8,128)(2,1)}, u32[]{:S(2)}) copy-start(bf16[1,192,1536]{2,1,0:T(8,128)(2,1)} %param.9) | copy-start | bytes 1769476
  160.1 48.1 %all-to-all-start.3 = ((bf16[32,16,1536]{2,1,0:T(8,128)(2,1)}), bf16[32,16,1536]{2,1,0:T(8,128)(2,1)S(1)}, u32[]{:S(2)}, u32[]{:S(2)}) async-start(bf16[32,16,1536]{2,1,0:T(8,128)(2,1)} %bitcast.31), calls=%async_computation.3 | async-start | bytes 3145728 | tf_op jit(solution)/shard_map/all_to_all | solution.py:274
  168.1 1.1 copy-start.12
  169.1 0.9 copy-start.23
  170.0 19.0 %copy-start.24 = (f32[8,192,256]{2,1,0:T(8,128)S(1)}, f32[8,192,256]{2,1,0:T(8,128)}, u32[]{:S(2)}) copy-start(f32[8,192,256]{2,1,0:T(8,128)} %convert_add_fusion) | copy-start | bytes 4718596
  177.1 30.9 %copy-start.13 = (f32[192,1536]{1,0:T(8,128)}, f32[192,1536]{1,0:T(8,128)S(1)}, u32[]{:S(2)}) copy-start(f32[192,1536]{1,0:T(8,128)S(1)} %get-tuple-element.40.own) | copy-start | bytes 3538948
  177.1 30.9 %copy-start.20 = (f32[2,16,1536]{2,1,0:T(8,128)}, f32[2,16,1536]{2,1,0:T(8,128)S(1)}, u32[]{:S(2)}) copy-start(f32[2,16,1536]{2,1,0:T(8,128)S(1)} %get-tuple-element.39) | copy-start | bytes 589828
  177.1 14.7 %collective-permute-start.4 = (f32[8,1536]{1,0:T(8,128)S(1)}, f32[8,1536]{1,0:T(8,128)S(1)}, u32[]{:S(2)}, u32[]{:S(2)}) collective-permute-start(f32[8,1536]{1,0:T(8,128)S(1)} %select_select_fusion), channel_id=1, source_target_pairs={{0,384},{32,416},{64,448},{96,480},{128,256},{160,288},{192,320},{... | collective-permute-start | bytes 147464 | tf_op jit(solution)/shard_map/ppermute | solution.py:267
  183.1 8.8 %collective-permute-start.2 = (f32[8,1536]{1,0:T(8,128)S(1)}, f32[8,1536]{1,0:T(8,128)S(1)}, u32[]{:S(2)}, u32[]{:S(2)}) collective-permute-start(f32[8,1536]{1,0:T(8,128)S(1)} %get-tuple-element.70), channel_id=1, source_target_pairs={{0,128},{32,160},{64,192},{96,224},{128,0},{160,32},{192,64},{224,... | collective-permute-start | bytes 147464 | tf_op jit(solution)/shard_map/ppermute | solution.py:267
  186.8 9.1 %collective-permute-start.3 = (f32[8,1536]{1,0:T(8,128)S(1)}, f32[8,1536]{1,0:T(8,128)S(1)}, u32[]{:S(2)}, u32[]{:S(2)}) collective-permute-start(f32[8,1536]{1,0:T(8,128)S(1)} %get-tuple-element.71), channel_id=1, source_target_pairs={{0,256},{32,288},{64,320},{96,352},{128,384},{160,416},{192,448},{... | collective-permute-start | bytes 147464 | tf_op jit(solution)/shard_map/ppermute | solution.py:267
  189.1 17.9 %collective-permute-start.11 = (bf16[4,192,256]{2,1,0:T(8,128)(2,1)S(1)}, bf16[4,192,256]{2,1,0:T(8,128)(2,1)S(1)}, u32[]{:S(2)}, u32[]{:S(2)}) collective-permute-start(bf16[4,192,256]{2,1,0:T(8,128)(2,1)S(1)} %select_convert_fusion.1), channel_id=1, source_target_pairs={{0,64},{32,96},{64,0},{96,32},{128,192},{160,224},{192,128},{224,1... | collective-permute-start | bytes 1179656 | tf_op jit(solution)/shard_map/ppermute | solution.py:247
  195.9 12.1 %collective-permute-start.7 = (f32[2,1536]{1,0:T(2,128)S(1)}, f32[2,1536]{1,0:T(2,128)S(1)}, u32[]{:S(2)}, u32[]{:S(2)}) collective-permute-start(f32[2,1536]{1,0:T(2,128)S(1)} %select_select_fusion.3), channel_id=1, source_target_pairs={{0,96},{32,64},{64,32},{96,0},{128,224},{160,192},{192,160},{224,1... | collective-permute-start | bytes 36872 | tf_op jit(solution)/shard_map/ppermute | solution.py:267
  201.7 6.3 %collective-permute-start.5 = (f32[2,1536]{1,0:T(2,128)S(1)}, f32[2,1536]{1,0:T(2,128)S(1)}, u32[]{:S(2)}, u32[]{:S(2)}) collective-permute-start(f32[2,1536]{1,0:T(2,128)S(1)} %get-tuple-element.72), channel_id=1, source_target_pairs={{0,32},{32,0},{64,96},{96,64},{128,160},{160,128},{192,224},{224,1... | collective-permute-start | bytes 36872 | tf_op jit(solution)/shard_map/ppermute | solution.py:267
  203.7 4.4 %collective-permute-start.6 = (f32[2,1536]{1,0:T(2,128)S(1)}, f32[2,1536]{1,0:T(2,128)S(1)}, u32[]{:S(2)}, u32[]{:S(2)}) collective-permute-start(f32[2,1536]{1,0:T(2,128)S(1)} %get-tuple-element.73), channel_id=1, source_target_pairs={{0,64},{32,96},{64,0},{96,32},{128,192},{160,224},{192,128},{224,1... | collective-permute-start | bytes 36872 | tf_op jit(solution)/shard_map/ppermute | solution.py:267
  208.0 14.5 %copy-start.21 = (f32[2,16,1536]{2,1,0:T(8,128)S(1)}, f32[2,16,1536]{2,1,0:T(8,128)}, u32[]{:S(2)}) copy-start(f32[2,16,1536]{2,1,0:T(8,128)} %copy-done.20) | copy-start | bytes 589828
  209.0 25.0 %copy-start.17 = (f32[31,1536]{1,0:T(8,128)S(1)}, f32[31,1536]{1,0:T(8,128)}, u32[]{:S(2)}) copy-start(f32[31,1536]{1,0:T(8,128)} %taps.3) | copy-start | bytes 571396
  209.0 31.7 %all-to-all-start.4 = ((f32[32,2,1536]{2,1,0:T(2,128)}), f32[32,2,1536]{2,1,0:T(2,128)}, u32[]{:S(2)}, u32[]{:S(2)}) async-start(f32[32,2,1536]{2,1,0:T(2,128)} %broadcast_in_dim.8), calls=%async_computation.4 | async-start | bytes 786432 | tf_op jit(solution)/shard_map/all_to_all | solution.py:274
  218.8 15.3 %copy-start.14 = (f32[192,1536]{1,0:T(8,128)S(1)}, f32[192,1536]{1,0:T(8,128)}, u32[]{:S(2)}) copy-start(f32[192,1536]{1,0:T(8,128)} %copy-done.13) | copy-start | bytes 3538948
  220.0 12.8 %collective-permute-start.12 = (bf16[2,192,256]{2,1,0:T(8,128)(2,1)S(1)}, bf16[2,192,256]{2,1,0:T(8,128)(2,1)S(1)}, u32[]{:S(2)}, u32[]{:S(2)}) collective-permute-start(bf16[2,192,256]{2,1,0:T(8,128)(2,1)S(1)} %select_convert_fusion.2), channel_id=1, source_target_pairs={{0,128},{32,160},{64,192},{96,224},{128,0},{160,32},{192,64},{224,... | collective-permute-start | bytes 589832 | tf_op jit(solution)/shard_map/ppermute | solution.py:247
  222.5 11.5 %collective-permute-start.8 = (f32[16,1536]{1,0:T(8,128)S(1)}, f32[16,1536]{1,0:T(8,128)S(1)}, u32[]{:S(2)}, u32[]{:S(2)}) collective-permute-start(f32[16,1536]{1,0:T(8,128)S(1)} %get-tuple-element.69), channel_id=1, source_target_pairs={{0,1},{1,2},{2,3},{3,4},{4,5},{5,6},{6,7},{7,8},{8,9},{9,10},{10,1... | collective-permute-start | bytes 294920 | tf_op jit(solution)/shard_map/ppermute | solution.py:229
  225.6 8.4 %collective-permute-start.9 = (f32[16,1536]{1,0:T(8,128)S(1)}, f32[16,1536]{1,0:T(8,128)S(1)}, u32[]{:S(2)}, u32[]{:S(2)}) collective-permute-start(f32[16,1536]{1,0:T(8,128)S(1)} %get-tuple-element.68), channel_id=1, source_target_pairs={{1,0},{2,1},{3,2},{4,3},{5,4},{6,5},{7,6},{8,7},{9,8},{10,9},{11,1... | collective-permute-start | bytes 294920 | tf_op jit(solution)/shard_map/ppermute | solution.py:230
  242.6 21.6 %all-to-all-start.5 = ((f32[16,2,1536]{2,1,0:T(2,128)}), f32[16,2,1536]{2,1,0:T(2,128)S(1)}, u32[]{:S(2)}, u32[]{:S(2)}) async-start(f32[16,2,1536]{2,1,0:T(2,128)} %broadcast_in_dim.21), calls=%async_computation.5 | async-start | bytes 393216 | tf_op jit(solution)/shard_map/all_to_all | solution.py:274
  247.9 14.9 %collective-permute-start.13 = (bf16[1,192,256]{2,1,0:T(8,128)(2,1)S(1)}, bf16[1,192,256]{2,1,0:T(8,128)(2,1)S(1)}, u32[]{:S(2)}, u32[]{:S(2)}) collective-permute-start(bf16[1,192,256]{2,1,0:T(8,128)(2,1)S(1)} %select_convert_fusion.3), channel_id=1, source_target_pairs={{0,256},{32,288},{64,320},{96,352},{128,384},{160,416},{192,448},{... | collective-permute-start | bytes 294920 | tf_op jit(solution)/shard_map/ppermute | solution.py:247
  264.3 0.7 copy-start.25

commit v2 on v1

--- a/solution.py
+++ b/solution.py
@@ -19,9 +19,11 @@
 BF16 = jnp.bfloat16
 
 
-def call(body, outs, ins, scratch=()):
+def call(body, outs, ins, scratch=(), moves=None):
+    cost = None if moves is None else pl.CostEstimate(flops=0, transcendentals=0, bytes_accessed=moves)
     return pl.pallas_call(
         body,
+        cost_estimate=cost,
         out_shape=tuple(jax.ShapeDtypeStruct(shape, kind) for shape, kind in outs),
         in_specs=[SMEM if space == "s" else VMEM for space, _ in ins],
         out_specs=tuple(VMEM for _ in outs),
@@ -132,19 +134,40 @@
     branch[...] = jnp.dot(act[...], both_up, preferred_element_type=F32).astype(BF16)
 
 
-def keeper_grads(rows_in, cot_in, pre_grad, act, grads):
-    parts, twice, units = grads.shape
+def keeper_grads(place, rows_in, cot_in, pre_grad, act, kept, given, down, up):
+    parts, twice, _ = kept.shape
     part = twice // 2
-    down = lax.dot_general(rows_in[...], pre_grad[...], (((0,), (0,)), ((), ())), preferred_element_type=F32)
-    up = lax.dot_general(cot_in[...], act[...], (((0,), (0,)), ((), ())), preferred_element_type=F32)
-    for place, at in enumerate(turned(parts)):
-        grads[place, :part] = down[at * part : at * part + part]
-        grads[place, part:] = up[at * part : at * part + part]
+    core = place[0] % 2
+    down[...] = lax.dot_general(rows_in[...], pre_grad[...], (((0,), (0,)), ((), ())), preferred_element_type=F32)
+    up[...] = lax.dot_general(cot_in[...], act[...], (((0,), (0,)), ((), ())), preferred_element_type=F32)
+    for at in range(parts):
+        near = pl.ds(pl.multiple_of((2 * at + core) * part, part), part)
+        far = pl.ds(pl.multiple_of((2 * at + 1 - core) * part, part), part)
+        kept[at, :part] = down[near]
+        kept[at, part:] = up[near]
+        given[at, :part] = down[far].astype(BF16)
+        given[at, part:] = up[far].astype(BF16)
+
+
+def share_grads(place, kept, got, own, *given):
+    chip = place[0] // 2
+    for turn, out in enumerate((own,) + given):
+        for high in range(out.shape[0]):
+            at = 4 * high + ((chip % 4) ^ turn)
+            out[high] = (kept[at] + got[at].astype(F32)).astype(out.dtype)
+
+
+def pair_grads(place, own, first, second, third, kept, given):
+    high = place[0] // 8
+    for at, out in ((high, kept), (1 - high, given)):
+        total = own[at] + first[at].astype(F32) + second[at].astype(F32) + third[at].astype(F32)
+        out[...] = total.astype(out.dtype)
 
 
 def sum_gradients(
-    numbers, back, cot, summed, inv, gain, left, own, right, total, edges, sums, cells, frames_grad
+    numbers, place, back, cot, summed, inv, gain, left, own, right, total, edges, *rest
 ):
+    *quarters, sums, cells, frames_grad = rest
     frames, width = cot.shape
     gather = gather_matrix(segments(numbers), back.shape[0], frames)
     cells[:EDGE] = left[...].astype(F32)
@@ -184,6 +207,9 @@
     lax.fori_loop(0, width // LANES, column, 0)
     edges[0] = total[:EDGE]
     edges[1] = total[frames - EDGE :]
+    for turn, out in enumerate(quarters):
+        at = (place[0] // 4) ^ turn
+        out[...] = sums[pl.ds(pl.multiple_of(at * 8, 8), 8)]
 
 
 def input_gradient(left, own, right, taps, out, cells):
@@ -221,7 +247,7 @@
     for which in range(2):
         lanes = slice(which * units, which * units + units)
         down[which] = total[:share, lanes]
-        up[which] = total[share:, lanes].T
+        up[which] = total[share:, lanes]
 
 
 def from_sides(head, tail, axis):
@@ -231,43 +257,22 @@
     return left, right
 
 
-def turned(count):
-    bits = count.bit_length() - 1
-    return [sum(((at >> bit) & 1) << (bits - 1 - bit) for bit in range(bits)) for at in range(count)]
-
-
-def halved(cells, axis, kind):
-    count, me = lax.axis_size(axis), lax.axis_index(axis)
-    step = 1
-    while True:
-        half = cells.shape[0] // 2
-        upper = (me // step) % 2 == 1
-        given = jnp.where(upper, cells[:half], cells[half:]).astype(kind)
-        kept = jnp.where(upper, cells[half:], cells[:half])
-        got = lax.ppermute(given, axis, [(i, i ^ step) for i in range(count)])
-        step *= 2
-        if step == count:
-            return kept, got
-        cells = kept + got.astype(cells.dtype)
-
-
-def quartered(cells, axis):
-    count, me = lax.axis_size(axis), lax.axis_index(axis)
-    unit = count // 4
-    while unit > 0:
-        part = cells.shape[0] // 4
-        blocks = [cells[at * part : at * part + part] for at in range(4)]
-        mine = (me // unit) % 4
-
-        def block(turn):
-            place = mine ^ turn
-            low = jnp.where(place == 0, blocks[0], blocks[1])
-            return jnp.where(place < 2, low, jnp.where(place == 2, blocks[2], blocks[3]))
-
-        moved = [lax.ppermute(block(turn), axis, [(i, i ^ (turn * unit)) for i in range(count)]) for turn in (1, 2, 3)]
-        cells = (block(0) + moved[0]) + (moved[1] + moved[2])
-        unit //= 4
-    return cells
+def exchanged(blocks, axis, unit):
+    count = lax.axis_size(axis)
+    return [
+        lax.ppermute(block, axis, [(i, i ^ (turn * unit)) for i in range(count)])
+        for turn, block in enumerate(blocks[1:], 1)
+    ]
+
+
+def quarter(cells, mine):
+    part = cells.shape[0] // 4
+    blocks = [cells[at * part : at * part + part] for at in range(4)]
+    places = [mine ^ turn for turn in range(4)]
+    return [
+        jnp.where(at < 2, jnp.where(at == 0, blocks[0], blocks[1]), jnp.where(at == 2, blocks[2], blocks[3]))
+        for at in places
+    ]
 
 
 def swap(cells, axis):
@@ -300,6 +305,7 @@
         [((rows, width), BF16), ((frames, width), F32), ((frames, LANES), F32)],
         where + [("v", left), ("v", own), ("v", right), ("v", conv_kernel), ("v", gain)],
         [((frames + 2 * EDGE, width), F32), ((frames, width), BF16)],
+        moves=24_000_000,
     )
     got_rows = swap(send_rows, "ctx")
     back, pre_grad, act = call(
@@ -309,26 +315,48 @@
     )
     grad_back = swap(back, "ctx")
     (branch,) = call(keeper_branch, [((rows, width), BF16)], [("v", act), ("v", adapt_up)])
-    (parts,) = call(
+    share = width // dp
+    place = ("s", lax.axis_index("dp").astype(jnp.int32).reshape(1))
+    kept, given = call(
         keeper_grads,
-        [((dp, 2 * (width // dp), 2 * units), F32)],
-        [("v", got_rows), ("v", got_cot), ("v", pre_grad), ("v", act)],
-    )
-    kept, got = halved(parts, "dp", BF16)
-    grad_back, branch = lax.optimization_barrier((grad_back, branch))
+        [((dp // 2, 2 * share, 2 * units), F32), ((dp // 2, 2 * share, 2 * units), BF16)],
+        [place, ("v", got_rows), ("v", got_cot), ("v", pre_grad), ("v", act)],
+        [((width, 2 * units), F32), ((width, 2 * units), F32)],
+    )
+    (got,) = exchanged([kept, given], "dp", 1)
+    grad_scale = 1.0 / math.sqrt(dp * ctx * frames)
+    piece = (2 * share, 2 * units)
+    chips = call(
+        share_grads,
+        [((2,) + piece, F32)] + [((2,) + piece, BF16)] * 3,
+        [place, ("v", kept), ("v", got)],
+    )
+    got = exchanged(chips, "dp", 2)
+    kept, given = call(
+        pair_grads, [(piece, F32), (piece, BF16)], [place, ("v", chips[0])] + [("v", part) for part in got]
+    )
+    (got,) = exchanged([kept, given], "dp", 8)
+    grad_down, grad_up = call(
+        functools.partial(place_grads, grad_scale), [((2, share, units), F32)] * 2, [("v", kept), ("v", got)]
+    )
+    grad_back, branch, grad_down, grad_up = lax.optimization_barrier((grad_back, branch, grad_down, grad_up))
     branch_back = swap(branch, "ctx")
-    total, edges, sums = call(
+    total, edges, *sums = call(
         sum_gradients,
-        [((frames, width), F32), ((2, EDGE, width), F32), ((32, width), F32)],
+        [((frames, width), F32), ((2, EDGE, width), F32)] + [((8, width), F32)] * 4,
         where
+        + [place]
         + [("v", grad_back), ("v", cot), ("v", summed), ("v", inv), ("v", gain)]
         + [("v", left), ("v", own), ("v", right)],
-        [((frames + 2 * EDGE, width), F32), ((frames, width), F32)],
+        [((32, width), F32), ((frames + 2 * EDGE, width), F32), ((frames, width), F32)],
     )
     grad_left, grad_right = from_sides(edges[0], edges[1], "ctx")
-    mine, branch_back = lax.optimization_barrier((quartered(sums, "dp"), branch_back))
+    me = lax.axis_index("dp")
+    mine = sums[0] + sum(exchanged(sums, "dp", 4))
+    sums = quarter(mine, me % 4)
+    mine = sums[0] + sum(exchanged(sums, "dp", 1))
+    mine, branch_back = lax.optimization_barrier((mine, branch_back))
     mine = jnp.sum(spread_rows(mine, "ctx"), axis=0)
-    grad_scale = 1.0 / math.sqrt(dp * ctx * frames)
     (grad_input,) = call(
         input_gradient,
         [((frames, width), BF16)],
@@ -336,15 +364,9 @@
         [((frames + 2 * EDGE, width), F32)],
     )
     (output,) = call(add_branch, [((frames, width), BF16)], where + [("v", branch_back), ("v", summed)])
-    mine, grad_input, output = lax.optimization_barrier((mine, grad_input, output))
+    mine, grad_input = lax.optimization_barrier((mine, grad_input))
     reduced = spread_rows(mine * grad_scale, "dp").reshape(32, width)
-    share = width // dp
-    grad_down, grad_up = call(
-        functools.partial(place_grads, grad_scale),
-        [((2, share, units), F32), ((2, units, share), F32)],
-        [("v", kept[0]), ("v", got[0])],
-    )
-    return output[None], grad_input[None], reduced[:31], reduced[31], grad_down, grad_up
+    return output[None], grad_input[None], reduced[:31], reduced[31], grad_down, jnp.transpose(grad_up, (0, 2, 1))
 
 
 def solution(mesh):

time: 266 us -> 265 us (level)
  starting transfers between devices: 80.3 us -> 89.1 us
  other arithmetic: 9.25 us -> 1.98 us
  waiting for transfers between devices: 39.8 us -> 36.8 us
    all_to_all x4, waiting for transfers between devices: 21.9 us -> 8.07 us  [swap(): return lax.all_to_all(cells, axis, split_axis=0, concat_axis=0, tiled=True)]
    ppermute x10 -> x11, starting transfers between devices: 38.4 us -> 46.3 us  [exchanged(): lax.ppermute(block, axis, [(i, i ^ turn * unit) for i in range(count)])]
    add x5 -> x2, other arithmetic: 4.85 us -> 0.04 us  [the longest x1 0.03 us: local(): mine = sums[0] + sum(exchanged(sums, 'dp', 1))]
    ppermute x2, waiting for transfers between devices: 0.01 us -> 4.67 us  [from_sides(): left = lax.ppermute(tail, axis, [(i, i + 1) for i in range(count - 1)])]
    ppermute x2, waiting for transfers between devices: 0.17 us -> 3.35 us  [from_sides(): right = lax.ppermute(head, axis, [(i + 1, i) for i in range(count - 1)])]
    ppermute x10 -> x11, waiting for transfers between devices: 17.7 us -> 20.7 us  [exchanged(): lax.ppermute(block, axis, [(i, i ^ turn * unit) for i in range(count)])]
    unnamed x53 -> x42, local copies, waits for them, and re-layouts: 10.6 us -> 8.86 us
    pallas_call x9 -> x11, Pallas kernels: 25 us -> 26.4 us  [call(): pl.pallas_call(body, cost_estimate=cost, out_shape=tuple((jax.ShapeDtypeS...]
  transfers between devices with their start and end apart: 18 -> 19, of which waited for: 6 -> 10; matrix products, arithmetic and copies ran while one was open for 4% -> 1% of each run, Pallas kernels for 7% -> 8%
where the time goes in v2:
time: 265 us; the launch traced here: 263 us
  blocking collectives  94.6 us (36%)
  starting transfers between devices  89.1 us (34%)
  waiting for transfers between devices  36.8 us (14%)
  Pallas kernels  26.4 us (10%)
  local copies, waits for them, and re-layouts  12.8 us (5%)
    all_to_all x2, blocking collectives, swap(): return lax.all_to_all(cells, axis, split_axis=0, concat_axis=0, tiled=True)  94.6 us
    ppermute x11, starting transfers between devices, exchanged(): lax.ppermute(block, axis, [(i, i ^ turn * unit) for i in range(count)])  46.3 us
    all_to_all x4, starting transfers between devices, swap(): return lax.all_to_all(cells, axis, split_axis=0, concat_axis=0, tiled=True)  32.3 us
    pallas_call x11, Pallas kernels, call(): pl.pallas_call(body, cost_estimate=cost, out_shape=tuple((jax.ShapeDtypeS...  26.4 us
    ppermute x11, waiting for transfers between devices, exchanged(): lax.ppermute(block, axis, [(i, i ^ turn * unit) for i in range(count)])  20.7 us
    unnamed x42, local copies, waits for them, and re-layouts  8.86 us
    all_to_all x4, waiting for transfers between devices, swap(): return lax.all_to_all(cells, axis, split_axis=0, concat_axis=0, tiled=True)  8.07 us
    ppermute x2, starting transfers between devices, from_sides(): left = lax.ppermute(tail, axis, [(i, i + 1) for i in range(count - 1)])  7.89 us
  transfers between devices with their start and end apart: 19, of which 10 were waited for; matrix products, arithmetic and copies ran while one was open for 1% of the time, Pallas kernels for 8%

profile of v2, /device:TPU:1, one launch (start us, length us, event | category | flops | bytes accessed | tf_op | source)
XLA Modules:
  0.0 262.8 jit_solution(15319880206529713651)
XLA Ops:
  0.6 0.9 slice_bitcast_fusion.2
  1.5 4.8 %collective-permute-start = (bf16[16,1536]{1,0:T(8,128)(2,1)S(1)}, bf16[16,1536]{1,0:T(8,128)(2,1)S(1)}, u32[]{:S(2)}, u32[]{:S(2)}) collective-permute-start(bf16[16,1536]{1,0:T(8,128)(2,1)S(1)} %get-tuple-element.73), channel_id=1, source_target_pairs={{0,1},{1,2},{2,3},{3,4},{4,5},{5,6},{6,7},{7,8},{8,9},{9,10},{10,1... | collective-permute-start | bytes 147464 | tf_op jit(solution)/shard_map/ppermute | solution.py:255
  6.4 1.3 collective-permute-start.1
  7.7 0.8 pad_add_fusion.numbers
  9.1 1.1 copy-done.6
  10.2 1.5 shard_map.136
  11.8 4.9 %shard_map.137 = (bf16[512,1536]{1,0:T(8,128)(2,1)S(1)}, f32[192,1536]{1,0:T(8,128)S(1)}, f32[192,128]{1,0:T(8,128)S(1)}) custom-call(s32[96]{0:T(128)S(1)} %pad_add_fusion.numbers, bf16[16,1536]{1,0:T(8,128)(2,1)S(1)} %collective-permute-done.left, bf16[192,1536]{1,0:T(8,128)(2,1)S(1)} %bitcast.31, bf16[16,1536]{1,0:T(8,128)(2,1)S(1)} %collective-permute-done.1.right, ...), custom_call_target="tpu_custom_call" | custom-call | bytes 24000000 | tf_op jit(solution)/shard_map/pallas_call | solution.py:24
  16.8 49.5 %all_to_all.56 = bf16[32,16,1536]{2,1,0:T(8,128)(2,1)S(1)} all-to-all(bf16[32,16,1536]{2,1,0:T(8,128)(2,1)S(1)} %bitcast.36), channel_id=1, replica_groups=mesh['dp'=16,'ctx'=32] {'ctx'}, dimensions={0} | all-to-all | bytes 3145728 | tf_op jit(solution)/shard_map/all_to_all | solution.py:279
  66.3 45.1 %all_to_all.57 = bf16[32,16,1536]{2,1,0:T(8,128)(2,1)S(1)} all-to-all(bf16[32,16,1536]{2,1,0:T(8,128)(2,1)S(1)} %bitcast.30), channel_id=1, replica_groups=mesh['dp'=16,'ctx'=32] {'ctx'}, dimensions={0} | all-to-all | bytes 3145728 | tf_op jit(solution)/shard_map/all_to_all | solution.py:279
  111.4 1.5 shard_map.138
  113.7 1.2 copy-done.8
  114.8 8.5 %all-to-all-start.2 = ((bf16[32,16,1536]{2,1,0:T(8,128)(2,1)}), bf16[32,16,1536]{2,1,0:T(8,128)(2,1)}, u32[]{:S(2)}, u32[]{:S(2)}) async-start(bf16[32,16,1536]{2,1,0:T(8,128)(2,1)} %bitcast.35), calls=%async_computation.2 | async-start | bytes 3145728 | tf_op jit(solution)/shard_map/all_to_all | solution.py:279
  123.4 0.9 copy-done.15
  124.3 1.6 shard_map.140
  125.9 3.2 %collective-permute-start.2 = (bf16[8,192,256]{2,1,0:T(8,128)(2,1)S(1)}, bf16[8,192,256]{2,1,0:T(8,128)(2,1)S(1)}, u32[]{:S(2)}, u32[]{:S(2)}) collective-permute-start(bf16[8,192,256]{2,1,0:T(8,128)(2,1)S(1)} %get-tuple-element.47), channel_id=1, source_target_pairs={{0,32},{32,0},{64,96},{96,64},{128,160},{160,128},{192,224},{224,1... | collective-permute-start | bytes 2359304 | tf_op jit(solution)/shard_map/ppermute | solution.py:263
  129.1 1.9 collective-permute-done.2.got
  131.1 3.4 %collective-permute-start.3 = (bf16[2,192,256]{2,1,0:T(8,128)(2,1)S(1)}, bf16[2,192,256]{2,1,0:T(8,128)(2,1)S(1)}, u32[]{:S(2)}, u32[]{:S(2)}) collective-permute-start(bf16[2,192,256]{2,1,0:T(8,128)(2,1)S(1)} %get-tuple-element.49), channel_id=1, source_target_pairs={{0,64},{32,96},{64,0},{96,32},{128,192},{160,224},{192,128},{224,1... | collective-permute-start | bytes 589832 | tf_op jit(solution)/shard_map/ppermute | solution.py:263
  134.5 4.2 %collective-permute-start.4 = (bf16[2,192,256]{2,1,0:T(8,128)(2,1)S(1)}, bf16[2,192,256]{2,1,0:T(8,128)(2,1)S(1)}, u32[]{:S(2)}, u32[]{:S(2)}) collective-permute-start(bf16[2,192,256]{2,1,0:T(8,128)(2,1)S(1)} %get-tuple-element.50), channel_id=1, source_target_pairs={{0,128},{32,160},{64,192},{96,224},{128,0},{160,32},{192,64},{224,... | collective-permute-start | bytes 589832 | tf_op jit(solution)/shard_map/ppermute | solution.py:263
  138.7 1.9 collective-permute-start.5
  140.6 11.0 %collective-permute-done.4.second = bf16[2,192,256]{2,1,0:T(8,128)(2,1)S(1)} collective-permute-done((bf16[2,192,256]{2,1,0:T(8,128)(2,1)S(1)}, bf16[2,192,256]{2,1,0:T(8,128)(2,1)S(1)}, u32[]{:S(2)}, u32[]{:S(2)}) %collective-permute-start.4) | collective-permute-done | bytes 196640 | tf_op jit(solution)/shard_map/ppermute | solution.py:263
  151.7 6.6 %collective-permute-start.6 = (bf16[192,256]{1,0:T(8,128)(2,1)S(1)}, bf16[192,256]{1,0:T(8,128)(2,1)S(1)}, u32[]{:S(2)}, u32[]{:S(2)}) collective-permute-start(bf16[192,256]{1,0:T(8,128)(2,1)S(1)} %get-tuple-element.53), channel_id=1, source_target_pairs={{0,256},{32,288},{64,320},{96,352},{128,384},{160,416},{192,448},{... | collective-permute-start | bytes 294920 | tf_op jit(solution)/shard_map/ppermute | solution.py:263
  158.4 1.8 shard_map.139
  160.1 0.9 collective-permute-done.6.got
  161.7 9.6 %all-to-all-start.3 = ((bf16[32,16,1536]{2,1,0:T(8,128)(2,1)}), bf16[32,16,1536]{2,1,0:T(8,128)(2,1)S(1)}, u32[]{:S(2)}, u32[]{:S(2)}) async-start(bf16[32,16,1536]{2,1,0:T(8,128)(2,1)} %bitcast.13), calls=%async_computation.3 | async-start | bytes 3145728 | tf_op jit(solution)/shard_map/all_to_all | solution.py:279
  171.3 1.1 copy-done.7
  172.4 0.9 copy-done.19
  173.3 7.6 %shard_map.144 = (f32[192,1536]{1,0:T(8,128)S(1)}, f32[2,16,1536]{2,1,0:T(8,128)S(1)}, f32[8,1536]{1,0:T(8,128)S(1)}, f32[8,1536]{1,0:T(8,128)}, f32[8,1536]{1,0:T(8,128)}, /*index=5*/f32[8,1536]{1,0:T(8,128)}) custom-call(s32[96]{0:T(128)S(1)} %pad_add_fusion.numbers, s32[1]{0:T(128)} %bitcast.2.place, bf16[512,1536]{1,0:T(8,128)(2,1)} %bitcast.12.back, ...), custom_call_target="tpu_custom_call" | custom-call | tf_op jit(solution)/shard_map/pallas_call | solution.py:24
  180.9 1.0 copy-done.9
  182.6 8.1 %collective-permute-start.7 = (f32[8,1536]{1,0:T(8,128)}, f32[8,1536]{1,0:T(8,128)S(1)}, u32[]{:S(2)}, u32[]{:S(2)}) collective-permute-start(f32[8,1536]{1,0:T(8,128)} %get-tuple-element.60), channel_id=1, source_target_pairs={{0,128},{32,160},{64,192},{96,224},{128,0},{160,32},{192,64},{224,... | collective-permute-start | bytes 147464 | tf_op jit(solution)/shard_map/ppermute | solution.py:263
  190.7 6.7 %collective-permute-start.8 = (f32[8,1536]{1,0:T(8,128)}, f32[8,1536]{1,0:T(8,128)S(1)}, u32[]{:S(2)}, u32[]{:S(2)}) collective-permute-start(f32[8,1536]{1,0:T(8,128)} %get-tuple-element.61), channel_id=1, source_target_pairs={{0,256},{32,288},{64,320},{96,352},{128,384},{160,416},{192,448},{... | collective-permute-start | bytes 147464 | tf_op jit(solution)/shard_map/ppermute | solution.py:263
  197.4 1.9 collective-permute-start.9
  200.0 4.9 %collective-permute-done.9 = f32[8,1536]{1,0:T(8,128)S(1)} collective-permute-done((f32[8,1536]{1,0:T(8,128)}, f32[8,1536]{1,0:T(8,128)S(1)}, u32[]{:S(2)}, u32[]{:S(2)}) %collective-permute-start.9) | collective-permute-done | bytes 49184 | tf_op jit(solution)/shard_map/ppermute | solution.py:263
  204.9 4.8 %collective-permute-start.10 = (f32[2,1536]{1,0:T(2,128)S(1)}, f32[2,1536]{1,0:T(2,128)S(1)}, u32[]{:S(2)}, u32[]{:S(2)}) collective-permute-start(f32[2,1536]{1,0:T(2,128)S(1)} %get-tuple-element.77), channel_id=1, source_target_pairs={{0,32},{32,0},{64,96},{96,64},{128,160},{160,128},{192,224},{224,1... | collective-permute-start | bytes 36872 | tf_op jit(solution)/shard_map/ppermute | solution.py:263
  209.7 1.9 collective-permute-start.11
  211.7 3.5 %collective-permute-start.12 = (f32[2,1536]{1,0:T(2,128)S(1)}, f32[2,1536]{1,0:T(2,128)S(1)}, u32[]{:S(2)}, u32[]{:S(2)}) collective-permute-start(f32[2,1536]{1,0:T(2,128)S(1)} %select_select_fusion), channel_id=1, source_target_pairs={{0,96},{32,64},{64,32},{96,0},{128,224},{160,192},{192,160},{224,1... | collective-permute-start | bytes 36872 | tf_op jit(solution)/shard_map/ppermute | solution.py:263
  215.3 1.4 collective-permute-done.12
  216.7 0.8 broadcast_in_dim.9
  217.6 9.6 %all-to-all-start.4 = ((f32[32,2,1536]{2,1,0:T(2,128)}), f32[32,2,1536]{2,1,0:T(2,128)}, u32[]{:S(2)}, u32[]{:S(2)}) async-start(f32[32,2,1536]{2,1,0:T(2,128)} %broadcast_in_dim.9), calls=%async_computation.4 | async-start | bytes 786432 | tf_op jit(solution)/shard_map/all_to_all | solution.py:279
  227.3 3.1 %collective-permute-start.13 = (f32[16,1536]{1,0:T(8,128)S(1)}, f32[16,1536]{1,0:T(8,128)S(1)}, u32[]{:S(2)}, u32[]{:S(2)}) collective-permute-start(f32[16,1536]{1,0:T(8,128)S(1)} %get-tuple-element.75), channel_id=1, source_target_pairs={{0,1},{1,2},{2,3},{3,4},{4,5},{5,6},{6,7},{7,8},{8,9},{9,10},{10,1... | collective-permute-start | bytes 294920 | tf_op jit(solution)/shard_map/ppermute | solution.py:255
  230.3 1.3 collective-permute-start.14
  231.6 4.7 %collective-permute-done.13.left = f32[16,1536]{1,0:T(8,128)S(1)} collective-permute-done((f32[16,1536]{1,0:T(8,128)S(1)}, f32[16,1536]{1,0:T(8,128)S(1)}, u32[]{:S(2)}, u32[]{:S(2)}) %collective-permute-start.13) | collective-permute-done | bytes 98336 | tf_op jit(solution)/shard_map/ppermute | solution.py:255
  236.3 3.2 %collective-permute-done.14.right = f32[16,1536]{1,0:T(8,128)S(1)} collective-permute-done((f32[16,1536]{1,0:T(8,128)S(1)}, f32[16,1536]{1,0:T(8,128)S(1)}, u32[]{:S(2)}, u32[]{:S(2)}) %collective-permute-start.14) | collective-permute-done | bytes 98336 | tf_op jit(solution)/shard_map/ppermute | solution.py:256
  239.5 1.3 copy-done.10
  240.8 4.4 %shard_map.146 = bf16[192,1536]{1,0:T(8,128)(2,1)} custom-call(f32[16,1536]{1,0:T(8,128)S(1)} %collective-permute-done.13.left, f32[192,1536]{1,0:T(8,128)S(1)} %copy-done.10, f32[16,1536]{1,0:T(8,128)S(1)} %collective-permute-done.14.right, f32[31,1536]{1,0:T(8,128)S(1)} %copy-done.13), custom_call_target="tpu_custom_call" | custom-call | tf_op jit(solution)/shard_map/pallas_call | solution.py:24
  245.2 1.1 reduce_sum.9
  247.0 4.6 %all-to-all-start.5 = ((f32[16,2,1536]{2,1,0:T(2,128)}), f32[16,2,1536]{2,1,0:T(2,128)S(1)}, u32[]{:S(2)}, u32[]{:S(2)}) async-start(f32[16,2,1536]{2,1,0:T(2,128)} %broadcast_in_dim.21), calls=%async_computation.5 | async-start | bytes 393216 | tf_op jit(solution)/shard_map/all_to_all | solution.py:279
  251.6 2.3 shard_map.145
  253.9 8.1 %all-to-all-done.5 = f32[16,2,1536]{2,1,0:T(2,128)S(1)} async-done(((f32[16,2,1536]{2,1,0:T(2,128)}), f32[16,2,1536]{2,1,0:T(2,128)S(1)}, u32[]{:S(2)}, u32[]{:S(2)}) %all-to-all-start.5) | async-done | bytes 196640 | tf_op jit(solution)/shard_map/all_to_all | solution.py:279
  (59 shorter events, 5.5 us)
Async XLA Ops:
  0.6 11.2 %copy-start.4 = (bf16[1,192,1536]{2,1,0:T(8,128)(2,1)S(1)}, bf16[1,192,1536]{2,1,0:T(8,128)(2,1)}, u32[]{:S(2)}) copy-start(bf16[1,192,1536]{2,1,0:T(8,128)(2,1)} %param.9) | copy-start | bytes 1769476
  1.5 10.1 %collective-permute-start = (bf16[16,1536]{1,0:T(8,128)(2,1)S(1)}, bf16[16,1536]{1,0:T(8,128)(2,1)S(1)}, u32[]{:S(2)}, u32[]{:S(2)}) collective-permute-start(bf16[16,1536]{1,0:T(8,128)(2,1)S(1)} %get-tuple-element.73), channel_id=1, source_target_pairs={{0,1},{1,2},{2,3},{3,4},{4,5},{5,6},{6,7},{7,8},{8,9},{9,10},{10,1... | collective-permute-start | bytes 147464 | tf_op jit(solution)/shard_map/ppermute | solution.py:255
  6.4 5.5 %collective-permute-start.1 = (bf16[16,1536]{1,0:T(8,128)(2,1)S(1)}, bf16[16,1536]{1,0:T(8,128)(2,1)S(1)}, u32[]{:S(2)}, u32[]{:S(2)}) collective-permute-start(bf16[16,1536]{1,0:T(8,128)(2,1)S(1)} %get-tuple-element.72), channel_id=1, source_target_pairs={{1,0},{2,1},{3,2},{4,3},{5,4},{6,5},{7,6},{8,7},{9,8},{10,9},{11,1... | collective-permute-start | bytes 147464 | tf_op jit(solution)/shard_map/ppermute | solution.py:256
  9.1 1.1 copy-start.6
  10.2 1.6 copy-start.12
  16.8 49.6 %copy-start = (f32[192,1536]{1,0:T(8,128)}, f32[192,1536]{1,0:T(8,128)S(1)}, u32[]{:S(2)}) copy-start(f32[192,1536]{1,0:T(8,128)S(1)} %get-tuple-element.57.summed) | copy-start | bytes 3538948
  16.8 49.5 %copy-start.18 = (f32[192,128]{1,0:T(8,128)}, f32[192,128]{1,0:T(8,128)S(1)}, u32[]{:S(2)}) copy-start(f32[192,128]{1,0:T(8,128)S(1)} %get-tuple-element.58.inv) | copy-start | bytes 294916
  66.3 45.1 %copy-start.2 = (bf16[2,128,1536]{2,1,0:T(8,128)(2,1)S(1)}, bf16[2,128,1536]{2,1,0:T(8,128)(2,1)}, u32[]{:S(2)}) copy-start(bf16[2,128,1536]{2,1,0:T(8,128)(2,1)} %up.3) | copy-start | bytes 2359300
  66.3 45.1 %copy-start.11 = (bf16[2,1536,128]{2,1,0:T(8,128)(2,1)S(1)}, bf16[2,1536,128]{2,1,0:T(8,128)(2,1)}, u32[]{:S(2)}) copy-start(bf16[2,1536,128]{2,1,0:T(8,128)(2,1)} %down.1) | copy-start | bytes 2359300
  113.0 0.7 copy-start.14
  113.7 1.2 copy-start.8
  114.8 46.9 %all-to-all-start.2 = ((bf16[32,16,1536]{2,1,0:T(8,128)(2,1)}), bf16[32,16,1536]{2,1,0:T(8,128)(2,1)}, u32[]{:S(2)}, u32[]{:S(2)}) async-start(bf16[32,16,1536]{2,1,0:T(8,128)(2,1)} %bitcast.35), calls=%async_computation.2 | async-start | bytes 3145728 | tf_op jit(solution)/shard_map/all_to_all | solution.py:279
  123.3 1.0 copy-start.15
  125.9 5.1 %collective-permute-start.2 = (bf16[8,192,256]{2,1,0:T(8,128)(2,1)S(1)}, bf16[8,192,256]{2,1,0:T(8,128)(2,1)S(1)}, u32[]{:S(2)}, u32[]{:S(2)}) collective-permute-start(bf16[8,192,256]{2,1,0:T(8,128)(2,1)S(1)} %get-tuple-element.47), channel_id=1, source_target_pairs={{0,32},{32,0},{64,96},{96,64},{128,160},{160,128},{192,224},{224,1... | collective-permute-start | bytes 2359304 | tf_op jit(solution)/shard_map/ppermute | solution.py:263
  131.0 27.4 %copy-start.3 = (bf16[2,128,1536]{2,1,0:T(8,128)(2,1)S(1)}, bf16[2,128,1536]{2,1,0:T(8,128)(2,1)}, u32[]{:S(2)}) copy-start(bf16[2,128,1536]{2,1,0:T(8,128)(2,1)} %up.3) | copy-start | bytes 2359300
  131.1 9.5 %collective-permute-start.3 = (bf16[2,192,256]{2,1,0:T(8,128)(2,1)S(1)}, bf16[2,192,256]{2,1,0:T(8,128)(2,1)S(1)}, u32[]{:S(2)}, u32[]{:S(2)}) collective-permute-start(bf16[2,192,256]{2,1,0:T(8,128)(2,1)S(1)} %get-tuple-element.49), channel_id=1, source_target_pairs={{0,64},{32,96},{64,0},{96,32},{128,192},{160,224},{192,128},{224,1... | collective-permute-start | bytes 589832 | tf_op jit(solution)/shard_map/ppermute | solution.py:263
  134.5 17.2 %collective-permute-start.4 = (bf16[2,192,256]{2,1,0:T(8,128)(2,1)S(1)}, bf16[2,192,256]{2,1,0:T(8,128)(2,1)S(1)}, u32[]{:S(2)}, u32[]{:S(2)}) collective-permute-start(bf16[2,192,256]{2,1,0:T(8,128)(2,1)S(1)} %get-tuple-element.50), channel_id=1, source_target_pairs={{0,128},{32,160},{64,192},{96,224},{128,0},{160,32},{192,64},{224,... | collective-permute-start | bytes 589832 | tf_op jit(solution)/shard_map/ppermute | solution.py:263
  138.7 13.0 %collective-permute-start.5 = (bf16[2,192,256]{2,1,0:T(8,128)(2,1)S(1)}, bf16[2,192,256]{2,1,0:T(8,128)(2,1)S(1)}, u32[]{:S(2)}, u32[]{:S(2)}) collective-permute-start(bf16[2,192,256]{2,1,0:T(8,128)(2,1)S(1)} %get-tuple-element.51), channel_id=1, source_target_pairs={{0,192},{32,224},{64,128},{96,160},{128,64},{160,96},{192,0},{224,... | collective-permute-start | bytes 589832 | tf_op jit(solution)/shard_map/ppermute | solution.py:263
  151.7 9.3 %collective-permute-start.6 = (bf16[192,256]{1,0:T(8,128)(2,1)S(1)}, bf16[192,256]{1,0:T(8,128)(2,1)S(1)}, u32[]{:S(2)}, u32[]{:S(2)}) collective-permute-start(bf16[192,256]{1,0:T(8,128)(2,1)S(1)} %get-tuple-element.53), channel_id=1, source_target_pairs={{0,256},{32,288},{64,320},{96,352},{128,384},{160,416},{192,448},{... | collective-permute-start | bytes 294920 | tf_op jit(solution)/shard_map/ppermute | solution.py:263
  161.7 9.6 %copy-start.1 = (f32[192,1536]{1,0:T(8,128)S(1)}, f32[192,1536]{1,0:T(8,128)}, u32[]{:S(2)}) copy-start(f32[192,1536]{1,0:T(8,128)} %copy-done) | copy-start | bytes 3538948
  161.7 9.6 %copy-start.5 = (bf16[1,192,1536]{2,1,0:T(8,128)(2,1)S(1)}, bf16[1,192,1536]{2,1,0:T(8,128)(2,1)}, u32[]{:S(2)}) copy-start(bf16[1,192,1536]{2,1,0:T(8,128)(2,1)} %param.9) | copy-start | bytes 1769476
  161.7 55.0 %all-to-all-start.3 = ((bf16[32,16,1536]{2,1,0:T(8,128)(2,1)}), bf16[32,16,1536]{2,1,0:T(8,128)(2,1)S(1)}, u32[]{:S(2)}, u32[]{:S(2)}) async-start(bf16[32,16,1536]{2,1,0:T(8,128)(2,1)} %bitcast.13), calls=%async_computation.3 | async-start | bytes 3145728 | tf_op jit(solution)/shard_map/all_to_all | solution.py:279
  171.3 1.1 copy-start.7
  172.4 0.9 copy-start.19
  180.9 1.0 copy-start.9
  181.9 0.7 copy-start.16
  182.6 56.9 %copy-start.13 = (f32[31,1536]{1,0:T(8,128)S(1)}, f32[31,1536]{1,0:T(8,128)}, u32[]{:S(2)}) copy-start(f32[31,1536]{1,0:T(8,128)} %taps.3) | copy-start | bytes 571396
  182.6 44.6 %copy-start.17 = (f32[2,16,1536]{2,1,0:T(8,128)S(1)}, f32[2,16,1536]{2,1,0:T(8,128)}, u32[]{:S(2)}) copy-start(f32[2,16,1536]{2,1,0:T(8,128)} %copy-done.16) | copy-start | bytes 589828
  182.6 16.8 %collective-permute-start.7 = (f32[8,1536]{1,0:T(8,128)}, f32[8,1536]{1,0:T(8,128)S(1)}, u32[]{:S(2)}, u32[]{:S(2)}) collective-permute-start(f32[8,1536]{1,0:T(8,128)} %get-tuple-element.60), channel_id=1, source_target_pairs={{0,128},{32,160},{64,192},{96,224},{128,0},{160,32},{192,64},{224,... | collective-permute-start | bytes 147464 | tf_op jit(solution)/shard_map/ppermute | solution.py:263
  190.7 9.2 %collective-permute-start.8 = (f32[8,1536]{1,0:T(8,128)}, f32[8,1536]{1,0:T(8,128)S(1)}, u32[]{:S(2)}, u32[]{:S(2)}) collective-permute-start(f32[8,1536]{1,0:T(8,128)} %get-tuple-element.61), channel_id=1, source_target_pairs={{0,256},{32,288},{64,320},{96,352},{128,384},{160,416},{192,448},{... | collective-permute-start | bytes 147464 | tf_op jit(solution)/shard_map/ppermute | solution.py:263
  197.4 7.4 %collective-permute-start.9 = (f32[8,1536]{1,0:T(8,128)}, f32[8,1536]{1,0:T(8,128)S(1)}, u32[]{:S(2)}, u32[]{:S(2)}) collective-permute-start(f32[8,1536]{1,0:T(8,128)} %get-tuple-element.62), channel_id=1, source_target_pairs={{0,384},{32,416},{64,448},{96,480},{128,256},{160,288},{192,320},{... | collective-permute-start | bytes 147464 | tf_op jit(solution)/shard_map/ppermute | solution.py:263
  204.9 10.4 %collective-permute-start.10 = (f32[2,1536]{1,0:T(2,128)S(1)}, f32[2,1536]{1,0:T(2,128)S(1)}, u32[]{:S(2)}, u32[]{:S(2)}) collective-permute-start(f32[2,1536]{1,0:T(2,128)S(1)} %get-tuple-element.77), channel_id=1, source_target_pairs={{0,32},{32,0},{64,96},{96,64},{128,160},{160,128},{192,224},{224,1... | collective-permute-start | bytes 36872 | tf_op jit(solution)/shard_map/ppermute | solution.py:263
  209.7 5.5 %collective-permute-start.11 = (f32[2,1536]{1,0:T(2,128)S(1)}, f32[2,1536]{1,0:T(2,128)S(1)}, u32[]{:S(2)}, u32[]{:S(2)}) collective-permute-start(f32[2,1536]{1,0:T(2,128)S(1)} %get-tuple-element.76), channel_id=1, source_target_pairs={{0,64},{32,96},{64,0},{96,32},{128,192},{160,224},{192,128},{224,1... | collective-permute-start | bytes 36872 | tf_op jit(solution)/shard_map/ppermute | solution.py:263
  211.7 5.0 %collective-permute-start.12 = (f32[2,1536]{1,0:T(2,128)S(1)}, f32[2,1536]{1,0:T(2,128)S(1)}, u32[]{:S(2)}, u32[]{:S(2)}) collective-permute-start(f32[2,1536]{1,0:T(2,128)S(1)} %select_select_fusion), channel_id=1, source_target_pairs={{0,96},{32,64},{64,32},{96,0},{128,224},{160,192},{192,160},{224,1... | collective-permute-start | bytes 36872 | tf_op jit(solution)/shard_map/ppermute | solution.py:263
  217.6 27.6 %all-to-all-start.4 = ((f32[32,2,1536]{2,1,0:T(2,128)}), f32[32,2,1536]{2,1,0:T(2,128)}, u32[]{:S(2)}, u32[]{:S(2)}) async-start(f32[32,2,1536]{2,1,0:T(2,128)} %broadcast_in_dim.9), calls=%async_computation.4 | async-start | bytes 786432 | tf_op jit(solution)/shard_map/all_to_all | solution.py:279
  227.3 9.1 %collective-permute-start.13 = (f32[16,1536]{1,0:T(8,128)S(1)}, f32[16,1536]{1,0:T(8,128)S(1)}, u32[]{:S(2)}, u32[]{:S(2)}) collective-permute-start(f32[16,1536]{1,0:T(8,128)S(1)} %get-tuple-element.75), channel_id=1, source_target_pairs={{0,1},{1,2},{2,3},{3,4},{4,5},{5,6},{6,7},{7,8},{8,9},{9,10},{10,1... | collective-permute-start | bytes 294920 | tf_op jit(solution)/shard_map/ppermute | solution.py:255
  230.3 9.2 %collective-permute-start.14 = (f32[16,1536]{1,0:T(8,128)S(1)}, f32[16,1536]{1,0:T(8,128)S(1)}, u32[]{:S(2)}, u32[]{:S(2)}) collective-permute-start(f32[16,1536]{1,0:T(8,128)S(1)} %get-tuple-element.74), channel_id=1, source_target_pairs={{1,0},{2,1},{3,2},{4,3},{5,4},{6,5},{7,6},{8,7},{9,8},{10,9},{11,1... | collective-permute-start | bytes 294920 | tf_op jit(solution)/shard_map/ppermute | solution.py:256
  239.5 1.3 copy-start.10
  247.0 14.9 %all-to-all-start.5 = ((f32[16,2,1536]{2,1,0:T(2,128)}), f32[16,2,1536]{2,1,0:T(2,128)S(1)}, u32[]{:S(2)}, u32[]{:S(2)}) async-start(f32[16,2,1536]{2,1,0:T(2,128)} %broadcast_in_dim.21), calls=%async_computation.5 | async-start | bytes 393216 | tf_op jit(solution)/shard_map/all_to_all | solution.py:279
  262.1 0.7 copy-start.20

commit v3 on v2

--- a/solution.py
+++ b/solution.py
@@ -19,11 +19,9 @@
 BF16 = jnp.bfloat16
 
 
-def call(body, outs, ins, scratch=(), moves=None):
-    cost = None if moves is None else pl.CostEstimate(flops=0, transcendentals=0, bytes_accessed=moves)
+def call(body, outs, ins, scratch=()):
     return pl.pallas_call(
         body,
-        cost_estimate=cost,
         out_shape=tuple(jax.ShapeDtypeStruct(shape, kind) for shape, kind in outs),
         in_specs=[SMEM if space == "s" else VMEM for space, _ in ins],
         out_specs=tuple(VMEM for _ in outs),
@@ -68,21 +66,19 @@
     return cells if by == 0 else pltpu.roll(cells, cells.shape[0] - by, 0)
 
 
-def send_cotangent(numbers, cot, send):
+def conv_and_norm(numbers, left, own, right, cot, taps, gain, send, summed, inv, cells, normed):
+    frames, width = own.shape
+    rows = send.shape[0] * BLOCK
+    blocks = (send.shape[0], BLOCK, width)
     found = segments(numbers)
-    rows = send.shape[0]
-    spread = scatter_matrix(found, rows, cot.shape[0])
+    spread = scatter_matrix(found, rows, frames)
     row = lax.broadcasted_iota(jnp.int32, (rows, LANES), 0)
     mark = jnp.zeros((rows, LANES), F32)
     for _, _, keeper, which in found:
         mark = jnp.where(row == keeper * BLOCK + BLOCK - 1, which.astype(F32), mark)
     moved = jnp.dot(spread, cot[...], preferred_element_type=F32)
-    send[...] = moved.astype(BF16)
-    send[:, :LANES] = (moved[:, :LANES] + mark).astype(BF16)
-
-
-def conv_and_norm(numbers, left, own, right, taps, gain, send, summed, inv, cells, normed):
-    frames, width = own.shape
+    moved = jnp.concatenate([moved[:, :LANES] + mark, moved[:, LANES:]], axis=1)
+    send[:, BLOCK:] = moved.astype(BF16).reshape(blocks)
     cells[:EDGE] = left[...].astype(F32)
     cells[EDGE : EDGE + frames] = own[...].astype(F32)
     cells[EDGE + frames :] = right[...].astype(F32)
@@ -108,11 +104,16 @@
     scale = lax.rsqrt(jnp.sum(squares, axis=1, keepdims=True) * (1.0 / width) + 1e-06)
     inv[...] = jnp.broadcast_to(scale, inv.shape)
     normed[...] = (summed[...] * scale * gain[...]).astype(BF16)
-    spread = scatter_matrix(segments(numbers), send.shape[0], frames)
-    send[...] = jnp.dot(spread, normed[...], preferred_element_type=F32).astype(BF16)
-
-
-def keeper_back(rows_in, cot_in, down, up, back, pre_grad, act):
+    send[:, :BLOCK] = jnp.dot(spread, normed[...], preferred_element_type=F32).astype(BF16).reshape(blocks)
+
+
+def received(got):
+    shape = (got.shape[0] * BLOCK, got.shape[2])
+    return got[:, :BLOCK].reshape(shape), got[:, BLOCK:].reshape(shape)
+
+
+def keeper_back(got, down, up, back, pre_grad, act):
+    rows_in, cot_in = received(got)
     rows, width = rows_in.shape
     units = down.shape[2]
     marks = cot_in[:, :units].astype(F32).reshape(rows // BLOCK, BLOCK, units)
@@ -120,8 +121,8 @@
     keep = jnp.concatenate([1.0 - marks, marks], axis=1)
     both_down = jnp.concatenate([down[0], down[1]], axis=1)
     both_up = up[...].reshape(2 * units, width)
-    pre = jnp.dot(rows_in[...], both_down, preferred_element_type=F32)
-    slope_of = lax.dot_general(cot_in[...], both_up, (((1,), (1,)), ((), ())), preferred_element_type=F32)
+    pre = jnp.dot(rows_in, both_down, preferred_element_type=F32)
+    slope_of = lax.dot_general(cot_in, both_up, (((1,), (1,)), ((), ())), preferred_element_type=F32)
     sig = jax.nn.sigmoid(pre)
     act[...] = (keep * (pre * sig)).astype(BF16)
     grads = (keep * (slope_of * (sig * (1.0 + pre * (1.0 - sig))))).astype(BF16)
@@ -129,17 +130,19 @@
     back[...] = lax.dot_general(grads, both_down, (((1,), (1,)), ((), ())), preferred_element_type=F32).astype(BF16)
 
 
-def keeper_branch(act, up, branch):
-    both_up = up[...].reshape(act.shape[1], branch.shape[1])
-    branch[...] = jnp.dot(act[...], both_up, preferred_element_type=F32).astype(BF16)
-
-
-def keeper_grads(place, rows_in, cot_in, pre_grad, act, kept, given, down, up):
+def sum_last_rows(back, out):
+    row = lax.broadcasted_iota(jnp.int32, (out.shape[0], back.shape[0]), 1)
+    last = jnp.where(row % BLOCK == BLOCK - 1, 1.0, 0.0).astype(BF16)
+    out[...] = jnp.dot(last, back[...], preferred_element_type=F32)
+
+
+def keeper_grads(place, got, pre_grad, act, kept, given, down, up):
     parts, twice, _ = kept.shape
     part = twice // 2
     core = place[0] % 2
-    down[...] = lax.dot_general(rows_in[...], pre_grad[...], (((0,), (0,)), ((), ())), preferred_element_type=F32)
-    up[...] = lax.dot_general(cot_in[...], act[...], (((0,), (0,)), ((), ())), preferred_element_type=F32)
+    rows_in, cot_in = received(got)
+    down[...] = lax.dot_general(rows_in, pre_grad[...], (((0,), (0,)), ((), ())), preferred_element_type=F32)
+    up[...] = lax.dot_general(cot_in, act[...], (((0,), (0,)), ((), ())), preferred_element_type=F32)
     for at in range(parts):
         near = pl.ds(pl.multiple_of((2 * at + core) * part, part), part)
         far = pl.ds(pl.multiple_of((2 * at + 1 - core) * part, part), part)
@@ -165,9 +168,8 @@
 
 
 def sum_gradients(
-    numbers, place, back, cot, summed, inv, gain, left, own, right, total, edges, *rest
+    numbers, back, cot, summed, inv, gain, left, own, right, act, up, total, edges, branch, sums, cells, frames_grad
 ):
-    *quarters, sums, cells, frames_grad = rest
     frames, width = cot.shape
     gather = gather_matrix(segments(numbers), back.shape[0], frames)
     cells[:EDGE] = left[...].astype(F32)
@@ -207,9 +209,13 @@
     lax.fori_loop(0, width // LANES, column, 0)
     edges[0] = total[:EDGE]
     edges[1] = total[frames - EDGE :]
-    for turn, out in enumerate(quarters):
-        at = (place[0] // 4) ^ turn
-        out[...] = sums[pl.ds(pl.multiple_of(at * 8, 8), 8)]
+    both_up = up[...].reshape(act.shape[1], width)
+    row = lax.broadcasted_iota(jnp.int32, (branch.shape[0], sums.shape[0]), 0)
+    block = lax.broadcasted_iota(jnp.int32, (branch.shape[0], sums.shape[0]), 1)
+    last = jnp.where(row == block * BLOCK + BLOCK - 1, 1.0, 0.0).astype(BF16)
+    outputs = jnp.dot(act[...], both_up, preferred_element_type=F32)
+    outputs = outputs + jnp.dot(last, sums[...].astype(BF16), preferred_element_type=F32)
+    branch[...] = outputs.astype(BF16)
 
 
 def input_gradient(left, own, right, taps, out, cells):
@@ -265,16 +271,6 @@
     ]
 
 
-def quarter(cells, mine):
-    part = cells.shape[0] // 4
-    blocks = [cells[at * part : at * part + part] for at in range(4)]
-    places = [mine ^ turn for turn in range(4)]
-    return [
-        jnp.where(at < 2, jnp.where(at == 0, blocks[0], blocks[1]), jnp.where(at == 2, blocks[2], blocks[3]))
-        for at in places
-    ]
-
-
 def swap(cells, axis):
     return lax.all_to_all(cells, axis, split_axis=0, concat_axis=0, tiled=True)
 
@@ -297,30 +293,25 @@
     where = [("s", numbers)]
 
     left, right = from_sides(own[:EDGE], own[frames - EDGE :], "ctx")
-    (send_cot,) = call(send_cotangent, [((rows, width), BF16)], where + [("v", cot)])
-    left, right, send_cot = lax.optimization_barrier((left, right, send_cot))
-    got_cot = swap(send_cot, "ctx")
-    send_rows, summed, inv = call(
+    send, summed, inv = call(
         conv_and_norm,
-        [((rows, width), BF16), ((frames, width), F32), ((frames, LANES), F32)],
-        where + [("v", left), ("v", own), ("v", right), ("v", conv_kernel), ("v", gain)],
+        [((ctx, 2 * BLOCK, width), BF16), ((frames, width), F32), ((frames, LANES), F32)],
+        where + [("v", left), ("v", own), ("v", right), ("v", cot), ("v", conv_kernel), ("v", gain)],
         [((frames + 2 * EDGE, width), F32), ((frames, width), BF16)],
-        moves=24_000_000,
-    )
-    got_rows = swap(send_rows, "ctx")
+    )
+    got = swap(send, "ctx")
     back, pre_grad, act = call(
         keeper_back,
         [((rows, width), BF16), ((rows, 2 * units), BF16), ((rows, 2 * units), BF16)],
-        [("v", got_rows), ("v", got_cot), ("v", adapt_down), ("v", adapt_up)],
+        [("v", got), ("v", adapt_down), ("v", adapt_up)],
     )
     grad_back = swap(back, "ctx")
-    (branch,) = call(keeper_branch, [((rows, width), BF16)], [("v", act), ("v", adapt_up)])
     share = width // dp
     place = ("s", lax.axis_index("dp").astype(jnp.int32).reshape(1))
     kept, given = call(
         keeper_grads,
         [((dp // 2, 2 * share, 2 * units), F32), ((dp // 2, 2 * share, 2 * units), BF16)],
-        [place, ("v", got_rows), ("v", got_cot), ("v", pre_grad), ("v", act)],
+        [place, ("v", got), ("v", pre_grad), ("v", act)],
         [((width, 2 * units), F32), ((width, 2 * units), F32)],
     )
     (got,) = exchanged([kept, given], "dp", 1)
@@ -335,37 +326,36 @@
     kept, given = call(
         pair_grads, [(piece, F32), (piece, BF16)], [place, ("v", chips[0])] + [("v", part) for part in got]
     )
+    grad_back, kept, given = lax.optimization_barrier((grad_back, kept, given))
+    total, edges, branch = call(
+        sum_gradients,
+        [((frames, width), F32), ((2, EDGE, width), F32), ((rows, width), BF16)],
+        where
+        + [("v", grad_back), ("v", cot), ("v", summed), ("v", inv), ("v", gain)]
+        + [("v", left), ("v", own), ("v", right), ("v", act), ("v", adapt_up)],
+        [((ctx, width), F32), ((frames + 2 * EDGE, width), F32), ((frames, width), F32)],
+    )
+    branch_back = swap(branch, "ctx")
     (got,) = exchanged([kept, given], "dp", 8)
     grad_down, grad_up = call(
         functools.partial(place_grads, grad_scale), [((2, share, units), F32)] * 2, [("v", kept), ("v", got)]
     )
-    grad_back, branch, grad_down, grad_up = lax.optimization_barrier((grad_back, branch, grad_down, grad_up))
-    branch_back = swap(branch, "ctx")
-    total, edges, *sums = call(
-        sum_gradients,
-        [((frames, width), F32), ((2, EDGE, width), F32)] + [((8, width), F32)] * 4,
-        where
-        + [place]
-        + [("v", grad_back), ("v", cot), ("v", summed), ("v", inv), ("v", gain)]
-        + [("v", left), ("v", own), ("v", right)],
-        [((32, width), F32), ((frames + 2 * EDGE, width), F32), ((frames, width), F32)],
-    )
     grad_left, grad_right = from_sides(edges[0], edges[1], "ctx")
-    me = lax.axis_index("dp")
-    mine = sums[0] + sum(exchanged(sums, "dp", 4))
-    sums = quarter(mine, me % 4)
-    mine = sums[0] + sum(exchanged(sums, "dp", 1))
-    mine, branch_back = lax.optimization_barrier((mine, branch_back))
-    mine = jnp.sum(spread_rows(mine, "ctx"), axis=0)
+    branch_back, grad_down, grad_up, grad_left, grad_right = lax.optimization_barrier(
+        (branch_back, grad_down, grad_up, grad_left, grad_right)
+    )
+    (mine,) = call(sum_last_rows, [((8, width), F32)], [("v", branch_back)])
     (grad_input,) = call(
         input_gradient,
         [((frames, width), BF16)],
         [("v", grad_left), ("v", total), ("v", grad_right), ("v", conv_kernel)],
         [((frames + 2 * EDGE, width), F32)],
     )
+    mine = spread_rows(mine[:1], "dp")
+    mine, grad_input = lax.optimization_barrier((mine, grad_input))
+    mine = jnp.sum(mine, axis=0) * grad_scale
+    reduced = spread_rows(mine, "ctx").reshape(ctx, width)
     (output,) = call(add_branch, [((frames, width), BF16)], where + [("v", branch_back), ("v", summed)])
-    mine, grad_input = lax.optimization_barrier((mine, grad_input))
-    reduced = spread_rows(mine * grad_scale, "dp").reshape(32, width)
     return output[None], grad_input[None], reduced[:31], reduced[31], grad_down, jnp.transpose(grad_up, (0, 2, 1))
 
 

time: 265 us -> 247 us (0.932)
  starting transfers between devices: 89.1 us -> 70.6 us
  blocking collectives: 94.6 us -> 83.7 us
  waiting for transfers between devices: 36.8 us -> 47 us
  local copies, waits for them, and re-layouts: 12.8 us -> 18.6 us
    ppermute x11 -> x5, starting transfers between devices: 46.3 us -> 22.3 us  [exchanged(): lax.ppermute(block, axis, [(i, i ^ turn * unit) for i in range(count)])]
    ppermute x2, waiting for transfers between devices: 3.35 us -> 20.9 us  [from_sides(): right = lax.ppermute(head, axis, [(i + 1, i) for i in range(count - 1)])]
    all_to_all x2 -> x1, blocking collectives: 94.6 us -> 83.7 us  [swap(): return lax.all_to_all(cells, axis, split_axis=0, concat_axis=0, tiled=True)]
    ppermute x11 -> x5, waiting for transfers between devices: 20.7 us -> 12.9 us  [exchanged(): lax.ppermute(block, axis, [(i, i ^ turn * unit) for i in range(count)])]
    unnamed x42 -> x55, local copies, waits for them, and re-layouts: 8.86 us -> 14.9 us
    all_to_all x4, waiting for transfers between devices: 8.07 us -> 13.2 us  [swap(): return lax.all_to_all(cells, axis, split_axis=0, concat_axis=0, tiled=True)]
    ppermute x2, waiting for transfers between devices: 4.67 us -> 0.01 us  [from_sides(): left = lax.ppermute(tail, axis, [(i, i + 1) for i in range(count - 1)])]
    all_to_all x4, starting transfers between devices: 32.3 us -> 36.3 us  [swap(): return lax.all_to_all(cells, axis, split_axis=0, concat_axis=0, tiled=True)]
  transfers between devices with their start and end apart: 19 -> 13, of which waited for: 10 -> 6; matrix products, arithmetic and copies ran while one was open for 1% -> 1% of each run, Pallas kernels for 8% -> 4%
where the time goes in v3:
time: 247 us; the launch traced here: 246 us
  blocking collectives  83.7 us (34%)
  starting transfers between devices  70.6 us (29%)
  waiting for transfers between devices  47 us (19%)
  Pallas kernels  24.7 us (10%)
  local copies, waits for them, and re-layouts  18.6 us (8%)
    all_to_all x1, blocking collectives, swap(): return lax.all_to_all(cells, axis, split_axis=0, concat_axis=0, tiled=True)  83.7 us
    all_to_all x4, starting transfers between devices, swap(): return lax.all_to_all(cells, axis, split_axis=0, concat_axis=0, tiled=True)  36.3 us
    pallas_call x10, Pallas kernels, call(): pl.pallas_call(body, out_shape=tuple((jax.ShapeDtypeStruct(shape, kind) f...  24.7 us
    ppermute x5, starting transfers between devices, exchanged(): lax.ppermute(block, axis, [(i, i ^ turn * unit) for i in range(count)])  22.3 us
    ppermute x2, waiting for transfers between devices, from_sides(): right = lax.ppermute(head, axis, [(i + 1, i) for i in range(count - 1)])  20.9 us
    unnamed x55, local copies, waits for them, and re-layouts  14.9 us
    all_to_all x4, waiting for transfers between devices, swap(): return lax.all_to_all(cells, axis, split_axis=0, concat_axis=0, tiled=True)  13.2 us
    ppermute x5, waiting for transfers between devices, exchanged(): lax.ppermute(block, axis, [(i, i ^ turn * unit) for i in range(count)])  12.9 us
  transfers between devices with their start and end apart: 13, of which 6 were waited for; matrix products, arithmetic and copies ran while one was open for 1% of the time, Pallas kernels for 4%

profile of v3, /device:TPU:1, one launch (start us, length us, event | category | flops | bytes accessed | tf_op | source)
XLA Modules:
  0.0 246.3 jit_solution(8181960645781578078)
XLA Ops:
  0.6 0.8 slice_bitcast_fusion.2
  1.5 1.3 collective-permute-start.1
  2.8 5.5 %collective-permute-start = (bf16[16,1536]{1,0:T(8,128)(2,1)S(1)}, bf16[16,1536]{1,0:T(8,128)(2,1)S(1)}, u32[]{:S(2)}, u32[]{:S(2)}) collective-permute-start(bf16[16,1536]{1,0:T(8,128)(2,1)S(1)} %get-tuple-element.65), channel_id=1, source_target_pairs={{0,1},{1,2},{2,3},{3,4},{4,5},{5,6},{6,7},{7,8},{8,9},{9,10},{10,1... | collective-permute-start | bytes 147464 | tf_op jit(solution)/shard_map/ppermute | solution.py:261
  8.2 0.8 pad_add_fusion.numbers
  9.0 0.7 reshape.48.gain
  9.7 1.1 copy-done.4
  10.8 1.1 copy-done.6
  11.8 0.9 copy-done.15
  12.8 5.7 %shard_map.136 = (bf16[32,32,1536]{2,1,0:T(8,128)(2,1)S(1)}, f32[192,1536]{1,0:T(8,128)S(1)}, f32[192,128]{1,0:T(8,128)S(1)}) custom-call(s32[96]{0:T(128)S(1)} %pad_add_fusion.numbers, bf16[16,1536]{1,0:T(8,128)(2,1)S(1)} %collective-permute-done.left, bf16[192,1536]{1,0:T(8,128)(2,1)S(1)} %bitcast.25, bf16[16,1536]{1,0:T(8,128)(2,1)S(1)} %collective-permute-done.1.right, ...), custom_call_target="tpu_custom_call" | custom-call | tf_op jit(solution)/shard_map/pallas_call | solution.py:23
  18.5 1.0 copy-done
  19.5 83.7 %all_to_all.39.got = bf16[32,32,1536]{2,1,0:T(8,128)(2,1)S(1)} all-to-all(bf16[32,32,1536]{2,1,0:T(8,128)(2,1)S(1)} %get-tuple-element.35), channel_id=1, replica_groups=mesh['dp'=16,'ctx'=32] {'ctx'}, dimensions={0} | all-to-all | bytes 6291456 | tf_op jit(solution)/shard_map/all_to_all | solution.py:275
  103.2 1.5 shard_map.137
  104.7 0.7 copy-done.17
  105.4 1.2 copy-done.8
  106.6 7.4 %all-to-all-start.1 = ((bf16[32,16,1536]{2,1,0:T(8,128)(2,1)}), bf16[32,16,1536]{2,1,0:T(8,128)(2,1)}, u32[]{:S(2)}, u32[]{:S(2)}) async-start(bf16[32,16,1536]{2,1,0:T(8,128)(2,1)} %bitcast.29), calls=%async_computation.1 | async-start | bytes 3145728 | tf_op jit(solution)/shard_map/all_to_all | solution.py:275
  114.0 0.9 copy-done.18
  114.9 1.6 shard_map.138
  116.5 5.1 %collective-permute-start.2 = (bf16[8,192,256]{2,1,0:T(8,128)(2,1)S(1)}, bf16[8,192,256]{2,1,0:T(8,128)(2,1)S(1)}, u32[]{:S(2)}, u32[]{:S(2)}) collective-permute-start(bf16[8,192,256]{2,1,0:T(8,128)(2,1)S(1)} %get-tuple-element.40), channel_id=1, source_target_pairs={{0,32},{32,0},{64,96},{96,64},{128,160},{160,128},{192,224},{224,1... | collective-permute-start | bytes 2359304 | tf_op jit(solution)/shard_map/ppermute | solution.py:269
  121.7 1.9 collective-permute-done.2.got
  123.7 3.5 %collective-permute-start.3 = (bf16[2,192,256]{2,1,0:T(8,128)(2,1)S(1)}, bf16[2,192,256]{2,1,0:T(8,128)(2,1)S(1)}, u32[]{:S(2)}, u32[]{:S(2)}) collective-permute-start(bf16[2,192,256]{2,1,0:T(8,128)(2,1)S(1)} %get-tuple-element.42), channel_id=1, source_target_pairs={{0,64},{32,96},{64,0},{96,32},{128,192},{160,224},{192,128},{224,1... | collective-permute-start | bytes 589832 | tf_op jit(solution)/shard_map/ppermute | solution.py:269
  127.2 4.2 %collective-permute-start.4 = (bf16[2,192,256]{2,1,0:T(8,128)(2,1)S(1)}, bf16[2,192,256]{2,1,0:T(8,128)(2,1)S(1)}, u32[]{:S(2)}, u32[]{:S(2)}) collective-permute-start(bf16[2,192,256]{2,1,0:T(8,128)(2,1)S(1)} %get-tuple-element.43), channel_id=1, source_target_pairs={{0,128},{32,160},{64,192},{96,224},{128,0},{160,32},{192,64},{224,... | collective-permute-start | bytes 589832 | tf_op jit(solution)/shard_map/ppermute | solution.py:269
  131.4 1.9 collective-permute-start.5
  133.4 11.0 %collective-permute-done.4.second = bf16[2,192,256]{2,1,0:T(8,128)(2,1)S(1)} collective-permute-done((bf16[2,192,256]{2,1,0:T(8,128)(2,1)S(1)}, bf16[2,192,256]{2,1,0:T(8,128)(2,1)S(1)}, u32[]{:S(2)}, u32[]{:S(2)}) %collective-permute-start.4) | collective-permute-done | bytes 196640 | tf_op jit(solution)/shard_map/ppermute | solution.py:269
  144.5 0.7 copy-done.19
  145.2 0.6 copy-done.25
  145.8 2.8 %all-to-all-done.1 = bf16[32,16,1536]{2,1,0:T(8,128)(2,1)} async-done(((bf16[32,16,1536]{2,1,0:T(8,128)(2,1)}), bf16[32,16,1536]{2,1,0:T(8,128)(2,1)}, u32[]{:S(2)}, u32[]{:S(2)}) %all-to-all-start.1) | async-done | bytes 1572896 | tf_op jit(solution)/shard_map/all_to_all | solution.py:275
  148.6 0.9 copy-done.13
  149.6 0.9 copy-done.24
  150.5 7.9 %shard_map.141 = (f32[192,1536]{1,0:T(8,128)S(1)}, f32[2,16,1536]{2,1,0:T(8,128)S(1)}, bf16[512,1536]{1,0:T(8,128)(2,1)S(1)}) custom-call(s32[96]{0:T(128)S(1)} %pad_add_fusion.numbers, bf16[512,1536]{1,0:T(8,128)(2,1)} %bitcast.7.back, bf16[192,1536]{1,0:T(8,128)(2,1)S(1)} %bitcast.28, f32[192,1536]{1,0:T(8,128)S(1)} %copy-done.1, ...), custom_call_target="tpu_custom_call" | custom-call | tf_op jit(solution)/shard_map/pallas_call | solution.py:23
  158.4 1.0 copy-done.10
  159.4 0.7 copy-done.21
  160.1 1.2 copy-done.9
  161.2 8.1 %all-to-all-start.2 = ((bf16[32,16,1536]{2,1,0:T(8,128)(2,1)}), bf16[32,16,1536]{2,1,0:T(8,128)(2,1)S(1)}, u32[]{:S(2)}, u32[]{:S(2)}) async-start(bf16[32,16,1536]{2,1,0:T(8,128)(2,1)} %bitcast.30), calls=%async_computation.2 | async-start | bytes 3145728 | tf_op jit(solution)/shard_map/all_to_all | solution.py:275
  169.4 7.6 %collective-permute-start.6 = (bf16[192,256]{1,0:T(8,128)(2,1)S(1)}, bf16[192,256]{1,0:T(8,128)(2,1)S(1)}, u32[]{:S(2)}, u32[]{:S(2)}) collective-permute-start(bf16[192,256]{1,0:T(8,128)(2,1)S(1)} %copy-done.26), channel_id=1, source_target_pairs={{0,256},{32,288},{64,320},{96,352},{128,384},{160,416},{192,448},{... | collective-permute-start | bytes 294920 | tf_op jit(solution)/shard_map/ppermute | solution.py:269
  177.0 1.3 collective-permute-start.8
  178.3 4.0 %collective-permute-start.7 = (f32[16,1536]{1,0:T(8,128)S(1)}, f32[16,1536]{1,0:T(8,128)S(1)}, u32[]{:S(2)}, u32[]{:S(2)}) collective-permute-start(f32[16,1536]{1,0:T(8,128)S(1)} %get-tuple-element.67), channel_id=1, source_target_pairs={{0,1},{1,2},{2,3},{3,4},{4,5},{5,6},{6,7},{7,8},{8,9},{9,10},{10,1... | collective-permute-start | bytes 294920 | tf_op jit(solution)/shard_map/ppermute | solution.py:261
  182.3 0.7 shard_map.142
  183.0 20.9 %collective-permute-done.8.right = f32[16,1536]{1,0:T(8,128)S(1)} collective-permute-done((f32[16,1536]{1,0:T(8,128)S(1)}, f32[16,1536]{1,0:T(8,128)S(1)}, u32[]{:S(2)}, u32[]{:S(2)}) %collective-permute-start.8) | collective-permute-done | bytes 98336 | tf_op jit(solution)/shard_map/ppermute | solution.py:262
  204.3 0.7 broadcast_in_dim.22
  205.0 15.8 %all-to-all-start.3 = ((f32[16,1,1536]{2,1,0:T(1,128)}), f32[16,1,1536]{2,1,0:T(1,128)S(1)}, u32[]{:S(2)}, u32[]{:S(2)}) async-start(f32[16,1,1536]{2,1,0:T(1,128)} %broadcast_in_dim.22), calls=%async_computation.3 | async-start | bytes 196608 | tf_op jit(solution)/shard_map/all_to_all | solution.py:275
  220.8 1.3 copy-done.11
  222.1 4.4 %shard_map.145 = bf16[192,1536]{1,0:T(8,128)(2,1)} custom-call(f32[16,1536]{1,0:T(8,128)S(1)} %collective-permute-done.7.left, f32[192,1536]{1,0:T(8,128)S(1)} %copy-done.11, f32[16,1536]{1,0:T(8,128)S(1)} %collective-permute-done.8.right, f32[31,1536]{1,0:T(8,128)S(1)} %copy-done.16), custom_call_target="tpu_custom_call" | custom-call | tf_op jit(solution)/shard_map/pallas_call | solution.py:23
  226.4 2.8 %all-to-all-done.3 = f32[16,1,1536]{2,1,0:T(1,128)S(1)} async-done(((f32[16,1,1536]{2,1,0:T(1,128)}), f32[16,1,1536]{2,1,0:T(1,128)S(1)}, u32[]{:S(2)}, u32[]{:S(2)}) %all-to-all-start.3) | async-done | bytes 98336 | tf_op jit(solution)/shard_map/all_to_all | solution.py:275
  229.3 0.8 broadcast_in_dim.24
  230.1 5.0 %all-to-all-start.4 = ((f32[32,1,1536]{2,1,0:T(1,128)}), f32[32,1,1536]{2,1,0:T(1,128)S(1)}, u32[]{:S(2)}, u32[]{:S(2)}) async-start(f32[32,1,1536]{2,1,0:T(1,128)} %broadcast_in_dim.24), calls=%async_computation.4 | async-start | bytes 393216 | tf_op jit(solution)/shard_map/all_to_all | solution.py:275
  235.1 2.3 shard_map.143
  237.4 7.6 %all-to-all-done.4 = f32[32,1,1536]{2,1,0:T(1,128)S(1)} async-done(((f32[32,1,1536]{2,1,0:T(1,128)}), f32[32,1,1536]{2,1,0:T(1,128)S(1)}, u32[]{:S(2)}, u32[]{:S(2)}) %all-to-all-start.4) | async-done | bytes 196640 | tf_op jit(solution)/shard_map/all_to_all | solution.py:275
  244.9 0.7 copy.17
  (55 shorter events, 1.4 us)
Async XLA Ops:
  1.5 8.2 %collective-permute-start.1 = (bf16[16,1536]{1,0:T(8,128)(2,1)S(1)}, bf16[16,1536]{1,0:T(8,128)(2,1)S(1)}, u32[]{:S(2)}, u32[]{:S(2)}) collective-permute-start(bf16[16,1536]{1,0:T(8,128)(2,1)S(1)} %get-tuple-element.64), channel_id=1, source_target_pairs={{1,0},{2,1},{3,2},{4,3},{5,4},{6,5},{7,6},{8,7},{9,8},{10,9},{11,1... | collective-permute-start | bytes 147464 | tf_op jit(solution)/shard_map/ppermute | solution.py:262
  2.8 6.9 %collective-permute-start = (bf16[16,1536]{1,0:T(8,128)(2,1)S(1)}, bf16[16,1536]{1,0:T(8,128)(2,1)S(1)}, u32[]{:S(2)}, u32[]{:S(2)}) collective-permute-start(bf16[16,1536]{1,0:T(8,128)(2,1)S(1)} %get-tuple-element.65), channel_id=1, source_target_pairs={{0,1},{1,2},{2,3},{3,4},{4,5},{5,6},{6,7},{7,8},{8,9},{9,10},{10,1... | collective-permute-start | bytes 147464 | tf_op jit(solution)/shard_map/ppermute | solution.py:261
  9.7 1.1 copy-start.4
  10.8 1.1 copy-start.6
  11.8 0.9 copy-start.15
  18.5 1.0 copy-start
  19.5 83.7 %copy-start.23 = (f32[192,128]{1,0:T(8,128)}, f32[192,128]{1,0:T(8,128)S(1)}, u32[]{:S(2)}) copy-start(f32[192,128]{1,0:T(8,128)S(1)} %get-tuple-element.49.inv) | copy-start | bytes 294916
  19.5 83.7 %copy-start.2 = (bf16[2,128,1536]{2,1,0:T(8,128)(2,1)S(1)}, bf16[2,128,1536]{2,1,0:T(8,128)(2,1)}, u32[]{:S(2)}) copy-start(bf16[2,128,1536]{2,1,0:T(8,128)(2,1)} %up.3) | copy-start | bytes 2359300
  19.5 83.7 %copy-start.14 = (bf16[2,1536,128]{2,1,0:T(8,128)(2,1)S(1)}, bf16[2,1536,128]{2,1,0:T(8,128)(2,1)}, u32[]{:S(2)}) copy-start(bf16[2,1536,128]{2,1,0:T(8,128)(2,1)} %down.1) | copy-start | bytes 2359300
  104.7 0.7 copy-start.17
  105.4 1.2 copy-start.8
  105.4 8.5 %copy-start.12 = (bf16[512,256]{1,0:T(8,128)(2,1)}, bf16[512,256]{1,0:T(8,128)(2,1)S(1)}, u32[]{:S(2)}) copy-start(bf16[512,256]{1,0:T(8,128)(2,1)S(1)} %get-tuple-element.38.act) | copy-start | bytes 786436
  106.6 42.0 %all-to-all-start.1 = ((bf16[32,16,1536]{2,1,0:T(8,128)(2,1)}), bf16[32,16,1536]{2,1,0:T(8,128)(2,1)}, u32[]{:S(2)}, u32[]{:S(2)}) async-start(bf16[32,16,1536]{2,1,0:T(8,128)(2,1)} %bitcast.29), calls=%async_computation.1 | async-start | bytes 3145728 | tf_op jit(solution)/shard_map/all_to_all | solution.py:275
  114.0 1.0 copy-start.18
  116.5 7.0 %collective-permute-start.2 = (bf16[8,192,256]{2,1,0:T(8,128)(2,1)S(1)}, bf16[8,192,256]{2,1,0:T(8,128)(2,1)S(1)}, u32[]{:S(2)}, u32[]{:S(2)}) collective-permute-start(bf16[8,192,256]{2,1,0:T(8,128)(2,1)S(1)} %get-tuple-element.40), channel_id=1, source_target_pairs={{0,32},{32,0},{64,96},{96,64},{128,160},{160,128},{192,224},{224,1... | collective-permute-start | bytes 2359304 | tf_op jit(solution)/shard_map/ppermute | solution.py:269
  123.6 25.0 %copy-start.1 = (f32[192,1536]{1,0:T(8,128)S(1)}, f32[192,1536]{1,0:T(8,128)}, u32[]{:S(2)}) copy-start(f32[192,1536]{1,0:T(8,128)} %copy-done) | copy-start | bytes 3538948
  123.6 25.0 %copy-start.3 = (bf16[2,128,1536]{2,1,0:T(8,128)(2,1)S(1)}, bf16[2,128,1536]{2,1,0:T(8,128)(2,1)}, u32[]{:S(2)}) copy-start(bf16[2,128,1536]{2,1,0:T(8,128)(2,1)} %up.3) | copy-start | bytes 2359300
  123.6 25.0 %copy-start.5 = (bf16[1,192,1536]{2,1,0:T(8,128)(2,1)S(1)}, bf16[1,192,1536]{2,1,0:T(8,128)(2,1)}, u32[]{:S(2)}) copy-start(bf16[1,192,1536]{2,1,0:T(8,128)(2,1)} %param.9) | copy-start | bytes 1769476
  123.6 25.0 %copy-start.7 = (bf16[1,192,1536]{2,1,0:T(8,128)(2,1)S(1)}, bf16[1,192,1536]{2,1,0:T(8,128)(2,1)}, u32[]{:S(2)}) copy-start(bf16[1,192,1536]{2,1,0:T(8,128)(2,1)} %param.10) | copy-start | bytes 1769476
  123.7 9.6 %collective-permute-start.3 = (bf16[2,192,256]{2,1,0:T(8,128)(2,1)S(1)}, bf16[2,192,256]{2,1,0:T(8,128)(2,1)S(1)}, u32[]{:S(2)}, u32[]{:S(2)}) collective-permute-start(bf16[2,192,256]{2,1,0:T(8,128)(2,1)S(1)} %get-tuple-element.42), channel_id=1, source_target_pairs={{0,64},{32,96},{64,0},{96,32},{128,192},{160,224},{192,128},{224,1... | collective-permute-start | bytes 589832 | tf_op jit(solution)/shard_map/ppermute | solution.py:269
  127.2 17.2 %collective-permute-start.4 = (bf16[2,192,256]{2,1,0:T(8,128)(2,1)S(1)}, bf16[2,192,256]{2,1,0:T(8,128)(2,1)S(1)}, u32[]{:S(2)}, u32[]{:S(2)}) collective-permute-start(bf16[2,192,256]{2,1,0:T(8,128)(2,1)S(1)} %get-tuple-element.43), channel_id=1, source_target_pairs={{0,128},{32,160},{64,192},{96,224},{128,0},{160,32},{192,64},{224,... | collective-permute-start | bytes 589832 | tf_op jit(solution)/shard_map/ppermute | solution.py:269
  131.4 13.0 %collective-permute-start.5 = (bf16[2,192,256]{2,1,0:T(8,128)(2,1)S(1)}, bf16[2,192,256]{2,1,0:T(8,128)(2,1)S(1)}, u32[]{:S(2)}, u32[]{:S(2)}) collective-permute-start(bf16[2,192,256]{2,1,0:T(8,128)(2,1)S(1)} %get-tuple-element.44), channel_id=1, source_target_pairs={{0,192},{32,224},{64,128},{96,160},{128,64},{160,96},{192,0},{224,... | collective-permute-start | bytes 589832 | tf_op jit(solution)/shard_map/ppermute | solution.py:269
  144.5 0.7 copy-start.19
  145.2 0.6 copy-start.25
  148.6 1.0 copy-start.13
  149.6 0.9 copy-start.24
  158.4 1.0 copy-start.10
  159.4 0.7 copy-start.21
  160.1 1.2 copy-start.9
  161.2 8.1 %copy-start.26 = (bf16[192,256]{1,0:T(8,128)(2,1)S(1)}, bf16[192,256]{1,0:T(8,128)(2,1)}, u32[]{:S(2)}) copy-start(bf16[192,256]{1,0:T(8,128)(2,1)} %copy-done.25) | copy-start | bytes 294916
  161.2 15.8 %copy-start.22 = (f32[2,16,1536]{2,1,0:T(8,128)S(1)}, f32[2,16,1536]{2,1,0:T(8,128)}, u32[]{:S(2)}) copy-start(f32[2,16,1536]{2,1,0:T(8,128)} %copy-done.21) | copy-start | bytes 589828
  161.2 21.1 %copy-start.20 = (f32[192,256]{1,0:T(8,128)S(1)}, f32[192,256]{1,0:T(8,128)}, u32[]{:S(2)}) copy-start(f32[192,256]{1,0:T(8,128)} %copy-done.19) | copy-start | bytes 589828
  161.2 42.7 %all-to-all-start.2 = ((bf16[32,16,1536]{2,1,0:T(8,128)(2,1)}), bf16[32,16,1536]{2,1,0:T(8,128)(2,1)S(1)}, u32[]{:S(2)}, u32[]{:S(2)}) async-start(bf16[32,16,1536]{2,1,0:T(8,128)(2,1)} %bitcast.30), calls=%async_computation.2 | async-start | bytes 3145728 | tf_op jit(solution)/shard_map/all_to_all | solution.py:275
  169.4 51.4 %copy-start.16 = (f32[31,1536]{1,0:T(8,128)S(1)}, f32[31,1536]{1,0:T(8,128)}, u32[]{:S(2)}) copy-start(f32[31,1536]{1,0:T(8,128)} %taps.3) | copy-start | bytes 571396
  169.4 12.9 %collective-permute-start.6 = (bf16[192,256]{1,0:T(8,128)(2,1)S(1)}, bf16[192,256]{1,0:T(8,128)(2,1)S(1)}, u32[]{:S(2)}, u32[]{:S(2)}) collective-permute-start(bf16[192,256]{1,0:T(8,128)(2,1)S(1)} %copy-done.26), channel_id=1, source_target_pairs={{0,256},{32,288},{64,320},{96,352},{128,384},{160,416},{192,448},{... | collective-permute-start | bytes 294920 | tf_op jit(solution)/shard_map/ppermute | solution.py:269
  177.0 26.9 %collective-permute-start.8 = (f32[16,1536]{1,0:T(8,128)S(1)}, f32[16,1536]{1,0:T(8,128)S(1)}, u32[]{:S(2)}, u32[]{:S(2)}) collective-permute-start(f32[16,1536]{1,0:T(8,128)S(1)} %get-tuple-element.66), channel_id=1, source_target_pairs={{1,0},{2,1},{3,2},{4,3},{5,4},{6,5},{7,6},{8,7},{9,8},{10,9},{11,1... | collective-permute-start | bytes 294920 | tf_op jit(solution)/shard_map/ppermute | solution.py:262
  178.3 25.6 %collective-permute-start.7 = (f32[16,1536]{1,0:T(8,128)S(1)}, f32[16,1536]{1,0:T(8,128)S(1)}, u32[]{:S(2)}, u32[]{:S(2)}) collective-permute-start(f32[16,1536]{1,0:T(8,128)S(1)} %get-tuple-element.67), channel_id=1, source_target_pairs={{0,1},{1,2},{2,3},{3,4},{4,5},{5,6},{6,7},{7,8},{8,9},{9,10},{10,1... | collective-permute-start | bytes 294920 | tf_op jit(solution)/shard_map/ppermute | solution.py:261
  205.0 24.3 %all-to-all-start.3 = ((f32[16,1,1536]{2,1,0:T(1,128)}), f32[16,1,1536]{2,1,0:T(1,128)S(1)}, u32[]{:S(2)}, u32[]{:S(2)}) async-start(f32[16,1,1536]{2,1,0:T(1,128)} %broadcast_in_dim.22), calls=%async_computation.3 | async-start | bytes 196608 | tf_op jit(solution)/shard_map/all_to_all | solution.py:275
  220.8 1.3 copy-start.11
  230.1 14.8 %all-to-all-start.4 = ((f32[32,1,1536]{2,1,0:T(1,128)}), f32[32,1,1536]{2,1,0:T(1,128)S(1)}, u32[]{:S(2)}, u32[]{:S(2)}) async-start(f32[32,1,1536]{2,1,0:T(1,128)} %broadcast_in_dim.24), calls=%async_computation.4 | async-start | bytes 393216 | tf_op jit(solution)/shard_map/all_to_all | solution.py:275

commit v4 on v3

--- a/solution.py
+++ b/solution.py
@@ -19,15 +19,32 @@
 BF16 = jnp.bfloat16
 
 
-def call(body, outs, ins, scratch=()):
+HBM = pl.BlockSpec(memory_space=pltpu.HBM)
+SPACES = {"s": SMEM, "v": VMEM, "h": HBM}
+
+
+def call(body, outs, ins, scratch=(), copies=0):
     return pl.pallas_call(
         body,
-        out_shape=tuple(jax.ShapeDtypeStruct(shape, kind) for shape, kind in outs),
-        in_specs=[SMEM if space == "s" else VMEM for space, _ in ins],
-        out_specs=tuple(VMEM for _ in outs),
-        scratch_shapes=[pltpu.VMEM(shape, kind) for shape, kind in scratch],
+        out_shape=tuple(jax.ShapeDtypeStruct(out[0], out[1]) for out in outs),
+        in_specs=[SPACES[space] for space, _ in ins],
+        out_specs=tuple(SPACES[(out + ("v",))[2]] for out in outs),
+        scratch_shapes=[pltpu.VMEM(shape, kind) for shape, kind in scratch]
+        + ([pltpu.SemaphoreType.DMA((copies,))] if copies else []),
         compiler_params=PARAMS,
     )(*[array for _, array in ins])
+
+
+def started(pairs, sems, first=0):
+    copies = [pltpu.make_async_copy(source, target, sems.at[first + at]) for at, (source, target) in enumerate(pairs)]
+    for copy in copies:
+        copy.start()
+    return copies
+
+
+def finish(copies):
+    for copy in copies:
+        copy.wait()
 
 
 def segments(numbers):
@@ -66,8 +83,12 @@
     return cells if by == 0 else pltpu.roll(cells, cells.shape[0] - by, 0)
 
 
-def conv_and_norm(numbers, left, own, right, cot, taps, gain, send, summed, inv, cells, normed):
+def conv_and_norm(
+    numbers, left_h, own_h, right_h, cot_h, taps_h, gain, send, summed_h, inv_h,
+    cells, normed, left, own, right, cot, taps, summed, inv, sems,
+):
     frames, width = own.shape
+    loads = started([(cot_h, cot), (own_h, own), (left_h, left), (right_h, right), (taps_h, taps)], sems)
     rows = send.shape[0] * BLOCK
     blocks = (send.shape[0], BLOCK, width)
     found = segments(numbers)
@@ -76,9 +97,11 @@
     mark = jnp.zeros((rows, LANES), F32)
     for _, _, keeper, which in found:
         mark = jnp.where(row == keeper * BLOCK + BLOCK - 1, which.astype(F32), mark)
+    finish(loads[:1])
     moved = jnp.dot(spread, cot[...], preferred_element_type=F32)
     moved = jnp.concatenate([moved[:, :LANES] + mark, moved[:, LANES:]], axis=1)
     send[:, BLOCK:] = moved.astype(BF16).reshape(blocks)
+    finish(loads[1:])
     cells[:EDGE] = left[...].astype(F32)
     cells[EDGE : EDGE + frames] = own[...].astype(F32)
     cells[EDGE + frames :] = right[...].astype(F32)
@@ -103,8 +126,10 @@
     squares = lax.fori_loop(0, width // LANES, column, jnp.zeros((frames, LANES), F32))
     scale = lax.rsqrt(jnp.sum(squares, axis=1, keepdims=True) * (1.0 / width) + 1e-06)
     inv[...] = jnp.broadcast_to(scale, inv.shape)
+    stores = started([(summed, summed_h), (inv, inv_h)], sems, len(loads))
     normed[...] = (summed[...] * scale * gain[...]).astype(BF16)
     send[:, :BLOCK] = jnp.dot(spread, normed[...], preferred_element_type=F32).astype(BF16).reshape(blocks)
+    finish(stores)
 
 
 def received(got):
@@ -112,7 +137,7 @@
     return got[:, :BLOCK].reshape(shape), got[:, BLOCK:].reshape(shape)
 
 
-def keeper_back(got, down, up, back, pre_grad, act):
+def keeper_back(got, down, up, back_h, pre_grad_h, act_h, back, pre_grad, act, sems):
     rows_in, cot_in = received(got)
     rows, width = rows_in.shape
     units = down.shape[2]
@@ -127,7 +152,9 @@
     act[...] = (keep * (pre * sig)).astype(BF16)
     grads = (keep * (slope_of * (sig * (1.0 + pre * (1.0 - sig))))).astype(BF16)
     pre_grad[...] = grads
+    stores = started([(pre_grad, pre_grad_h), (act, act_h)], sems)
     back[...] = lax.dot_general(grads, both_down, (((1,), (1,)), ((), ())), preferred_element_type=F32).astype(BF16)
+    finish(started([(back, back_h)], sems, len(stores)) + stores)
 
 
 def sum_last_rows(back, out):
@@ -168,14 +195,22 @@
 
 
 def sum_gradients(
-    numbers, back, cot, summed, inv, gain, left, own, right, act, up, total, edges, branch, sums, cells, frames_grad
+    numbers, gain, back_h, summed_h, inv_h, cot_h, own_h, left_h, right_h, act_h, up_h, total_h, edges_h, branch_h,
+    sums, cells, frames_grad, back, summed, inv, cot, own, left, right, act, up, total, branch, sems,
 ):
     frames, width = cot.shape
+    loads = started(
+        [(back_h, back), (summed_h, summed), (inv_h, inv), (cot_h, cot), (own_h, own)]
+        + [(left_h, left), (right_h, right), (act_h, act), (up_h, up)],
+        sems,
+    )
     gather = gather_matrix(segments(numbers), back.shape[0], frames)
+    finish(loads[:1])
+    frames_grad[...] = jnp.dot(gather, back[...], preferred_element_type=F32)
+    finish(loads[1:7])
     cells[:EDGE] = left[...].astype(F32)
     cells[EDGE : EDGE + frames] = own[...].astype(F32)
     cells[EDGE + frames :] = right[...].astype(F32)
-    frames_grad[...] = jnp.dot(gather, back[...], preferred_element_type=F32)
     scale = inv[:, :1]
     inner = jnp.sum(gain[...] * frames_grad[...] * summed[...], axis=1, keepdims=True) * (1.0 / width)
     pull = scale * scale * scale * inner
@@ -207,8 +242,9 @@
         return carry
 
     lax.fori_loop(0, width // LANES, column, 0)
-    edges[0] = total[:EDGE]
-    edges[1] = total[frames - EDGE :]
+    ends = [(total.at[pl.ds(0, EDGE)], edges_h.at[0]), (total.at[pl.ds(frames - EDGE, EDGE)], edges_h.at[1])]
+    stores = started(ends + [(total, total_h)], sems, len(loads))
+    finish(loads[7:])
     both_up = up[...].reshape(act.shape[1], width)
     row = lax.broadcasted_iota(jnp.int32, (branch.shape[0], sums.shape[0]), 0)
     block = lax.broadcasted_iota(jnp.int32, (branch.shape[0], sums.shape[0]), 1)
@@ -216,6 +252,7 @@
     outputs = jnp.dot(act[...], both_up, preferred_element_type=F32)
     outputs = outputs + jnp.dot(last, sums[...].astype(BF16), preferred_element_type=F32)
     branch[...] = outputs.astype(BF16)
+    finish(started([(branch, branch_h)], sems, len(loads) + len(stores)) + stores)
 
 
 def input_gradient(left, own, right, taps, out, cells):
@@ -295,15 +332,20 @@
     left, right = from_sides(own[:EDGE], own[frames - EDGE :], "ctx")
     send, summed, inv = call(
         conv_and_norm,
-        [((ctx, 2 * BLOCK, width), BF16), ((frames, width), F32), ((frames, LANES), F32)],
-        where + [("v", left), ("v", own), ("v", right), ("v", cot), ("v", conv_kernel), ("v", gain)],
-        [((frames + 2 * EDGE, width), F32), ((frames, width), BF16)],
+        [((ctx, 2 * BLOCK, width), BF16), ((frames, width), F32, "h"), ((frames, LANES), F32, "h")],
+        where + [("h", left), ("h", own), ("h", right), ("h", cot), ("h", conv_kernel), ("v", gain)],
+        [((frames + 2 * EDGE, width), F32), ((frames, width), BF16)]
+        + [((EDGE, width), BF16), ((frames, width), BF16), ((EDGE, width), BF16), ((frames, width), BF16)]
+        + [(conv_kernel.shape, F32), ((frames, width), F32), ((frames, LANES), F32)],
+        copies=7,
     )
     got = swap(send, "ctx")
     back, pre_grad, act = call(
         keeper_back,
+        [((rows, width), BF16, "h"), ((rows, 2 * units), BF16, "h"), ((rows, 2 * units), BF16, "h")],
+        [("v", got), ("v", adapt_down), ("v", adapt_up)],
         [((rows, width), BF16), ((rows, 2 * units), BF16), ((rows, 2 * units), BF16)],
-        [("v", got), ("v", adapt_down), ("v", adapt_up)],
+        copies=3,
     )
     grad_back = swap(back, "ctx")
     share = width // dp
@@ -329,11 +371,15 @@
     grad_back, kept, given = lax.optimization_barrier((grad_back, kept, given))
     total, edges, branch = call(
         sum_gradients,
-        [((frames, width), F32), ((2, EDGE, width), F32), ((rows, width), BF16)],
+        [((frames, width), F32, "h"), ((2, EDGE, width), F32, "h"), ((rows, width), BF16, "h")],
         where
-        + [("v", grad_back), ("v", cot), ("v", summed), ("v", inv), ("v", gain)]
-        + [("v", left), ("v", own), ("v", right), ("v", act), ("v", adapt_up)],
-        [((ctx, width), F32), ((frames + 2 * EDGE, width), F32), ((frames, width), F32)],
+        + [("v", gain), ("h", grad_back), ("h", summed), ("h", inv), ("h", cot), ("h", own)]
+        + [("h", left), ("h", right), ("h", act), ("h", adapt_up)],
+        [((ctx, width), F32), ((frames + 2 * EDGE, width), F32), ((frames, width), F32), ((rows, width), BF16)]
+        + [((frames, width), F32), ((frames, LANES), F32), ((frames, width), BF16), ((frames, width), BF16)]
+        + [((EDGE, width), BF16), ((EDGE, width), BF16), ((rows, 2 * units), BF16), (adapt_up.shape, BF16)]
+        + [((frames, width), F32), ((rows, width), BF16)],
+        copies=13,
     )
     branch_back = swap(branch, "ctx")
     (got,) = exchanged([kept, given], "dp", 8)

time: 247 us -> 251 us (1.016)
  Pallas kernels: 24.7 us -> 28.1 us
    pallas_call x10, Pallas kernels: 24.7 us -> 28.1 us  [call(): pl.pallas_call(body, out_shape=tuple((jax.ShapeDtypeStruct(out[0], out[1]...]
where the time goes in v4:
time: 251 us; the launch traced here: 250 us
  blocking collectives  83.7 us (33%)
  starting transfers between devices  70.6 us (28%)
  waiting for transfers between devices  47 us (19%)
  Pallas kernels  28.1 us (11%)
  local copies, waits for them, and re-layouts  18.6 us (7%)
    all_to_all x1, blocking collectives, swap(): return lax.all_to_all(cells, axis, split_axis=0, concat_axis=0, tiled=True)  83.7 us
    all_to_all x4, starting transfers between devices, swap(): return lax.all_to_all(cells, axis, split_axis=0, concat_axis=0, tiled=True)  36.2 us
    pallas_call x10, Pallas kernels, call(): pl.pallas_call(body, out_shape=tuple((jax.ShapeDtypeStruct(out[0], out[1]...  28.1 us
    ppermute x5, starting transfers between devices, exchanged(): lax.ppermute(block, axis, [(i, i ^ turn * unit) for i in range(count)])  22.3 us
    ppermute x2, waiting for transfers between devices, from_sides(): right = lax.ppermute(head, axis, [(i + 1, i) for i in range(count - 1)])  20.9 us
    unnamed x55, local copies, waits for them, and re-layouts  14.9 us
    all_to_all x4, waiting for transfers between devices, swap(): return lax.all_to_all(cells, axis, split_axis=0, concat_axis=0, tiled=True)  13.1 us
    ppermute x5, waiting for transfers between devices, exchanged(): lax.ppermute(block, axis, [(i, i ^ turn * unit) for i in range(count)])  12.9 us
  transfers between devices with their start and end apart: 13, of which 6 were waited for; matrix products, arithmetic and copies ran while one was open for 1% of the time, Pallas kernels for 4%

profile of v4, /device:TPU:1, one launch (start us, length us, event | category | flops | bytes accessed | tf_op | source)
XLA Modules:
  0.0 249.7 jit_solution(16198890961135452491)
XLA Ops:
  0.6 0.8 slice_bitcast_fusion.2
  1.5 1.3 collective-permute-start.1
  2.8 5.5 %collective-permute-start = (bf16[16,1536]{1,0:T(8,128)(2,1)S(1)}, bf16[16,1536]{1,0:T(8,128)(2,1)S(1)}, u32[]{:S(2)}, u32[]{:S(2)}) collective-permute-start(bf16[16,1536]{1,0:T(8,128)(2,1)S(1)} %get-tuple-element.65), channel_id=1, source_target_pairs={{0,1},{1,2},{2,3},{3,4},{4,5},{5,6},{6,7},{7,8},{8,9},{9,10},{10,1... | collective-permute-start | bytes 147464 | tf_op jit(solution)/shard_map/ppermute | solution.py:298
  8.2 0.8 pad_add_fusion.numbers
  9.0 0.7 reshape.48.gain
  9.7 1.1 copy-done.4
  10.8 1.1 copy-done.6
  11.8 0.9 copy-done.15
  12.8 7.6 %shard_map.136 = (bf16[32,32,1536]{2,1,0:T(8,128)(2,1)S(1)}, f32[192,1536]{1,0:T(8,128)S(1)}, f32[192,128]{1,0:T(8,128)S(1)}) custom-call(s32[96]{0:T(128)S(1)} %pad_add_fusion.numbers, bf16[16,1536]{1,0:T(8,128)(2,1)S(1)} %collective-permute-done.left_h, bf16[192,1536]{1,0:T(8,128)(2,1)S(1)} %bitcast.25, ...), custom_call_target="tpu_custom_call" | custom-call | tf_op jit(solution)/shard_map/pallas_call | solution.py:27
  20.4 1.0 copy-done
  21.4 83.7 %all_to_all.39.got = bf16[32,32,1536]{2,1,0:T(8,128)(2,1)S(1)} all-to-all(bf16[32,32,1536]{2,1,0:T(8,128)(2,1)S(1)} %get-tuple-element.35), channel_id=1, replica_groups=mesh['dp'=16,'ctx'=32] {'ctx'}, dimensions={0} | all-to-all | bytes 6291456 | tf_op jit(solution)/shard_map/all_to_all | solution.py:312
  105.1 1.9 shard_map.137
  107.0 0.7 copy-done.17
  107.7 1.2 copy-done.8
  108.8 7.4 %all-to-all-start.1 = ((bf16[32,16,1536]{2,1,0:T(8,128)(2,1)}), bf16[32,16,1536]{2,1,0:T(8,128)(2,1)}, u32[]{:S(2)}, u32[]{:S(2)}) async-start(bf16[32,16,1536]{2,1,0:T(8,128)(2,1)} %bitcast.29), calls=%async_computation.1 | async-start | bytes 3145728 | tf_op jit(solution)/shard_map/all_to_all | solution.py:312
  116.2 0.9 copy-done.18
  117.2 1.6 shard_map.138
  118.8 5.1 %collective-permute-start.2 = (bf16[8,192,256]{2,1,0:T(8,128)(2,1)S(1)}, bf16[8,192,256]{2,1,0:T(8,128)(2,1)S(1)}, u32[]{:S(2)}, u32[]{:S(2)}) collective-permute-start(bf16[8,192,256]{2,1,0:T(8,128)(2,1)S(1)} %get-tuple-element.40), channel_id=1, source_target_pairs={{0,32},{32,0},{64,96},{96,64},{128,160},{160,128},{192,224},{224,1... | collective-permute-start | bytes 2359304 | tf_op jit(solution)/shard_map/ppermute | solution.py:306
  123.9 1.9 collective-permute-done.2.got
  126.0 3.5 %collective-permute-start.3 = (bf16[2,192,256]{2,1,0:T(8,128)(2,1)S(1)}, bf16[2,192,256]{2,1,0:T(8,128)(2,1)S(1)}, u32[]{:S(2)}, u32[]{:S(2)}) collective-permute-start(bf16[2,192,256]{2,1,0:T(8,128)(2,1)S(1)} %get-tuple-element.42), channel_id=1, source_target_pairs={{0,64},{32,96},{64,0},{96,32},{128,192},{160,224},{192,128},{224,1... | collective-permute-start | bytes 589832 | tf_op jit(solution)/shard_map/ppermute | solution.py:306
  129.5 4.2 %collective-permute-start.4 = (bf16[2,192,256]{2,1,0:T(8,128)(2,1)S(1)}, bf16[2,192,256]{2,1,0:T(8,128)(2,1)S(1)}, u32[]{:S(2)}, u32[]{:S(2)}) collective-permute-start(bf16[2,192,256]{2,1,0:T(8,128)(2,1)S(1)} %get-tuple-element.43), channel_id=1, source_target_pairs={{0,128},{32,160},{64,192},{96,224},{128,0},{160,32},{192,64},{224,... | collective-permute-start | bytes 589832 | tf_op jit(solution)/shard_map/ppermute | solution.py:306
  133.7 1.9 collective-permute-start.5
  135.6 11.0 %collective-permute-done.4.second = bf16[2,192,256]{2,1,0:T(8,128)(2,1)S(1)} collective-permute-done((bf16[2,192,256]{2,1,0:T(8,128)(2,1)S(1)}, bf16[2,192,256]{2,1,0:T(8,128)(2,1)S(1)}, u32[]{:S(2)}, u32[]{:S(2)}) %collective-permute-start.4) | collective-permute-done | bytes 196640 | tf_op jit(solution)/shard_map/ppermute | solution.py:306
  146.8 0.7 copy-done.19
  147.4 0.6 copy-done.25
  148.1 2.8 %all-to-all-done.1 = bf16[32,16,1536]{2,1,0:T(8,128)(2,1)} async-done(((bf16[32,16,1536]{2,1,0:T(8,128)(2,1)}), bf16[32,16,1536]{2,1,0:T(8,128)(2,1)}, u32[]{:S(2)}, u32[]{:S(2)}) %all-to-all-start.1) | async-done | bytes 1572896 | tf_op jit(solution)/shard_map/all_to_all | solution.py:312
  150.9 0.9 copy-done.13
  151.8 0.9 copy-done.24
  152.7 9.0 %shard_map.141 = (f32[192,1536]{1,0:T(8,128)S(1)}, f32[2,16,1536]{2,1,0:T(8,128)S(1)}, bf16[512,1536]{1,0:T(8,128)(2,1)S(1)}) custom-call(s32[96]{0:T(128)S(1)} %pad_add_fusion.numbers, f32[1,1536]{1,0:T(1,128)S(1)} %reshape.48.gain, bf16[512,1536]{1,0:T(8,128)(2,1)} %bitcast.7.back_h, f32[192,1536]{1,0:T(8,128)S(1)} %copy-done.1, ...), custom_call_target="tpu_custom_call" | custom-call | tf_op jit(solution)/shard_map/pallas_call | solution.py:27
  161.8 1.0 copy-done.10
  162.8 0.7 copy-done.21
  163.5 1.2 copy-done.9
  164.6 8.2 %all-to-all-start.2 = ((bf16[32,16,1536]{2,1,0:T(8,128)(2,1)}), bf16[32,16,1536]{2,1,0:T(8,128)(2,1)S(1)}, u32[]{:S(2)}, u32[]{:S(2)}) async-start(bf16[32,16,1536]{2,1,0:T(8,128)(2,1)} %bitcast.30), calls=%async_computation.2 | async-start | bytes 3145728 | tf_op jit(solution)/shard_map/all_to_all | solution.py:312
  172.8 7.6 %collective-permute-start.6 = (bf16[192,256]{1,0:T(8,128)(2,1)S(1)}, bf16[192,256]{1,0:T(8,128)(2,1)S(1)}, u32[]{:S(2)}, u32[]{:S(2)}) collective-permute-start(bf16[192,256]{1,0:T(8,128)(2,1)S(1)} %copy-done.26), channel_id=1, source_target_pairs={{0,256},{32,288},{64,320},{96,352},{128,384},{160,416},{192,448},{... | collective-permute-start | bytes 294920 | tf_op jit(solution)/shard_map/ppermute | solution.py:306
  180.4 1.3 collective-permute-start.8
  181.7 4.0 %collective-permute-start.7 = (f32[16,1536]{1,0:T(8,128)S(1)}, f32[16,1536]{1,0:T(8,128)S(1)}, u32[]{:S(2)}, u32[]{:S(2)}) collective-permute-start(f32[16,1536]{1,0:T(8,128)S(1)} %get-tuple-element.67), channel_id=1, source_target_pairs={{0,1},{1,2},{2,3},{3,4},{4,5},{5,6},{6,7},{7,8},{8,9},{9,10},{10,1... | collective-permute-start | bytes 294920 | tf_op jit(solution)/shard_map/ppermute | solution.py:298
  185.8 0.7 shard_map.142
  186.5 20.9 %collective-permute-done.8.right = f32[16,1536]{1,0:T(8,128)S(1)} collective-permute-done((f32[16,1536]{1,0:T(8,128)S(1)}, f32[16,1536]{1,0:T(8,128)S(1)}, u32[]{:S(2)}, u32[]{:S(2)}) %collective-permute-start.8) | collective-permute-done | bytes 98336 | tf_op jit(solution)/shard_map/ppermute | solution.py:299
  207.7 0.7 broadcast_in_dim.22
  208.4 15.7 %all-to-all-start.3 = ((f32[16,1,1536]{2,1,0:T(1,128)}), f32[16,1,1536]{2,1,0:T(1,128)S(1)}, u32[]{:S(2)}, u32[]{:S(2)}) async-start(f32[16,1,1536]{2,1,0:T(1,128)} %broadcast_in_dim.22), calls=%async_computation.3 | async-start | bytes 196608 | tf_op jit(solution)/shard_map/all_to_all | solution.py:312
  224.2 1.3 copy-done.11
  225.4 4.4 %shard_map.145 = bf16[192,1536]{1,0:T(8,128)(2,1)} custom-call(f32[16,1536]{1,0:T(8,128)S(1)} %collective-permute-done.7.left, f32[192,1536]{1,0:T(8,128)S(1)} %copy-done.11, f32[16,1536]{1,0:T(8,128)S(1)} %collective-permute-done.8.right, f32[31,1536]{1,0:T(8,128)S(1)} %copy-done.16), custom_call_target="tpu_custom_call" | custom-call | tf_op jit(solution)/shard_map/pallas_call | solution.py:27
  229.8 2.8 %all-to-all-done.3 = f32[16,1,1536]{2,1,0:T(1,128)S(1)} async-done(((f32[16,1,1536]{2,1,0:T(1,128)}), f32[16,1,1536]{2,1,0:T(1,128)S(1)}, u32[]{:S(2)}, u32[]{:S(2)}) %all-to-all-start.3) | async-done | bytes 98336 | tf_op jit(solution)/shard_map/all_to_all | solution.py:312
  232.7 0.8 broadcast_in_dim.24
  233.5 5.0 %all-to-all-start.4 = ((f32[32,1,1536]{2,1,0:T(1,128)}), f32[32,1,1536]{2,1,0:T(1,128)S(1)}, u32[]{:S(2)}, u32[]{:S(2)}) async-start(f32[32,1,1536]{2,1,0:T(1,128)} %broadcast_in_dim.24), calls=%async_computation.4 | async-start | bytes 393216 | tf_op jit(solution)/shard_map/all_to_all | solution.py:312
  238.5 2.3 shard_map.143
  240.8 7.5 %all-to-all-done.4 = f32[32,1,1536]{2,1,0:T(1,128)S(1)} async-done(((f32[32,1,1536]{2,1,0:T(1,128)}), f32[32,1,1536]{2,1,0:T(1,128)S(1)}, u32[]{:S(2)}, u32[]{:S(2)}) %all-to-all-start.4) | async-done | bytes 196640 | tf_op jit(solution)/shard_map/all_to_all | solution.py:312
  248.3 0.7 copy.17
  (55 shorter events, 1.4 us)
Async XLA Ops:
  1.5 8.2 %collective-permute-start.1 = (bf16[16,1536]{1,0:T(8,128)(2,1)S(1)}, bf16[16,1536]{1,0:T(8,128)(2,1)S(1)}, u32[]{:S(2)}, u32[]{:S(2)}) collective-permute-start(bf16[16,1536]{1,0:T(8,128)(2,1)S(1)} %get-tuple-element.64), channel_id=1, source_target_pairs={{1,0},{2,1},{3,2},{4,3},{5,4},{6,5},{7,6},{8,7},{9,8},{10,9},{11,1... | collective-permute-start | bytes 147464 | tf_op jit(solution)/shard_map/ppermute | solution.py:299
  2.8 6.9 %collective-permute-start = (bf16[16,1536]{1,0:T(8,128)(2,1)S(1)}, bf16[16,1536]{1,0:T(8,128)(2,1)S(1)}, u32[]{:S(2)}, u32[]{:S(2)}) collective-permute-start(bf16[16,1536]{1,0:T(8,128)(2,1)S(1)} %get-tuple-element.65), channel_id=1, source_target_pairs={{0,1},{1,2},{2,3},{3,4},{4,5},{5,6},{6,7},{7,8},{8,9},{9,10},{10,1... | collective-permute-start | bytes 147464 | tf_op jit(solution)/shard_map/ppermute | solution.py:298
  9.7 1.1 copy-start.4
  10.8 1.1 copy-start.6
  11.8 0.9 copy-start.15
  20.4 1.0 copy-start
  21.4 83.7 %copy-start.23 = (f32[192,128]{1,0:T(8,128)}, f32[192,128]{1,0:T(8,128)S(1)}, u32[]{:S(2)}) copy-start(f32[192,128]{1,0:T(8,128)S(1)} %get-tuple-element.49.inv_h) | copy-start | bytes 294916
  21.4 83.7 %copy-start.2 = (bf16[2,128,1536]{2,1,0:T(8,128)(2,1)S(1)}, bf16[2,128,1536]{2,1,0:T(8,128)(2,1)}, u32[]{:S(2)}) copy-start(bf16[2,128,1536]{2,1,0:T(8,128)(2,1)} %up_h.1) | copy-start | bytes 2359300
  21.4 83.7 %copy-start.14 = (bf16[2,1536,128]{2,1,0:T(8,128)(2,1)S(1)}, bf16[2,1536,128]{2,1,0:T(8,128)(2,1)}, u32[]{:S(2)}) copy-start(bf16[2,1536,128]{2,1,0:T(8,128)(2,1)} %down.1) | copy-start | bytes 2359300
  107.0 0.7 copy-start.17
  107.7 1.2 copy-start.8
  107.7 8.5 %copy-start.12 = (bf16[512,256]{1,0:T(8,128)(2,1)}, bf16[512,256]{1,0:T(8,128)(2,1)S(1)}, u32[]{:S(2)}) copy-start(bf16[512,256]{1,0:T(8,128)(2,1)S(1)} %get-tuple-element.38.act.act_h) | copy-start | bytes 786436
  108.8 42.0 %all-to-all-start.1 = ((bf16[32,16,1536]{2,1,0:T(8,128)(2,1)}), bf16[32,16,1536]{2,1,0:T(8,128)(2,1)}, u32[]{:S(2)}, u32[]{:S(2)}) async-start(bf16[32,16,1536]{2,1,0:T(8,128)(2,1)} %bitcast.29), calls=%async_computation.1 | async-start | bytes 3145728 | tf_op jit(solution)/shard_map/all_to_all | solution.py:312
  116.2 1.0 copy-start.18
  118.8 7.0 %collective-permute-start.2 = (bf16[8,192,256]{2,1,0:T(8,128)(2,1)S(1)}, bf16[8,192,256]{2,1,0:T(8,128)(2,1)S(1)}, u32[]{:S(2)}, u32[]{:S(2)}) collective-permute-start(bf16[8,192,256]{2,1,0:T(8,128)(2,1)S(1)} %get-tuple-element.40), channel_id=1, source_target_pairs={{0,32},{32,0},{64,96},{96,64},{128,160},{160,128},{192,224},{224,1... | collective-permute-start | bytes 2359304 | tf_op jit(solution)/shard_map/ppermute | solution.py:306
  125.8 25.0 %copy-start.1 = (f32[192,1536]{1,0:T(8,128)S(1)}, f32[192,1536]{1,0:T(8,128)}, u32[]{:S(2)}) copy-start(f32[192,1536]{1,0:T(8,128)} %copy-done) | copy-start | bytes 3538948
  125.8 25.0 %copy-start.3 = (bf16[2,128,1536]{2,1,0:T(8,128)(2,1)S(1)}, bf16[2,128,1536]{2,1,0:T(8,128)(2,1)}, u32[]{:S(2)}) copy-start(bf16[2,128,1536]{2,1,0:T(8,128)(2,1)} %up_h.1) | copy-start | bytes 2359300
  125.8 25.0 %copy-start.5 = (bf16[1,192,1536]{2,1,0:T(8,128)(2,1)S(1)}, bf16[1,192,1536]{2,1,0:T(8,128)(2,1)}, u32[]{:S(2)}) copy-start(bf16[1,192,1536]{2,1,0:T(8,128)(2,1)} %param.9) | copy-start | bytes 1769476
  125.8 25.0 %copy-start.7 = (bf16[1,192,1536]{2,1,0:T(8,128)(2,1)S(1)}, bf16[1,192,1536]{2,1,0:T(8,128)(2,1)}, u32[]{:S(2)}) copy-start(bf16[1,192,1536]{2,1,0:T(8,128)(2,1)} %param.10) | copy-start | bytes 1769476
  126.0 9.6 %collective-permute-start.3 = (bf16[2,192,256]{2,1,0:T(8,128)(2,1)S(1)}, bf16[2,192,256]{2,1,0:T(8,128)(2,1)S(1)}, u32[]{:S(2)}, u32[]{:S(2)}) collective-permute-start(bf16[2,192,256]{2,1,0:T(8,128)(2,1)S(1)} %get-tuple-element.42), channel_id=1, source_target_pairs={{0,64},{32,96},{64,0},{96,32},{128,192},{160,224},{192,128},{224,1... | collective-permute-start | bytes 589832 | tf_op jit(solution)/shard_map/ppermute | solution.py:306
  129.5 17.2 %collective-permute-start.4 = (bf16[2,192,256]{2,1,0:T(8,128)(2,1)S(1)}, bf16[2,192,256]{2,1,0:T(8,128)(2,1)S(1)}, u32[]{:S(2)}, u32[]{:S(2)}) collective-permute-start(bf16[2,192,256]{2,1,0:T(8,128)(2,1)S(1)} %get-tuple-element.43), channel_id=1, source_target_pairs={{0,128},{32,160},{64,192},{96,224},{128,0},{160,32},{192,64},{224,... | collective-permute-start | bytes 589832 | tf_op jit(solution)/shard_map/ppermute | solution.py:306
  133.7 13.0 %collective-permute-start.5 = (bf16[2,192,256]{2,1,0:T(8,128)(2,1)S(1)}, bf16[2,192,256]{2,1,0:T(8,128)(2,1)S(1)}, u32[]{:S(2)}, u32[]{:S(2)}) collective-permute-start(bf16[2,192,256]{2,1,0:T(8,128)(2,1)S(1)} %get-tuple-element.44), channel_id=1, source_target_pairs={{0,192},{32,224},{64,128},{96,160},{128,64},{160,96},{192,0},{224,... | collective-permute-start | bytes 589832 | tf_op jit(solution)/shard_map/ppermute | solution.py:306
  146.8 0.7 copy-start.19
  147.4 0.6 copy-start.25
  150.9 1.0 copy-start.13
  151.8 0.9 copy-start.24
  161.8 1.0 copy-start.10
  162.8 0.7 copy-start.21
  163.5 1.2 copy-start.9
  164.6 8.2 %copy-start.26 = (bf16[192,256]{1,0:T(8,128)(2,1)S(1)}, bf16[192,256]{1,0:T(8,128)(2,1)}, u32[]{:S(2)}) copy-start(bf16[192,256]{1,0:T(8,128)(2,1)} %copy-done.25) | copy-start | bytes 294916
  164.6 15.8 %copy-start.22 = (f32[2,16,1536]{2,1,0:T(8,128)S(1)}, f32[2,16,1536]{2,1,0:T(8,128)}, u32[]{:S(2)}) copy-start(f32[2,16,1536]{2,1,0:T(8,128)} %copy-done.21) | copy-start | bytes 589828
  164.6 21.1 %copy-start.20 = (f32[192,256]{1,0:T(8,128)S(1)}, f32[192,256]{1,0:T(8,128)}, u32[]{:S(2)}) copy-start(f32[192,256]{1,0:T(8,128)} %copy-done.19) | copy-start | bytes 589828
  164.6 42.8 %all-to-all-start.2 = ((bf16[32,16,1536]{2,1,0:T(8,128)(2,1)}), bf16[32,16,1536]{2,1,0:T(8,128)(2,1)S(1)}, u32[]{:S(2)}, u32[]{:S(2)}) async-start(bf16[32,16,1536]{2,1,0:T(8,128)(2,1)} %bitcast.30), calls=%async_computation.2 | async-start | bytes 3145728 | tf_op jit(solution)/shard_map/all_to_all | solution.py:312
  172.8 51.4 %copy-start.16 = (f32[31,1536]{1,0:T(8,128)S(1)}, f32[31,1536]{1,0:T(8,128)}, u32[]{:S(2)}) copy-start(f32[31,1536]{1,0:T(8,128)} %taps.1) | copy-start | bytes 571396
  172.8 12.9 %collective-permute-start.6 = (bf16[192,256]{1,0:T(8,128)(2,1)S(1)}, bf16[192,256]{1,0:T(8,128)(2,1)S(1)}, u32[]{:S(2)}, u32[]{:S(2)}) collective-permute-start(bf16[192,256]{1,0:T(8,128)(2,1)S(1)} %copy-done.26), channel_id=1, source_target_pairs={{0,256},{32,288},{64,320},{96,352},{128,384},{160,416},{192,448},{... | collective-permute-start | bytes 294920 | tf_op jit(solution)/shard_map/ppermute | solution.py:306
  180.4 26.9 %collective-permute-start.8 = (f32[16,1536]{1,0:T(8,128)S(1)}, f32[16,1536]{1,0:T(8,128)S(1)}, u32[]{:S(2)}, u32[]{:S(2)}) collective-permute-start(f32[16,1536]{1,0:T(8,128)S(1)} %get-tuple-element.66), channel_id=1, source_target_pairs={{1,0},{2,1},{3,2},{4,3},{5,4},{6,5},{7,6},{8,7},{9,8},{10,9},{11,1... | collective-permute-start | bytes 294920 | tf_op jit(solution)/shard_map/ppermute | solution.py:299
  181.7 25.6 %collective-permute-start.7 = (f32[16,1536]{1,0:T(8,128)S(1)}, f32[16,1536]{1,0:T(8,128)S(1)}, u32[]{:S(2)}, u32[]{:S(2)}) collective-permute-start(f32[16,1536]{1,0:T(8,128)S(1)} %get-tuple-element.67), channel_id=1, source_target_pairs={{0,1},{1,2},{2,3},{3,4},{4,5},{5,6},{6,7},{7,8},{8,9},{9,10},{10,1... | collective-permute-start | bytes 294920 | tf_op jit(solution)/shard_map/ppermute | solution.py:298
  208.4 24.2 %all-to-all-start.3 = ((f32[16,1,1536]{2,1,0:T(1,128)}), f32[16,1,1536]{2,1,0:T(1,128)S(1)}, u32[]{:S(2)}, u32[]{:S(2)}) async-start(f32[16,1,1536]{2,1,0:T(1,128)} %broadcast_in_dim.22), calls=%async_computation.3 | async-start | bytes 196608 | tf_op jit(solution)/shard_map/all_to_all | solution.py:312
  224.2 1.3 copy-start.11
  233.5 14.8 %all-to-all-start.4 = ((f32[32,1,1536]{2,1,0:T(1,128)}), f32[32,1,1536]{2,1,0:T(1,128)S(1)}, u32[]{:S(2)}, u32[]{:S(2)}) async-start(f32[32,1,1536]{2,1,0:T(1,128)} %broadcast_in_dim.24), calls=%async_computation.4 | async-start | bytes 393216 | tf_op jit(solution)/shard_map/all_to_all | solution.py:312

commit v5 on v3

--- a/solution.py
+++ b/solution.py
@@ -9,6 +9,7 @@
 from jax.sharding import PartitionSpec as P
 
 BLOCK = 16
+HALF = BLOCK // 2
 SEGMENTS = 16
 EDGE = 16
 LANES = 128
@@ -66,7 +67,7 @@
     return cells if by == 0 else pltpu.roll(cells, cells.shape[0] - by, 0)
 
 
-def conv_and_norm(numbers, left, own, right, cot, taps, gain, send, summed, inv, cells, normed):
+def conv_and_norm(numbers, left, own, right, cot, taps, gain, send, summed, cells, normed):
     frames, width = own.shape
     rows = send.shape[0] * BLOCK
     blocks = (send.shape[0], BLOCK, width)
@@ -102,7 +103,6 @@
 
     squares = lax.fori_loop(0, width // LANES, column, jnp.zeros((frames, LANES), F32))
     scale = lax.rsqrt(jnp.sum(squares, axis=1, keepdims=True) * (1.0 / width) + 1e-06)
-    inv[...] = jnp.broadcast_to(scale, inv.shape)
     normed[...] = (summed[...] * scale * gain[...]).astype(BF16)
     send[:, :BLOCK] = jnp.dot(spread, normed[...], preferred_element_type=F32).astype(BF16).reshape(blocks)
 
@@ -112,7 +112,7 @@
     return got[:, :BLOCK].reshape(shape), got[:, BLOCK:].reshape(shape)
 
 
-def keeper_back(got, down, up, back, pre_grad, act):
+def keeper_values(got, down, up):
     rows_in, cot_in = received(got)
     rows, width = rows_in.shape
     units = down.shape[2]
@@ -124,25 +124,30 @@
     pre = jnp.dot(rows_in, both_down, preferred_element_type=F32)
     slope_of = lax.dot_general(cot_in, both_up, (((1,), (1,)), ((), ())), preferred_element_type=F32)
     sig = jax.nn.sigmoid(pre)
-    act[...] = (keep * (pre * sig)).astype(BF16)
+    act = (keep * (pre * sig)).astype(BF16)
     grads = (keep * (slope_of * (sig * (1.0 + pre * (1.0 - sig))))).astype(BF16)
-    pre_grad[...] = grads
+    return rows_in, cot_in, both_down, grads, act
+
+
+def keeper_back(got, down, up, back):
+    _, _, both_down, grads, _ = keeper_values(got, down, up)
     back[...] = lax.dot_general(grads, both_down, (((1,), (1,)), ((), ())), preferred_element_type=F32).astype(BF16)
 
 
 def sum_last_rows(back, out):
     row = lax.broadcasted_iota(jnp.int32, (out.shape[0], back.shape[0]), 1)
-    last = jnp.where(row % BLOCK == BLOCK - 1, 1.0, 0.0).astype(BF16)
+    last = jnp.where(row % HALF == HALF - 1, 1.0, 0.0).astype(BF16)
     out[...] = jnp.dot(last, back[...], preferred_element_type=F32)
 
 
-def keeper_grads(place, got, pre_grad, act, kept, given, down, up):
+def keeper_grads(place, got, down_w, up_w, kept, given, act, down, up):
     parts, twice, _ = kept.shape
     part = twice // 2
     core = place[0] % 2
-    rows_in, cot_in = received(got)
-    down[...] = lax.dot_general(rows_in, pre_grad[...], (((0,), (0,)), ((), ())), preferred_element_type=F32)
-    up[...] = lax.dot_general(cot_in, act[...], (((0,), (0,)), ((), ())), preferred_element_type=F32)
+    rows_in, cot_in, _, grads, acts = keeper_values(got, down_w, up_w)
+    act[...] = acts
+    down[...] = lax.dot_general(rows_in, grads, (((0,), (0,)), ((), ())), preferred_element_type=F32)
+    up[...] = lax.dot_general(cot_in, acts, (((0,), (0,)), ((), ())), preferred_element_type=F32)
     for at in range(parts):
         near = pl.ds(pl.multiple_of((2 * at + core) * part, part), part)
         far = pl.ds(pl.multiple_of((2 * at + 1 - core) * part, part), part)
@@ -168,7 +173,7 @@
 
 
 def sum_gradients(
-    numbers, back, cot, summed, inv, gain, left, own, right, act, up, total, edges, branch, sums, cells, frames_grad
+    numbers, back, cot, summed, gain, left, own, right, act, up, total, edges, low, high, sums, cells, frames_grad, inv
 ):
     frames, width = cot.shape
     gather = gather_matrix(segments(numbers), back.shape[0], frames)
@@ -176,7 +181,8 @@
     cells[EDGE : EDGE + frames] = own[...].astype(F32)
     cells[EDGE + frames :] = right[...].astype(F32)
     frames_grad[...] = jnp.dot(gather, back[...], preferred_element_type=F32)
-    scale = inv[:, :1]
+    scale = lax.rsqrt(jnp.sum(summed[...] * summed[...], axis=1, keepdims=True) * (1.0 / width) + 1e-06)
+    inv[...] = jnp.broadcast_to(scale, inv.shape)
     inner = jnp.sum(gain[...] * frames_grad[...] * summed[...], axis=1, keepdims=True) * (1.0 / width)
     pull = scale * scale * scale * inner
     half = frames // 2
@@ -210,12 +216,15 @@
     edges[0] = total[:EDGE]
     edges[1] = total[frames - EDGE :]
     both_up = up[...].reshape(act.shape[1], width)
-    row = lax.broadcasted_iota(jnp.int32, (branch.shape[0], sums.shape[0]), 0)
-    block = lax.broadcasted_iota(jnp.int32, (branch.shape[0], sums.shape[0]), 1)
+    count, blocks = act.shape[0], sums.shape[0]
+    row = lax.broadcasted_iota(jnp.int32, (count, blocks), 0)
+    block = lax.broadcasted_iota(jnp.int32, (count, blocks), 1)
     last = jnp.where(row == block * BLOCK + BLOCK - 1, 1.0, 0.0).astype(BF16)
-    outputs = jnp.dot(act[...], both_up, preferred_element_type=F32)
-    outputs = outputs + jnp.dot(last, sums[...].astype(BF16), preferred_element_type=F32)
-    branch[...] = outputs.astype(BF16)
+    branch = jnp.dot(act[...], both_up, preferred_element_type=F32)
+    branch = branch + jnp.dot(last, sums[...].astype(BF16), preferred_element_type=F32)
+    branch = branch.reshape(blocks, BLOCK, width)
+    low[...] = branch[:, :HALF].reshape(low.shape).astype(BF16)
+    high[...] = branch[:, HALF:].reshape(high.shape).astype(BF16)
 
 
 def input_gradient(left, own, right, taps, out, cells):
@@ -242,9 +251,18 @@
     lax.fori_loop(0, width // LANES, column, 0)
 
 
-def add_branch(numbers, back, summed, out):
-    gather = gather_matrix(segments(numbers), back.shape[0], summed.shape[0])
-    out[...] = (summed[...] + jnp.dot(gather, back[...], preferred_element_type=F32)).astype(BF16)
+def add_branch(numbers, low, high, summed, out):
+    frames = summed.shape[0]
+    slot = frame_slots(segments(numbers), (frames, LANES), 0)
+    lane = lax.broadcasted_iota(jnp.int32, (frames, LANES), 1)
+    within = slot % BLOCK
+    place = (slot // BLOCK) * HALF + within % HALF
+    total = summed[...]
+    for part, first in ((low, True), (high, False)):
+        here = (within < HALF) if first else (within >= HALF)
+        hits = [jnp.where(here & (lane + at == place), 1.0, 0.0) for at in range(0, part.shape[0], LANES)]
+        total = total + jnp.dot(jnp.concatenate(hits, axis=1).astype(BF16), part[...], preferred_element_type=F32)
+    out[...] = total.astype(BF16)
 
 
 def place_grads(scale, kept, got, down, up):
@@ -293,25 +311,23 @@
     where = [("s", numbers)]
 
     left, right = from_sides(own[:EDGE], own[frames - EDGE :], "ctx")
-    send, summed, inv = call(
+    send, summed = call(
         conv_and_norm,
-        [((ctx, 2 * BLOCK, width), BF16), ((frames, width), F32), ((frames, LANES), F32)],
+        [((ctx, 2 * BLOCK, width), BF16), ((frames, width), F32)],
         where + [("v", left), ("v", own), ("v", right), ("v", cot), ("v", conv_kernel), ("v", gain)],
         [((frames + 2 * EDGE, width), F32), ((frames, width), BF16)],
     )
     got = swap(send, "ctx")
-    back, pre_grad, act = call(
-        keeper_back,
-        [((rows, width), BF16), ((rows, 2 * units), BF16), ((rows, 2 * units), BF16)],
-        [("v", got), ("v", adapt_down), ("v", adapt_up)],
+    (back,) = call(
+        keeper_back, [((rows, width), BF16)], [("v", got), ("v", adapt_down), ("v", adapt_up)]
     )
     grad_back = swap(back, "ctx")
     share = width // dp
     place = ("s", lax.axis_index("dp").astype(jnp.int32).reshape(1))
-    kept, given = call(
+    kept, given, act = call(
         keeper_grads,
-        [((dp // 2, 2 * share, 2 * units), F32), ((dp // 2, 2 * share, 2 * units), BF16)],
-        [place, ("v", got), ("v", pre_grad), ("v", act)],
+        [((dp // 2, 2 * share, 2 * units), F32), ((dp // 2, 2 * share, 2 * units), BF16), ((rows, 2 * units), BF16)],
+        [place, ("v", got), ("v", adapt_down), ("v", adapt_up)],
         [((width, 2 * units), F32), ((width, 2 * units), F32)],
     )
     (got,) = exchanged([kept, given], "dp", 1)
@@ -327,35 +343,40 @@
         pair_grads, [(piece, F32), (piece, BF16)], [place, ("v", chips[0])] + [("v", part) for part in got]
     )
     grad_back, kept, given = lax.optimization_barrier((grad_back, kept, given))
-    total, edges, branch = call(
+    total, edges, low, high = call(
         sum_gradients,
-        [((frames, width), F32), ((2, EDGE, width), F32), ((rows, width), BF16)],
+        [((frames, width), F32), ((2, EDGE, width), F32), ((rows // 2, width), BF16), ((rows // 2, width), BF16)],
         where
-        + [("v", grad_back), ("v", cot), ("v", summed), ("v", inv), ("v", gain)]
+        + [("v", grad_back), ("v", cot), ("v", summed), ("v", gain)]
         + [("v", left), ("v", own), ("v", right), ("v", act), ("v", adapt_up)],
-        [((ctx, width), F32), ((frames + 2 * EDGE, width), F32), ((frames, width), F32)],
-    )
-    branch_back = swap(branch, "ctx")
+        [((ctx, width), F32), ((frames + 2 * EDGE, width), F32), ((frames, width), F32), ((frames, LANES), F32)],
+    )
+    high_back = swap(high, "ctx")
     (got,) = exchanged([kept, given], "dp", 8)
     grad_down, grad_up = call(
         functools.partial(place_grads, grad_scale), [((2, share, units), F32)] * 2, [("v", kept), ("v", got)]
     )
     grad_left, grad_right = from_sides(edges[0], edges[1], "ctx")
-    branch_back, grad_down, grad_up, grad_left, grad_right = lax.optimization_barrier(
-        (branch_back, grad_down, grad_up, grad_left, grad_right)
-    )
-    (mine,) = call(sum_last_rows, [((8, width), F32)], [("v", branch_back)])
+    high_back, low, grad_down, grad_up, grad_left, grad_right = lax.optimization_barrier(
+        (high_back, low, grad_down, grad_up, grad_left, grad_right)
+    )
+    low_back = swap(low, "ctx")
+    (mine,) = call(sum_last_rows, [((8, width), F32)], [("v", high_back)])
+    mine = lax.all_gather(mine[:1], "dp", axis=0, tiled=True)
     (grad_input,) = call(
         input_gradient,
         [((frames, width), BF16)],
         [("v", grad_left), ("v", total), ("v", grad_right), ("v", conv_kernel)],
         [((frames + 2 * EDGE, width), F32)],
     )
-    mine = spread_rows(mine[:1], "dp")
-    mine, grad_input = lax.optimization_barrier((mine, grad_input))
-    mine = jnp.sum(mine, axis=0) * grad_scale
+    mine, low_back, grad_input = lax.optimization_barrier((mine, low_back, grad_input))
+    mine = jnp.sum(mine, axis=0, keepdims=True) * grad_scale
     reduced = spread_rows(mine, "ctx").reshape(ctx, width)
-    (output,) = call(add_branch, [((frames, width), BF16)], where + [("v", branch_back), ("v", summed)])
+    (output,) = call(
+        add_branch,
+        [((frames, width), BF16)],
+        where + [("v", low_back), ("v", high_back), ("v", summed)],
+    )
     return output[None], grad_input[None], reduced[:31], reduced[31], grad_down, jnp.transpose(grad_up, (0, 2, 1))
 
 

time: 247 us -> 247 us (level)
  blocking collectives: 83.7 us -> 102 us
  waiting for transfers between devices: 47 us -> 34.1 us
  starting transfers between devices: 70.6 us -> 65.7 us
  local copies, waits for them, and re-layouts: 18.6 us -> 15.4 us
    all_gather x0 -> x1, blocking collectives: none -> 20 us  [local(): mine = lax.all_gather(mine[:1], 'dp', axis=0, tiled=True)]
    ppermute x2, waiting for transfers between devices: 20.9 us -> 7.7 us  [from_sides(): right = lax.ppermute(head, axis, [(i + 1, i) for i in range(count - 1)])]
    ppermute x2, waiting for transfers between devices: 0.01 us -> 2.53 us  [from_sides(): left = lax.ppermute(tail, axis, [(i, i + 1) for i in range(count - 1)])]
    unnamed x55 -> x49, local copies, waits for them, and re-layouts: 14.9 us -> 12.4 us
  transfers between devices with their start and end apart: 13 -> 13, of which waited for: 6 -> 7; matrix products, arithmetic and copies ran while one was open for 1% -> 1% of each run, Pallas kernels for 4% -> 4%
where the time goes in v5:
time: 247 us; the launch traced here: 245 us
  blocking collectives  102 us (41%)
  starting transfers between devices  65.7 us (27%)
  waiting for transfers between devices  34.1 us (14%)
  Pallas kernels  26.5 us (11%)
  local copies, waits for them, and re-layouts  15.4 us (6%)
    all_to_all x1, blocking collectives, swap(): return lax.all_to_all(cells, axis, split_axis=0, concat_axis=0, tiled=True)  81.7 us
    all_to_all x4, starting transfers between devices, swap(): return lax.all_to_all(cells, axis, split_axis=0, concat_axis=0, tiled=True)  34 us
    pallas_call x10, Pallas kernels, call(): pl.pallas_call(body, out_shape=tuple((jax.ShapeDtypeStruct(shape, kind) f...  26.5 us
    ppermute x5, starting transfers between devices, exchanged(): lax.ppermute(block, axis, [(i, i ^ turn * unit) for i in range(count)])  21 us
    all_gather x1, blocking collectives, local(): mine = lax.all_gather(mine[:1], 'dp', axis=0, tiled=True)  20 us
    ppermute x5, waiting for transfers between devices, exchanged(): lax.ppermute(block, axis, [(i, i ^ turn * unit) for i in range(count)])  12.9 us
    unnamed x49, local copies, waits for them, and re-layouts  12.4 us
    all_to_all x4, waiting for transfers between devices, swap(): return lax.all_to_all(cells, axis, split_axis=0, concat_axis=0, tiled=True)  10.9 us
  transfers between devices with their start and end apart: 13, of which 7 were waited for; matrix products, arithmetic and copies ran while one was open for 1% of the time, Pallas kernels for 4%

profile of v5, /device:TPU:1, one launch (start us, length us, event | category | flops | bytes accessed | tf_op | source)
XLA Modules:
  0.0 245.1 jit_solution(2230471222433219969)
XLA Ops:
  0.6 0.8 slice_bitcast_fusion.2
  1.5 4.8 %collective-permute-start = (bf16[16,1536]{1,0:T(8,128)(2,1)S(1)}, bf16[16,1536]{1,0:T(8,128)(2,1)S(1)}, u32[]{:S(2)}, u32[]{:S(2)}) collective-permute-start(bf16[16,1536]{1,0:T(8,128)(2,1)S(1)} %get-tuple-element.65), channel_id=1, source_target_pairs={{0,1},{1,2},{2,3},{3,4},{4,5},{5,6},{6,7},{7,8},{8,9},{9,10},{10,1... | collective-permute-start | bytes 147464 | tf_op jit(solution)/shard_map/ppermute | solution.py:279
  6.3 1.3 collective-permute-start.1
  7.6 0.8 pad_add_fusion.numbers
  8.4 0.7 reshape.45.gain
  9.1 2.7 %collective-permute-done.1.right = bf16[16,1536]{1,0:T(8,128)(2,1)S(1)} collective-permute-done((bf16[16,1536]{1,0:T(8,128)(2,1)S(1)}, bf16[16,1536]{1,0:T(8,128)(2,1)S(1)}, u32[]{:S(2)}, u32[]{:S(2)}) %collective-permute-start.1) | collective-permute-done | bytes 49184 | tf_op jit(solution)/shard_map/ppermute | solution.py:280
  11.8 1.1 copy-done.8
  12.8 1.1 copy-done.10
  13.9 0.9 copy-done.15
  14.8 5.7 %shard_map.136 = (bf16[32,32,1536]{2,1,0:T(8,128)(2,1)S(1)}, f32[192,1536]{1,0:T(8,128)S(1)}) custom-call(s32[96]{0:T(128)S(1)} %pad_add_fusion.numbers, bf16[16,1536]{1,0:T(8,128)(2,1)S(1)} %collective-permute-done.left, bf16[192,1536]{1,0:T(8,128)(2,1)S(1)} %bitcast.34, bf16[16,1536]{1,0:T(8,128)(2,1)S(1)} %collective-permute-done.1.right, ...), custom_call_target="tpu_custom_call" | custom-call | tf_op jit(solution)/shard_map/pallas_call | solution.py:24
  20.6 81.7 %all_to_all.46.got = bf16[32,32,1536]{2,1,0:T(8,128)(2,1)S(1)} all-to-all(bf16[32,32,1536]{2,1,0:T(8,128)(2,1)S(1)} %get-tuple-element.35), channel_id=1, replica_groups=mesh['dp'=16,'ctx'=32] {'ctx'}, dimensions={0} | all-to-all | bytes 6291456 | tf_op jit(solution)/shard_map/all_to_all | solution.py:293
  102.3 1.4 shard_map.137
  103.7 1.2 copy-done.3
  104.9 8.3 %all-to-all-start.1 = ((bf16[32,16,1536]{2,1,0:T(8,128)(2,1)}), bf16[32,16,1536]{2,1,0:T(8,128)(2,1)}, u32[]{:S(2)}, u32[]{:S(2)}) async-start(bf16[32,16,1536]{2,1,0:T(8,128)(2,1)} %bitcast.32), calls=%async_computation.1 | async-start | bytes 3145728 | tf_op jit(solution)/shard_map/all_to_all | solution.py:293
  113.2 1.1 copy-done.1
  114.4 1.1 copy-done.7
  115.5 2.5 %shard_map.138 = (f32[8,192,256]{2,1,0:T(8,128)S(1)}, bf16[8,192,256]{2,1,0:T(8,128)(2,1)S(1)}, bf16[512,256]{1,0:T(8,128)(2,1)S(1)}) custom-call(s32[1]{0:T(128)} %bitcast.8.place, bf16[32,32,1536]{2,1,0:T(8,128)(2,1)S(1)} %all_to_all.46.got, bf16[2,1536,128]{2,1,0:T(8,128)(2,1)S(1)} %copy-done.7, bf16[2,128,1536]{2,1,0:T(8,128)(2,1)S(1)} %copy-done.1), custom_call_target="tpu_custom_call" | custom-call | tf_op jit(solution)/shard_map/pallas_call | solution.py:24
  118.0 4.0 %collective-permute-start.2 = (bf16[8,192,256]{2,1,0:T(8,128)(2,1)S(1)}, bf16[8,192,256]{2,1,0:T(8,128)(2,1)S(1)}, u32[]{:S(2)}, u32[]{:S(2)}) collective-permute-start(bf16[8,192,256]{2,1,0:T(8,128)(2,1)S(1)} %get-tuple-element.37), channel_id=1, source_target_pairs={{0,32},{32,0},{64,96},{96,64},{128,160},{160,128},{192,224},{224,1... | collective-permute-start | bytes 2359304 | tf_op jit(solution)/shard_map/ppermute | solution.py:287
  121.9 1.9 collective-permute-done.2.got
  124.0 3.5 %collective-permute-start.3 = (bf16[2,192,256]{2,1,0:T(8,128)(2,1)S(1)}, bf16[2,192,256]{2,1,0:T(8,128)(2,1)S(1)}, u32[]{:S(2)}, u32[]{:S(2)}) collective-permute-start(bf16[2,192,256]{2,1,0:T(8,128)(2,1)S(1)} %get-tuple-element.39), channel_id=1, source_target_pairs={{0,64},{32,96},{64,0},{96,32},{128,192},{160,224},{192,128},{224,1... | collective-permute-start | bytes 589832 | tf_op jit(solution)/shard_map/ppermute | solution.py:287
  127.5 4.2 %collective-permute-start.4 = (bf16[2,192,256]{2,1,0:T(8,128)(2,1)S(1)}, bf16[2,192,256]{2,1,0:T(8,128)(2,1)S(1)}, u32[]{:S(2)}, u32[]{:S(2)}) collective-permute-start(bf16[2,192,256]{2,1,0:T(8,128)(2,1)S(1)} %get-tuple-element.40), channel_id=1, source_target_pairs={{0,128},{32,160},{64,192},{96,224},{128,0},{160,32},{192,64},{224,... | collective-permute-start | bytes 589832 | tf_op jit(solution)/shard_map/ppermute | solution.py:287
  131.7 1.9 collective-permute-start.5
  133.6 11.0 %collective-permute-done.4.second = bf16[2,192,256]{2,1,0:T(8,128)(2,1)S(1)} collective-permute-done((bf16[2,192,256]{2,1,0:T(8,128)(2,1)S(1)}, bf16[2,192,256]{2,1,0:T(8,128)(2,1)S(1)}, u32[]{:S(2)}, u32[]{:S(2)}) %collective-permute-start.4) | collective-permute-done | bytes 196640 | tf_op jit(solution)/shard_map/ppermute | solution.py:287
  144.8 0.7 copy-done.17
  145.4 0.6 copy-done.21
  146.1 3.9 %all-to-all-done.1 = bf16[32,16,1536]{2,1,0:T(8,128)(2,1)} async-done(((bf16[32,16,1536]{2,1,0:T(8,128)(2,1)}), bf16[32,16,1536]{2,1,0:T(8,128)(2,1)}, u32[]{:S(2)}, u32[]{:S(2)}) %all-to-all-start.1) | async-done | bytes 1572896 | tf_op jit(solution)/shard_map/all_to_all | solution.py:293
  150.0 9.0 %shard_map.141 = (f32[192,1536]{1,0:T(8,128)S(1)}, f32[2,16,1536]{2,1,0:T(8,128)S(1)}, bf16[256,1536]{1,0:T(8,128)(2,1)}, bf16[256,1536]{1,0:T(8,128)(2,1)S(1)}) custom-call(s32[96]{0:T(128)S(1)} %pad_add_fusion.numbers, bf16[512,1536]{1,0:T(8,128)(2,1)} %bitcast.7.back, bf16[192,1536]{1,0:T(8,128)(2,1)S(1)} %bitcast.37, f32[192,1536]{1,0:T(8,128)S(1)} %copy-done.5, ...), custom_call_target="tpu_custom_call" | custom-call | tf_op jit(solution)/shard_map/pallas_call | solution.py:24
  159.0 1.0 copy-done.12
  160.0 0.9 copy-done.14
  160.9 0.7 copy-done.19
  161.6 7.6 %all-to-all-start.2 = ((bf16[32,8,1536]{2,1,0:T(8,128)(2,1)}), bf16[32,8,1536]{2,1,0:T(8,128)(2,1)S(1)}, u32[]{:S(2)}, u32[]{:S(2)}) async-start(bf16[32,8,1536]{2,1,0:T(8,128)(2,1)} %bitcast.38), calls=%async_computation.2 | async-start | bytes 1572864 | tf_op jit(solution)/shard_map/all_to_all | solution.py:293
  169.2 7.5 %collective-permute-start.6 = (bf16[192,256]{1,0:T(8,128)(2,1)S(1)}, bf16[192,256]{1,0:T(8,128)(2,1)S(1)}, u32[]{:S(2)}, u32[]{:S(2)}) collective-permute-start(bf16[192,256]{1,0:T(8,128)(2,1)S(1)} %copy-done.22), channel_id=1, source_target_pairs={{0,256},{32,288},{64,320},{96,352},{128,384},{160,416},{192,448},{... | collective-permute-start | bytes 294920 | tf_op jit(solution)/shard_map/ppermute | solution.py:287
  176.7 3.3 %collective-permute-start.7 = (f32[16,1536]{1,0:T(8,128)S(1)}, f32[16,1536]{1,0:T(8,128)S(1)}, u32[]{:S(2)}, u32[]{:S(2)}) collective-permute-start(f32[16,1536]{1,0:T(8,128)S(1)} %get-tuple-element.67), channel_id=1, source_target_pairs={{0,1},{1,2},{2,3},{3,4},{4,5},{5,6},{6,7},{7,8},{8,9},{9,10},{10,1... | collective-permute-start | bytes 294920 | tf_op jit(solution)/shard_map/ppermute | solution.py:279
  180.0 1.3 collective-permute-start.8
  181.3 0.7 shard_map.142
  182.0 2.5 %collective-permute-done.7.left = f32[16,1536]{1,0:T(8,128)S(1)} collective-permute-done((f32[16,1536]{1,0:T(8,128)S(1)}, f32[16,1536]{1,0:T(8,128)S(1)}, u32[]{:S(2)}, u32[]{:S(2)}) %collective-permute-start.7) | collective-permute-done | bytes 98336 | tf_op jit(solution)/shard_map/ppermute | solution.py:279
  184.5 5.0 %collective-permute-done.8.right = f32[16,1536]{1,0:T(8,128)S(1)} collective-permute-done((f32[16,1536]{1,0:T(8,128)S(1)}, f32[16,1536]{1,0:T(8,128)S(1)}, u32[]{:S(2)}, u32[]{:S(2)}) %collective-permute-start.8) | collective-permute-done | bytes 98336 | tf_op jit(solution)/shard_map/ppermute | solution.py:280
  189.5 8.6 %all-to-all-start.3 = ((bf16[32,8,1536]{2,1,0:T(8,128)(2,1)}), bf16[32,8,1536]{2,1,0:T(8,128)(2,1)S(1)}, u32[]{:S(2)}, u32[]{:S(2)}) async-start(bf16[32,8,1536]{2,1,0:T(8,128)(2,1)} %bitcast.14), calls=%async_computation.3 | async-start | bytes 1572864 | tf_op jit(solution)/shard_map/all_to_all | solution.py:293
  198.2 0.2 shard_map.143
  198.4 20.0 %all-gather = f32[16,1,1536]{2,1,0:T(1,128)S(1)} all-gather(f32[1,1,1536]{2,1,0:T(1,128)S(1)} %slice_bitcast_fusion.4), channel_id=1, replica_groups=mesh['dp'=16,'ctx'=32] {'dp'}, dimensions={0}, use_global_device_ids=true | all-gather | bytes 104448 | tf_op jit(solution)/shard_map/all_gather | solution.py:365
  218.4 1.3 copy-done.13
  219.7 4.4 %shard_map.144 = bf16[192,1536]{1,0:T(8,128)(2,1)} custom-call(f32[16,1536]{1,0:T(8,128)S(1)} %collective-permute-done.7.left, f32[192,1536]{1,0:T(8,128)S(1)} %copy-done.13, f32[16,1536]{1,0:T(8,128)S(1)} %collective-permute-done.8.right, f32[31,1536]{1,0:T(8,128)S(1)} %copy-done.16), custom_call_target="tpu_custom_call" | custom-call | tf_op jit(solution)/shard_map/pallas_call | solution.py:24
  224.1 0.8 broadcast_in_dim.15
  224.9 9.5 %all-to-all-start.4 = ((f32[32,1,1536]{2,1,0:T(1,128)}), f32[32,1,1536]{2,1,0:T(1,128)S(1)}, u32[]{:S(2)}, u32[]{:S(2)}) async-start(f32[32,1,1536]{2,1,0:T(1,128)} %broadcast_in_dim.15), calls=%async_computation.4 | async-start | bytes 393216 | tf_op jit(solution)/shard_map/all_to_all | solution.py:293
  234.4 2.4 shard_map.145
  236.8 7.0 %all-to-all-done.4 = f32[32,1,1536]{2,1,0:T(1,128)S(1)} async-done(((f32[32,1,1536]{2,1,0:T(1,128)}), f32[32,1,1536]{2,1,0:T(1,128)S(1)}, u32[]{:S(2)}, u32[]{:S(2)}) %all-to-all-start.4) | async-done | bytes 196640 | tf_op jit(solution)/shard_map/all_to_all | solution.py:293
  243.8 0.7 copy.19
  244.5 0.6 slice_reduce_fusion
  (48 shorter events, 0.4 us)
Async XLA Ops:
  1.5 7.6 %collective-permute-start = (bf16[16,1536]{1,0:T(8,128)(2,1)S(1)}, bf16[16,1536]{1,0:T(8,128)(2,1)S(1)}, u32[]{:S(2)}, u32[]{:S(2)}) collective-permute-start(bf16[16,1536]{1,0:T(8,128)(2,1)S(1)} %get-tuple-element.65), channel_id=1, source_target_pairs={{0,1},{1,2},{2,3},{3,4},{4,5},{5,6},{6,7},{7,8},{8,9},{9,10},{10,1... | collective-permute-start | bytes 147464 | tf_op jit(solution)/shard_map/ppermute | solution.py:279
  6.3 5.5 %collective-permute-start.1 = (bf16[16,1536]{1,0:T(8,128)(2,1)S(1)}, bf16[16,1536]{1,0:T(8,128)(2,1)S(1)}, u32[]{:S(2)}, u32[]{:S(2)}) collective-permute-start(bf16[16,1536]{1,0:T(8,128)(2,1)S(1)} %get-tuple-element.64), channel_id=1, source_target_pairs={{1,0},{2,1},{3,2},{4,3},{5,4},{6,5},{7,6},{8,7},{9,8},{10,9},{11,1... | collective-permute-start | bytes 147464 | tf_op jit(solution)/shard_map/ppermute | solution.py:280
  11.8 1.1 copy-start.8
  12.8 1.1 copy-start.10
  13.9 0.9 copy-start.15
  20.5 81.7 %copy-start.4 = (f32[192,1536]{1,0:T(8,128)}, f32[192,1536]{1,0:T(8,128)S(1)}, u32[]{:S(2)}) copy-start(f32[192,1536]{1,0:T(8,128)S(1)} %get-tuple-element.45.summed) | copy-start | bytes 3538948
  20.6 81.7 %copy-start = (bf16[2,128,1536]{2,1,0:T(8,128)(2,1)S(1)}, bf16[2,128,1536]{2,1,0:T(8,128)(2,1)}, u32[]{:S(2)}) copy-start(bf16[2,128,1536]{2,1,0:T(8,128)(2,1)} %up.3) | copy-start | bytes 2359300
  20.6 81.7 %copy-start.6 = (bf16[2,1536,128]{2,1,0:T(8,128)(2,1)S(1)}, bf16[2,1536,128]{2,1,0:T(8,128)(2,1)}, u32[]{:S(2)}) copy-start(bf16[2,1536,128]{2,1,0:T(8,128)(2,1)} %down_w.1) | copy-start | bytes 2359300
  103.7 1.2 copy-start.3
  104.9 45.1 %all-to-all-start.1 = ((bf16[32,16,1536]{2,1,0:T(8,128)(2,1)}), bf16[32,16,1536]{2,1,0:T(8,128)(2,1)}, u32[]{:S(2)}, u32[]{:S(2)}) async-start(bf16[32,16,1536]{2,1,0:T(8,128)(2,1)} %bitcast.32), calls=%async_computation.1 | async-start | bytes 3145728 | tf_op jit(solution)/shard_map/all_to_all | solution.py:293
  113.2 1.1 copy-start.1
  114.4 1.1 copy-start.7
  118.0 5.9 %collective-permute-start.2 = (bf16[8,192,256]{2,1,0:T(8,128)(2,1)S(1)}, bf16[8,192,256]{2,1,0:T(8,128)(2,1)S(1)}, u32[]{:S(2)}, u32[]{:S(2)}) collective-permute-start(bf16[8,192,256]{2,1,0:T(8,128)(2,1)S(1)} %get-tuple-element.37), channel_id=1, source_target_pairs={{0,32},{32,0},{64,96},{96,64},{128,160},{160,128},{192,224},{224,1... | collective-permute-start | bytes 2359304 | tf_op jit(solution)/shard_map/ppermute | solution.py:287
  123.8 26.1 %copy-start.2 = (bf16[2,128,1536]{2,1,0:T(8,128)(2,1)S(1)}, bf16[2,128,1536]{2,1,0:T(8,128)(2,1)}, u32[]{:S(2)}) copy-start(bf16[2,128,1536]{2,1,0:T(8,128)(2,1)} %up.3) | copy-start | bytes 2359300
  123.8 26.1 %copy-start.5 = (f32[192,1536]{1,0:T(8,128)S(1)}, f32[192,1536]{1,0:T(8,128)}, u32[]{:S(2)}) copy-start(f32[192,1536]{1,0:T(8,128)} %copy-done.4) | copy-start | bytes 3538948
  123.8 26.1 %copy-start.9 = (bf16[1,192,1536]{2,1,0:T(8,128)(2,1)S(1)}, bf16[1,192,1536]{2,1,0:T(8,128)(2,1)}, u32[]{:S(2)}) copy-start(bf16[1,192,1536]{2,1,0:T(8,128)(2,1)} %param.9) | copy-start | bytes 1769476
  123.8 26.1 %copy-start.11 = (bf16[1,192,1536]{2,1,0:T(8,128)(2,1)S(1)}, bf16[1,192,1536]{2,1,0:T(8,128)(2,1)}, u32[]{:S(2)}) copy-start(bf16[1,192,1536]{2,1,0:T(8,128)(2,1)} %param.10) | copy-start | bytes 1769476
  124.0 9.6 %collective-permute-start.3 = (bf16[2,192,256]{2,1,0:T(8,128)(2,1)S(1)}, bf16[2,192,256]{2,1,0:T(8,128)(2,1)S(1)}, u32[]{:S(2)}, u32[]{:S(2)}) collective-permute-start(bf16[2,192,256]{2,1,0:T(8,128)(2,1)S(1)} %get-tuple-element.39), channel_id=1, source_target_pairs={{0,64},{32,96},{64,0},{96,32},{128,192},{160,224},{192,128},{224,1... | collective-permute-start | bytes 589832 | tf_op jit(solution)/shard_map/ppermute | solution.py:287
  127.5 17.2 %collective-permute-start.4 = (bf16[2,192,256]{2,1,0:T(8,128)(2,1)S(1)}, bf16[2,192,256]{2,1,0:T(8,128)(2,1)S(1)}, u32[]{:S(2)}, u32[]{:S(2)}) collective-permute-start(bf16[2,192,256]{2,1,0:T(8,128)(2,1)S(1)} %get-tuple-element.40), channel_id=1, source_target_pairs={{0,128},{32,160},{64,192},{96,224},{128,0},{160,32},{192,64},{224,... | collective-permute-start | bytes 589832 | tf_op jit(solution)/shard_map/ppermute | solution.py:287
  131.7 13.0 %collective-permute-start.5 = (bf16[2,192,256]{2,1,0:T(8,128)(2,1)S(1)}, bf16[2,192,256]{2,1,0:T(8,128)(2,1)S(1)}, u32[]{:S(2)}, u32[]{:S(2)}) collective-permute-start(bf16[2,192,256]{2,1,0:T(8,128)(2,1)S(1)} %get-tuple-element.41), channel_id=1, source_target_pairs={{0,192},{32,224},{64,128},{96,160},{128,64},{160,96},{192,0},{224,... | collective-permute-start | bytes 589832 | tf_op jit(solution)/shard_map/ppermute | solution.py:287
  144.7 0.7 copy-start.17
  145.4 0.6 copy-start.21
  159.0 1.0 copy-start.12
  160.0 0.9 copy-start.14
  160.9 0.7 copy-start.19
  161.6 7.6 %copy-start.22 = (bf16[192,256]{1,0:T(8,128)(2,1)S(1)}, bf16[192,256]{1,0:T(8,128)(2,1)}, u32[]{:S(2)}) copy-start(bf16[192,256]{1,0:T(8,128)(2,1)} %copy-done.21) | copy-start | bytes 294916
  161.6 19.7 %copy-start.18 = (f32[192,256]{1,0:T(8,128)S(1)}, f32[192,256]{1,0:T(8,128)}, u32[]{:S(2)}) copy-start(f32[192,256]{1,0:T(8,128)} %copy-done.17) | copy-start | bytes 589828
  161.6 15.1 %copy-start.20 = (f32[2,16,1536]{2,1,0:T(8,128)S(1)}, f32[2,16,1536]{2,1,0:T(8,128)}, u32[]{:S(2)}) copy-start(f32[2,16,1536]{2,1,0:T(8,128)} %copy-done.19) | copy-start | bytes 589828
  161.6 27.9 %all-to-all-start.2 = ((bf16[32,8,1536]{2,1,0:T(8,128)(2,1)}), bf16[32,8,1536]{2,1,0:T(8,128)(2,1)S(1)}, u32[]{:S(2)}, u32[]{:S(2)}) async-start(bf16[32,8,1536]{2,1,0:T(8,128)(2,1)} %bitcast.38), calls=%async_computation.2 | async-start | bytes 1572864 | tf_op jit(solution)/shard_map/all_to_all | solution.py:293
  169.2 12.1 %collective-permute-start.6 = (bf16[192,256]{1,0:T(8,128)(2,1)S(1)}, bf16[192,256]{1,0:T(8,128)(2,1)S(1)}, u32[]{:S(2)}, u32[]{:S(2)}) collective-permute-start(bf16[192,256]{1,0:T(8,128)(2,1)S(1)} %copy-done.22), channel_id=1, source_target_pairs={{0,256},{32,288},{64,320},{96,352},{128,384},{160,416},{192,448},{... | collective-permute-start | bytes 294920 | tf_op jit(solution)/shard_map/ppermute | solution.py:287
  176.7 41.7 %copy-start.16 = (f32[31,1536]{1,0:T(8,128)S(1)}, f32[31,1536]{1,0:T(8,128)}, u32[]{:S(2)}) copy-start(f32[31,1536]{1,0:T(8,128)} %taps.3) | copy-start | bytes 571396
  176.7 7.8 %collective-permute-start.7 = (f32[16,1536]{1,0:T(8,128)S(1)}, f32[16,1536]{1,0:T(8,128)S(1)}, u32[]{:S(2)}, u32[]{:S(2)}) collective-permute-start(f32[16,1536]{1,0:T(8,128)S(1)} %get-tuple-element.67), channel_id=1, source_target_pairs={{0,1},{1,2},{2,3},{3,4},{4,5},{5,6},{6,7},{7,8},{8,9},{9,10},{10,1... | collective-permute-start | bytes 294920 | tf_op jit(solution)/shard_map/ppermute | solution.py:279
  180.0 9.5 %collective-permute-start.8 = (f32[16,1536]{1,0:T(8,128)S(1)}, f32[16,1536]{1,0:T(8,128)S(1)}, u32[]{:S(2)}, u32[]{:S(2)}) collective-permute-start(f32[16,1536]{1,0:T(8,128)S(1)} %get-tuple-element.66), channel_id=1, source_target_pairs={{1,0},{2,1},{3,2},{4,3},{5,4},{6,5},{7,6},{8,7},{9,8},{10,9},{11,1... | collective-permute-start | bytes 294920 | tf_op jit(solution)/shard_map/ppermute | solution.py:280
  189.5 34.5 %all-to-all-start.3 = ((bf16[32,8,1536]{2,1,0:T(8,128)(2,1)}), bf16[32,8,1536]{2,1,0:T(8,128)(2,1)S(1)}, u32[]{:S(2)}, u32[]{:S(2)}) async-start(bf16[32,8,1536]{2,1,0:T(8,128)(2,1)} %bitcast.14), calls=%async_computation.3 | async-start | bytes 1572864 | tf_op jit(solution)/shard_map/all_to_all | solution.py:293
  218.4 1.3 copy-start.13
  224.9 18.9 %all-to-all-start.4 = ((f32[32,1,1536]{2,1,0:T(1,128)}), f32[32,1,1536]{2,1,0:T(1,128)S(1)}, u32[]{:S(2)}, u32[]{:S(2)}) async-start(f32[32,1,1536]{2,1,0:T(1,128)} %broadcast_in_dim.15), calls=%async_computation.4 | async-start | bytes 393216 | tf_op jit(solution)/shard_map/all_to_all | solution.py:293

commit v6 on v5

--- a/solution.py
+++ b/solution.py
@@ -173,7 +173,7 @@
 
 
 def sum_gradients(
-    numbers, back, cot, summed, gain, left, own, right, act, up, total, edges, low, high, sums, cells, frames_grad, inv
+    numbers, back, cot, summed, gain, left, own, right, act, up, total, low, high, sums, cells, frames_grad, inv
 ):
     frames, width = cot.shape
     gather = gather_matrix(segments(numbers), back.shape[0], frames)
@@ -213,8 +213,6 @@
         return carry
 
     lax.fori_loop(0, width // LANES, column, 0)
-    edges[0] = total[:EDGE]
-    edges[1] = total[frames - EDGE :]
     both_up = up[...].reshape(act.shape[1], width)
     count, blocks = act.shape[0], sums.shape[0]
     row = lax.broadcasted_iota(jnp.int32, (count, blocks), 0)
@@ -343,9 +341,9 @@
         pair_grads, [(piece, F32), (piece, BF16)], [place, ("v", chips[0])] + [("v", part) for part in got]
     )
     grad_back, kept, given = lax.optimization_barrier((grad_back, kept, given))
-    total, edges, low, high = call(
+    total, low, high = call(
         sum_gradients,
-        [((frames, width), F32), ((2, EDGE, width), F32), ((rows // 2, width), BF16), ((rows // 2, width), BF16)],
+        [((frames, width), F32), ((rows // 2, width), BF16), ((rows // 2, width), BF16)],
         where
         + [("v", grad_back), ("v", cot), ("v", summed), ("v", gain)]
         + [("v", left), ("v", own), ("v", right), ("v", act), ("v", adapt_up)],
@@ -356,7 +354,7 @@
     grad_down, grad_up = call(
         functools.partial(place_grads, grad_scale), [((2, share, units), F32)] * 2, [("v", kept), ("v", got)]
     )
-    grad_left, grad_right = from_sides(edges[0], edges[1], "ctx")
+    grad_left, grad_right = from_sides(total[:EDGE], total[frames - EDGE :], "ctx")
     high_back, low, grad_down, grad_up, grad_left, grad_right = lax.optimization_barrier(
         (high_back, low, grad_down, grad_up, grad_left, grad_right)
     )
@@ -369,7 +367,7 @@
         [("v", grad_left), ("v", total), ("v", grad_right), ("v", conv_kernel)],
         [((frames + 2 * EDGE, width), F32)],
     )
-    mine, low_back, grad_input = lax.optimization_barrier((mine, low_back, grad_input))
+    mine, low_back = lax.optimization_barrier((mine, low_back))
     mine = jnp.sum(mine, axis=0, keepdims=True) * grad_scale
     reduced = spread_rows(mine, "ctx").reshape(ctx, width)
     (output,) = call(

time: 247 us -> 240 us (0.972)
  waiting for transfers between devices: 34.1 us -> 27.7 us
    all_to_all x4, waiting for transfers between devices: 10.9 us -> 5.36 us  [swap(): return lax.all_to_all(cells, axis, split_axis=0, concat_axis=0, tiled=True)]
    unnamed x49 -> x45, local copies, waits for them, and re-layouts: 12.4 us -> 11.7 us
where the time goes in v6:
time: 240 us; the launch traced here: 239 us
  blocking collectives  102 us (42%)
  starting transfers between devices  65.5 us (27%)
  waiting for transfers between devices  27.7 us (12%)
  Pallas kernels  26.5 us (11%)
  local copies, waits for them, and re-layouts  15.6 us (6%)
    all_to_all x1, blocking collectives, swap(): return lax.all_to_all(cells, axis, split_axis=0, concat_axis=0, tiled=True)  81.7 us
    all_to_all x4, starting transfers between devices, swap(): return lax.all_to_all(cells, axis, split_axis=0, concat_axis=0, tiled=True)  34 us
    pallas_call x10, Pallas kernels, call(): pl.pallas_call(body, out_shape=tuple((jax.ShapeDtypeStruct(shape, kind) f...  26.5 us
    ppermute x5, starting transfers between devices, exchanged(): lax.ppermute(block, axis, [(i, i ^ turn * unit) for i in range(count)])  20.9 us
    all_gather x1, blocking collectives, local(): mine = lax.all_gather(mine[:1], 'dp', axis=0, tiled=True)  19.9 us
    ppermute x5, waiting for transfers between devices, exchanged(): lax.ppermute(block, axis, [(i, i ^ turn * unit) for i in range(count)])  12.9 us
    unnamed x45, local copies, waits for them, and re-layouts  11.7 us
    ppermute x2, starting transfers between devices, from_sides(): left = lax.ppermute(tail, axis, [(i, i + 1) for i in range(count - 1)])  7.95 us
  transfers between devices with their start and end apart: 13, of which 7 were waited for; matrix products, arithmetic and copies ran while one was open for 1% of the time, Pallas kernels for 4%

profile of v6, /device:TPU:1, one launch (start us, length us, event | category | flops | bytes accessed | tf_op | source)
XLA Modules:
  0.0 238.7 jit_solution(55519094405663655)
XLA Ops:
  0.6 0.8 slice_bitcast_fusion
  1.5 4.8 %collective-permute-start = (bf16[16,1536]{1,0:T(8,128)(2,1)S(1)}, bf16[16,1536]{1,0:T(8,128)(2,1)S(1)}, u32[]{:S(2)}, u32[]{:S(2)}) collective-permute-start(bf16[16,1536]{1,0:T(8,128)(2,1)S(1)} %get-tuple-element.63), channel_id=1, source_target_pairs={{0,1},{1,2},{2,3},{3,4},{4,5},{5,6},{6,7},{7,8},{8,9},{9,10},{10,1... | collective-permute-start | bytes 147464 | tf_op jit(solution)/shard_map/ppermute | solution.py:277
  6.3 1.3 collective-permute-start.1
  7.6 0.8 pad_add_fusion.numbers
  8.4 0.7 reshape.45.gain
  9.1 2.7 %collective-permute-done.1.right = bf16[16,1536]{1,0:T(8,128)(2,1)S(1)} collective-permute-done((bf16[16,1536]{1,0:T(8,128)(2,1)S(1)}, bf16[16,1536]{1,0:T(8,128)(2,1)S(1)}, u32[]{:S(2)}, u32[]{:S(2)}) %collective-permute-start.1) | collective-permute-done | bytes 49184 | tf_op jit(solution)/shard_map/ppermute | solution.py:278
  11.8 1.1 copy-done.8
  12.8 1.1 copy-done.10
  13.9 0.9 copy-done.15
  14.8 5.7 %shard_map.136 = (bf16[32,32,1536]{2,1,0:T(8,128)(2,1)S(1)}, f32[192,1536]{1,0:T(8,128)S(1)}) custom-call(s32[96]{0:T(128)S(1)} %pad_add_fusion.numbers, bf16[16,1536]{1,0:T(8,128)(2,1)S(1)} %collective-permute-done.left, bf16[192,1536]{1,0:T(8,128)(2,1)S(1)} %bitcast.30, bf16[16,1536]{1,0:T(8,128)(2,1)S(1)} %collective-permute-done.1.right, ...), custom_call_target="tpu_custom_call" | custom-call | tf_op jit(solution)/shard_map/pallas_call | solution.py:24
  20.6 81.7 %all_to_all.46.got = bf16[32,32,1536]{2,1,0:T(8,128)(2,1)S(1)} all-to-all(bf16[32,32,1536]{2,1,0:T(8,128)(2,1)S(1)} %get-tuple-element.33), channel_id=1, replica_groups=mesh['dp'=16,'ctx'=32] {'ctx'}, dimensions={0} | all-to-all | bytes 6291456 | tf_op jit(solution)/shard_map/all_to_all | solution.py:291
  102.3 1.4 shard_map.137
  103.7 1.1 copy-done.3
  104.8 8.3 %all-to-all-start.1 = ((bf16[32,16,1536]{2,1,0:T(8,128)(2,1)}), bf16[32,16,1536]{2,1,0:T(8,128)(2,1)}, u32[]{:S(2)}, u32[]{:S(2)}) async-start(bf16[32,16,1536]{2,1,0:T(8,128)(2,1)} %bitcast.28), calls=%async_computation.1 | async-start | bytes 3145728 | tf_op jit(solution)/shard_map/all_to_all | solution.py:291
  113.2 1.1 copy-done.1
  114.3 1.1 copy-done.7
  115.5 2.5 %shard_map.138 = (f32[8,192,256]{2,1,0:T(8,128)S(1)}, bf16[8,192,256]{2,1,0:T(8,128)(2,1)S(1)}, bf16[512,256]{1,0:T(8,128)(2,1)S(1)}) custom-call(s32[1]{0:T(128)} %bitcast.8.place, bf16[32,32,1536]{2,1,0:T(8,128)(2,1)S(1)} %all_to_all.46.got, bf16[2,1536,128]{2,1,0:T(8,128)(2,1)S(1)} %copy-done.7, bf16[2,128,1536]{2,1,0:T(8,128)(2,1)S(1)} %copy-done.1), custom_call_target="tpu_custom_call" | custom-call | tf_op jit(solution)/shard_map/pallas_call | solution.py:24
  117.9 4.0 %collective-permute-start.2 = (bf16[8,192,256]{2,1,0:T(8,128)(2,1)S(1)}, bf16[8,192,256]{2,1,0:T(8,128)(2,1)S(1)}, u32[]{:S(2)}, u32[]{:S(2)}) collective-permute-start(bf16[8,192,256]{2,1,0:T(8,128)(2,1)S(1)} %get-tuple-element.35), channel_id=1, source_target_pairs={{0,32},{32,0},{64,96},{96,64},{128,160},{160,128},{192,224},{224,1... | collective-permute-start | bytes 2359304 | tf_op jit(solution)/shard_map/ppermute | solution.py:285
  121.9 1.9 collective-permute-done.2.got
  124.0 3.3 %collective-permute-start.3 = (bf16[2,192,256]{2,1,0:T(8,128)(2,1)S(1)}, bf16[2,192,256]{2,1,0:T(8,128)(2,1)S(1)}, u32[]{:S(2)}, u32[]{:S(2)}) collective-permute-start(bf16[2,192,256]{2,1,0:T(8,128)(2,1)S(1)} %get-tuple-element.37), channel_id=1, source_target_pairs={{0,64},{32,96},{64,0},{96,32},{128,192},{160,224},{192,128},{224,1... | collective-permute-start | bytes 589832 | tf_op jit(solution)/shard_map/ppermute | solution.py:285
  127.3 4.2 %collective-permute-start.4 = (bf16[2,192,256]{2,1,0:T(8,128)(2,1)S(1)}, bf16[2,192,256]{2,1,0:T(8,128)(2,1)S(1)}, u32[]{:S(2)}, u32[]{:S(2)}) collective-permute-start(bf16[2,192,256]{2,1,0:T(8,128)(2,1)S(1)} %get-tuple-element.38), channel_id=1, source_target_pairs={{0,128},{32,160},{64,192},{96,224},{128,0},{160,32},{192,64},{224,... | collective-permute-start | bytes 589832 | tf_op jit(solution)/shard_map/ppermute | solution.py:285
  131.6 1.9 collective-permute-start.5
  133.5 11.0 %collective-permute-done.4.second = bf16[2,192,256]{2,1,0:T(8,128)(2,1)S(1)} collective-permute-done((bf16[2,192,256]{2,1,0:T(8,128)(2,1)S(1)}, bf16[2,192,256]{2,1,0:T(8,128)(2,1)S(1)}, u32[]{:S(2)}, u32[]{:S(2)}) %collective-permute-start.4) | collective-permute-done | bytes 196640 | tf_op jit(solution)/shard_map/ppermute | solution.py:285
  144.6 0.7 copy-done.17
  145.3 0.6 copy-done.19
  146.0 4.0 %all-to-all-done.1 = bf16[32,16,1536]{2,1,0:T(8,128)(2,1)} async-done(((bf16[32,16,1536]{2,1,0:T(8,128)(2,1)}), bf16[32,16,1536]{2,1,0:T(8,128)(2,1)}, u32[]{:S(2)}, u32[]{:S(2)}) %all-to-all-start.1) | async-done | bytes 1572896 | tf_op jit(solution)/shard_map/all_to_all | solution.py:291
  150.0 9.0 %shard_map.141 = (f32[192,1536]{1,0:T(8,128)S(1)}, bf16[256,1536]{1,0:T(8,128)(2,1)}, bf16[256,1536]{1,0:T(8,128)(2,1)S(1)}) custom-call(s32[96]{0:T(128)S(1)} %pad_add_fusion.numbers, bf16[512,1536]{1,0:T(8,128)(2,1)} %bitcast.7.back, bf16[192,1536]{1,0:T(8,128)(2,1)S(1)} %bitcast.33, f32[192,1536]{1,0:T(8,128)S(1)} %copy-done.5, ...), custom_call_target="tpu_custom_call" | custom-call | tf_op jit(solution)/shard_map/pallas_call | solution.py:24
  159.0 1.0 copy-done.12
  160.0 0.9 copy-done.14
  160.9 7.4 %all-to-all-start.2 = ((bf16[32,8,1536]{2,1,0:T(8,128)(2,1)}), bf16[32,8,1536]{2,1,0:T(8,128)(2,1)S(1)}, u32[]{:S(2)}, u32[]{:S(2)}) async-start(bf16[32,8,1536]{2,1,0:T(8,128)(2,1)} %bitcast.34), calls=%async_computation.2 | async-start | bytes 1572864 | tf_op jit(solution)/shard_map/all_to_all | solution.py:291
  168.4 7.5 %collective-permute-start.6 = (bf16[192,256]{1,0:T(8,128)(2,1)S(1)}, bf16[192,256]{1,0:T(8,128)(2,1)S(1)}, u32[]{:S(2)}, u32[]{:S(2)}) collective-permute-start(bf16[192,256]{1,0:T(8,128)(2,1)S(1)} %copy-done.20), channel_id=1, source_target_pairs={{0,256},{32,288},{64,320},{96,352},{128,384},{160,416},{192,448},{... | collective-permute-start | bytes 294920 | tf_op jit(solution)/shard_map/ppermute | solution.py:285
  175.8 1.0 fusion
  176.8 3.1 %collective-permute-start.7 = (f32[16,1536]{1,0:T(8,128)S(1)}, f32[16,1536]{1,0:T(8,128)S(1)}, u32[]{:S(2)}, u32[]{:S(2)}) collective-permute-start(f32[16,1536]{1,0:T(8,128)S(1)} %get-tuple-element.61), channel_id=1, source_target_pairs={{0,1},{1,2},{2,3},{3,4},{4,5},{5,6},{6,7},{7,8},{8,9},{9,10},{10,1... | collective-permute-start | bytes 294920 | tf_op jit(solution)/shard_map/ppermute | solution.py:277
  179.9 1.3 collective-permute-start.8
  181.3 0.7 shard_map.142
  182.0 2.1 collective-permute-done.7.left
  184.1 4.6 %collective-permute-done.8.right = f32[16,1536]{1,0:T(8,128)S(1)} collective-permute-done((f32[16,1536]{1,0:T(8,128)S(1)}, f32[16,1536]{1,0:T(8,128)S(1)}, u32[]{:S(2)}, u32[]{:S(2)}) %collective-permute-start.8) | collective-permute-done | bytes 98336 | tf_op jit(solution)/shard_map/ppermute | solution.py:278
  188.7 8.8 %all-to-all-start.3 = ((bf16[32,8,1536]{2,1,0:T(8,128)(2,1)}), bf16[32,8,1536]{2,1,0:T(8,128)(2,1)S(1)}, u32[]{:S(2)}, u32[]{:S(2)}) async-start(bf16[32,8,1536]{2,1,0:T(8,128)(2,1)} %bitcast.12), calls=%async_computation.3 | async-start | bytes 1572864 | tf_op jit(solution)/shard_map/all_to_all | solution.py:291
  197.5 0.2 shard_map.143
  197.7 19.9 %all-gather = f32[16,1,1536]{2,1,0:T(1,128)S(1)} all-gather(f32[1,1,1536]{2,1,0:T(1,128)S(1)} %slice_bitcast_fusion.2), channel_id=1, replica_groups=mesh['dp'=16,'ctx'=32] {'dp'}, dimensions={0}, use_global_device_ids=true | all-gather | bytes 104448 | tf_op jit(solution)/shard_map/all_gather | solution.py:363
  217.6 0.8 broadcast_in_dim.15
  218.4 9.5 %all-to-all-start.4 = ((f32[32,1,1536]{2,1,0:T(1,128)}), f32[32,1,1536]{2,1,0:T(1,128)S(1)}, u32[]{:S(2)}, u32[]{:S(2)}) async-start(f32[32,1,1536]{2,1,0:T(1,128)} %broadcast_in_dim.15), calls=%async_computation.4 | async-start | bytes 393216 | tf_op jit(solution)/shard_map/all_to_all | solution.py:291
  228.0 1.3 copy-done.13
  229.2 4.4 %shard_map.145 = bf16[192,1536]{1,0:T(8,128)(2,1)} custom-call(f32[16,1536]{1,0:T(8,128)S(1)} %collective-permute-done.7.left, f32[192,1536]{1,0:T(8,128)S(1)} %copy-done.13, f32[16,1536]{1,0:T(8,128)S(1)} %collective-permute-done.8.right, f32[31,1536]{1,0:T(8,128)S(1)} %copy-done.16), custom_call_target="tpu_custom_call" | custom-call | tf_op jit(solution)/shard_map/pallas_call | solution.py:24
  233.6 2.4 shard_map.144
  236.0 1.4 all-to-all-done.4
  237.4 0.7 copy.19
  238.1 0.6 slice_reduce_fusion
  (44 shorter events, 0.4 us)
Async XLA Ops:
  1.5 7.6 %collective-permute-start = (bf16[16,1536]{1,0:T(8,128)(2,1)S(1)}, bf16[16,1536]{1,0:T(8,128)(2,1)S(1)}, u32[]{:S(2)}, u32[]{:S(2)}) collective-permute-start(bf16[16,1536]{1,0:T(8,128)(2,1)S(1)} %get-tuple-element.63), channel_id=1, source_target_pairs={{0,1},{1,2},{2,3},{3,4},{4,5},{5,6},{6,7},{7,8},{8,9},{9,10},{10,1... | collective-permute-start | bytes 147464 | tf_op jit(solution)/shard_map/ppermute | solution.py:277
  6.3 5.5 %collective-permute-start.1 = (bf16[16,1536]{1,0:T(8,128)(2,1)S(1)}, bf16[16,1536]{1,0:T(8,128)(2,1)S(1)}, u32[]{:S(2)}, u32[]{:S(2)}) collective-permute-start(bf16[16,1536]{1,0:T(8,128)(2,1)S(1)} %get-tuple-element.62), channel_id=1, source_target_pairs={{1,0},{2,1},{3,2},{4,3},{5,4},{6,5},{7,6},{8,7},{9,8},{10,9},{11,1... | collective-permute-start | bytes 147464 | tf_op jit(solution)/shard_map/ppermute | solution.py:278
  11.8 1.1 copy-start.8
  12.8 1.1 copy-start.10
  13.9 0.9 copy-start.15
  20.5 81.7 %copy-start.4 = (f32[192,1536]{1,0:T(8,128)}, f32[192,1536]{1,0:T(8,128)S(1)}, u32[]{:S(2)}) copy-start(f32[192,1536]{1,0:T(8,128)S(1)} %get-tuple-element.43.summed) | copy-start | bytes 3538948
  20.6 81.7 %copy-start = (bf16[2,128,1536]{2,1,0:T(8,128)(2,1)S(1)}, bf16[2,128,1536]{2,1,0:T(8,128)(2,1)}, u32[]{:S(2)}) copy-start(bf16[2,128,1536]{2,1,0:T(8,128)(2,1)} %up.3) | copy-start | bytes 2359300
  20.6 81.7 %copy-start.6 = (bf16[2,1536,128]{2,1,0:T(8,128)(2,1)S(1)}, bf16[2,1536,128]{2,1,0:T(8,128)(2,1)}, u32[]{:S(2)}) copy-start(bf16[2,1536,128]{2,1,0:T(8,128)(2,1)} %down_w.1) | copy-start | bytes 2359300
  103.7 1.1 copy-start.3
  104.8 45.1 %all-to-all-start.1 = ((bf16[32,16,1536]{2,1,0:T(8,128)(2,1)}), bf16[32,16,1536]{2,1,0:T(8,128)(2,1)}, u32[]{:S(2)}, u32[]{:S(2)}) async-start(bf16[32,16,1536]{2,1,0:T(8,128)(2,1)} %bitcast.28), calls=%async_computation.1 | async-start | bytes 3145728 | tf_op jit(solution)/shard_map/all_to_all | solution.py:291
  113.2 1.1 copy-start.1
  114.3 1.1 copy-start.7
  117.9 5.9 %collective-permute-start.2 = (bf16[8,192,256]{2,1,0:T(8,128)(2,1)S(1)}, bf16[8,192,256]{2,1,0:T(8,128)(2,1)S(1)}, u32[]{:S(2)}, u32[]{:S(2)}) collective-permute-start(bf16[8,192,256]{2,1,0:T(8,128)(2,1)S(1)} %get-tuple-element.35), channel_id=1, source_target_pairs={{0,32},{32,0},{64,96},{96,64},{128,160},{160,128},{192,224},{224,1... | collective-permute-start | bytes 2359304 | tf_op jit(solution)/shard_map/ppermute | solution.py:285
  123.8 26.2 %copy-start.2 = (bf16[2,128,1536]{2,1,0:T(8,128)(2,1)S(1)}, bf16[2,128,1536]{2,1,0:T(8,128)(2,1)}, u32[]{:S(2)}) copy-start(bf16[2,128,1536]{2,1,0:T(8,128)(2,1)} %up.3) | copy-start | bytes 2359300
  123.8 26.2 %copy-start.5 = (f32[192,1536]{1,0:T(8,128)S(1)}, f32[192,1536]{1,0:T(8,128)}, u32[]{:S(2)}) copy-start(f32[192,1536]{1,0:T(8,128)} %copy-done.4) | copy-start | bytes 3538948
  123.8 26.2 %copy-start.9 = (bf16[1,192,1536]{2,1,0:T(8,128)(2,1)S(1)}, bf16[1,192,1536]{2,1,0:T(8,128)(2,1)}, u32[]{:S(2)}) copy-start(bf16[1,192,1536]{2,1,0:T(8,128)(2,1)} %param.9) | copy-start | bytes 1769476
  123.8 26.2 %copy-start.11 = (bf16[1,192,1536]{2,1,0:T(8,128)(2,1)S(1)}, bf16[1,192,1536]{2,1,0:T(8,128)(2,1)}, u32[]{:S(2)}) copy-start(bf16[1,192,1536]{2,1,0:T(8,128)(2,1)} %param.10) | copy-start | bytes 1769476
  124.0 9.5 %collective-permute-start.3 = (bf16[2,192,256]{2,1,0:T(8,128)(2,1)S(1)}, bf16[2,192,256]{2,1,0:T(8,128)(2,1)S(1)}, u32[]{:S(2)}, u32[]{:S(2)}) collective-permute-start(bf16[2,192,256]{2,1,0:T(8,128)(2,1)S(1)} %get-tuple-element.37), channel_id=1, source_target_pairs={{0,64},{32,96},{64,0},{96,32},{128,192},{160,224},{192,128},{224,1... | collective-permute-start | bytes 589832 | tf_op jit(solution)/shard_map/ppermute | solution.py:285
  127.3 17.2 %collective-permute-start.4 = (bf16[2,192,256]{2,1,0:T(8,128)(2,1)S(1)}, bf16[2,192,256]{2,1,0:T(8,128)(2,1)S(1)}, u32[]{:S(2)}, u32[]{:S(2)}) collective-permute-start(bf16[2,192,256]{2,1,0:T(8,128)(2,1)S(1)} %get-tuple-element.38), channel_id=1, source_target_pairs={{0,128},{32,160},{64,192},{96,224},{128,0},{160,32},{192,64},{224,... | collective-permute-start | bytes 589832 | tf_op jit(solution)/shard_map/ppermute | solution.py:285
  131.6 13.0 %collective-permute-start.5 = (bf16[2,192,256]{2,1,0:T(8,128)(2,1)S(1)}, bf16[2,192,256]{2,1,0:T(8,128)(2,1)S(1)}, u32[]{:S(2)}, u32[]{:S(2)}) collective-permute-start(bf16[2,192,256]{2,1,0:T(8,128)(2,1)S(1)} %get-tuple-element.39), channel_id=1, source_target_pairs={{0,192},{32,224},{64,128},{96,160},{128,64},{160,96},{192,0},{224,... | collective-permute-start | bytes 589832 | tf_op jit(solution)/shard_map/ppermute | solution.py:285
  144.6 0.7 copy-start.17
  145.3 0.6 copy-start.19
  159.0 1.0 copy-start.12
  160.0 0.9 copy-start.14
  160.0 8.4 %copy-start.20 = (bf16[192,256]{1,0:T(8,128)(2,1)S(1)}, bf16[192,256]{1,0:T(8,128)(2,1)}, u32[]{:S(2)}) copy-start(bf16[192,256]{1,0:T(8,128)(2,1)} %copy-done.19) | copy-start | bytes 294916
  160.0 21.2 %copy-start.18 = (f32[192,256]{1,0:T(8,128)S(1)}, f32[192,256]{1,0:T(8,128)}, u32[]{:S(2)}) copy-start(f32[192,256]{1,0:T(8,128)} %copy-done.17) | copy-start | bytes 589828
  160.9 27.8 %all-to-all-start.2 = ((bf16[32,8,1536]{2,1,0:T(8,128)(2,1)}), bf16[32,8,1536]{2,1,0:T(8,128)(2,1)S(1)}, u32[]{:S(2)}, u32[]{:S(2)}) async-start(bf16[32,8,1536]{2,1,0:T(8,128)(2,1)} %bitcast.34), calls=%async_computation.2 | async-start | bytes 1572864 | tf_op jit(solution)/shard_map/all_to_all | solution.py:291
  168.4 12.9 %collective-permute-start.6 = (bf16[192,256]{1,0:T(8,128)(2,1)S(1)}, bf16[192,256]{1,0:T(8,128)(2,1)S(1)}, u32[]{:S(2)}, u32[]{:S(2)}) collective-permute-start(bf16[192,256]{1,0:T(8,128)(2,1)S(1)} %copy-done.20), channel_id=1, source_target_pairs={{0,256},{32,288},{64,320},{96,352},{128,384},{160,416},{192,448},{... | collective-permute-start | bytes 294920 | tf_op jit(solution)/shard_map/ppermute | solution.py:285
  176.8 7.3 %collective-permute-start.7 = (f32[16,1536]{1,0:T(8,128)S(1)}, f32[16,1536]{1,0:T(8,128)S(1)}, u32[]{:S(2)}, u32[]{:S(2)}) collective-permute-start(f32[16,1536]{1,0:T(8,128)S(1)} %get-tuple-element.61), channel_id=1, source_target_pairs={{0,1},{1,2},{2,3},{3,4},{4,5},{5,6},{6,7},{7,8},{8,9},{9,10},{10,1... | collective-permute-start | bytes 294920 | tf_op jit(solution)/shard_map/ppermute | solution.py:277
  179.9 8.8 %collective-permute-start.8 = (f32[16,1536]{1,0:T(8,128)S(1)}, f32[16,1536]{1,0:T(8,128)S(1)}, u32[]{:S(2)}, u32[]{:S(2)}) collective-permute-start(f32[16,1536]{1,0:T(8,128)S(1)} %get-tuple-element.60), channel_id=1, source_target_pairs={{1,0},{2,1},{3,2},{4,3},{5,4},{6,5},{7,6},{8,7},{9,8},{10,9},{11,1... | collective-permute-start | bytes 294920 | tf_op jit(solution)/shard_map/ppermute | solution.py:278
  188.7 39.2 %copy-start.16 = (f32[31,1536]{1,0:T(8,128)S(1)}, f32[31,1536]{1,0:T(8,128)}, u32[]{:S(2)}) copy-start(f32[31,1536]{1,0:T(8,128)} %taps.3) | copy-start | bytes 571396
  188.7 28.9 %all-to-all-start.3 = ((bf16[32,8,1536]{2,1,0:T(8,128)(2,1)}), bf16[32,8,1536]{2,1,0:T(8,128)(2,1)S(1)}, u32[]{:S(2)}, u32[]{:S(2)}) async-start(bf16[32,8,1536]{2,1,0:T(8,128)(2,1)} %bitcast.12), calls=%async_computation.3 | async-start | bytes 1572864 | tf_op jit(solution)/shard_map/all_to_all | solution.py:291
  218.4 18.9 %all-to-all-start.4 = ((f32[32,1,1536]{2,1,0:T(1,128)}), f32[32,1,1536]{2,1,0:T(1,128)S(1)}, u32[]{:S(2)}, u32[]{:S(2)}) async-start(f32[32,1,1536]{2,1,0:T(1,128)} %broadcast_in_dim.15), calls=%async_computation.4 | async-start | bytes 393216 | tf_op jit(solution)/shard_map/all_to_all | solution.py:291
  227.9 1.3 copy-start.13

commit v7 on v6

--- a/solution.py
+++ b/solution.py
@@ -134,6 +134,12 @@
     back[...] = lax.dot_general(grads, both_down, (((1,), (1,)), ((), ())), preferred_element_type=F32).astype(BF16)
 
 
+def keeper_low(act, up, low):
+    count, width = act.shape[0], low.shape[1]
+    branch = jnp.dot(act[...], up[...].reshape(act.shape[1], width), preferred_element_type=F32)
+    low[...] = branch.reshape(count // BLOCK, BLOCK, width)[:, :HALF].reshape(low.shape).astype(BF16)
+
+
 def sum_last_rows(back, out):
     row = lax.broadcasted_iota(jnp.int32, (out.shape[0], back.shape[0]), 1)
     last = jnp.where(row % HALF == HALF - 1, 1.0, 0.0).astype(BF16)
@@ -173,7 +179,7 @@
 
 
 def sum_gradients(
-    numbers, back, cot, summed, gain, left, own, right, act, up, total, low, high, sums, cells, frames_grad, inv
+    numbers, back, cot, summed, gain, left, own, right, act, up, total, high, sums, cells, frames_grad, inv
 ):
     frames, width = cot.shape
     gather = gather_matrix(segments(numbers), back.shape[0], frames)
@@ -221,7 +227,6 @@
     branch = jnp.dot(act[...], both_up, preferred_element_type=F32)
     branch = branch + jnp.dot(last, sums[...].astype(BF16), preferred_element_type=F32)
     branch = branch.reshape(blocks, BLOCK, width)
-    low[...] = branch[:, :HALF].reshape(low.shape).astype(BF16)
     high[...] = branch[:, HALF:].reshape(high.shape).astype(BF16)
 
 
@@ -341,14 +346,15 @@
         pair_grads, [(piece, F32), (piece, BF16)], [place, ("v", chips[0])] + [("v", part) for part in got]
     )
     grad_back, kept, given = lax.optimization_barrier((grad_back, kept, given))
-    total, low, high = call(
+    total, high = call(
         sum_gradients,
-        [((frames, width), F32), ((rows // 2, width), BF16), ((rows // 2, width), BF16)],
+        [((frames, width), F32), ((rows // 2, width), BF16)],
         where
         + [("v", grad_back), ("v", cot), ("v", summed), ("v", gain)]
         + [("v", left), ("v", own), ("v", right), ("v", act), ("v", adapt_up)],
         [((ctx, width), F32), ((frames + 2 * EDGE, width), F32), ((frames, width), F32), ((frames, LANES), F32)],
     )
+    (low,) = call(keeper_low, [((rows // 2, width), BF16)], [("v", act), ("v", adapt_up)])
     high_back = swap(high, "ctx")
     (got,) = exchanged([kept, given], "dp", 8)
     grad_down, grad_up = call(

time: 240 us -> 240 us (level)
    pallas_call x10 -> x11, Pallas kernels: 26.5 us -> 27.1 us  [call(): pl.pallas_call(body, out_shape=tuple((jax.ShapeDtypeStruct(shape, kind) f...]
    unnamed x45 -> x47, local copies, waits for them, and re-layouts: 11.7 us -> 12 us
  transfers between devices with their start and end apart: 13 -> 13, of which waited for: 7 -> 8; matrix products, arithmetic and copies ran while one was open for 1% -> 1% of each run, Pallas kernels for 4% -> 5%
where the time goes in v7:
time: 240 us; the launch traced here: 238 us
  blocking collectives  101 us (42%)
  starting transfers between devices  65.3 us (27%)
  waiting for transfers between devices  27.2 us (11%)
  Pallas kernels  27.1 us (11%)
  local copies, waits for them, and re-layouts  15.9 us (7%)
    all_to_all x1, blocking collectives, swap(): return lax.all_to_all(cells, axis, split_axis=0, concat_axis=0, tiled=True)  81.7 us
    all_to_all x4, starting transfers between devices, swap(): return lax.all_to_all(cells, axis, split_axis=0, concat_axis=0, tiled=True)  33.9 us
    pallas_call x11, Pallas kernels, call(): pl.pallas_call(body, out_shape=tuple((jax.ShapeDtypeStruct(shape, kind) f...  27.1 us
    ppermute x5, starting transfers between devices, exchanged(): lax.ppermute(block, axis, [(i, i ^ turn * unit) for i in range(count)])  20.9 us
    all_gather x1, blocking collectives, local(): mine = lax.all_gather(mine[:1], 'dp', axis=0, tiled=True)  19.3 us
    ppermute x5, waiting for transfers between devices, exchanged(): lax.ppermute(block, axis, [(i, i ^ turn * unit) for i in range(count)])  12.9 us
    unnamed x47, local copies, waits for them, and re-layouts  12 us
    ppermute x2, starting transfers between devices, from_sides(): left = lax.ppermute(tail, axis, [(i, i + 1) for i in range(count - 1)])  7.95 us
  transfers between devices with their start and end apart: 13, of which 8 were waited for; matrix products, arithmetic and copies ran while one was open for 1% of the time, Pallas kernels for 5%

profile of v7, /device:TPU:1, one launch (start us, length us, event | category | flops | bytes accessed | tf_op | source)
XLA Modules:
  0.0 238.2 jit_solution(9401185485825869684)
XLA Ops:
  0.6 0.8 slice_bitcast_fusion
  1.5 4.8 %collective-permute-start = (bf16[16,1536]{1,0:T(8,128)(2,1)S(1)}, bf16[16,1536]{1,0:T(8,128)(2,1)S(1)}, u32[]{:S(2)}, u32[]{:S(2)}) collective-permute-start(bf16[16,1536]{1,0:T(8,128)(2,1)S(1)} %get-tuple-element.61), channel_id=1, source_target_pairs={{0,1},{1,2},{2,3},{3,4},{4,5},{5,6},{6,7},{7,8},{8,9},{9,10},{10,1... | collective-permute-start | bytes 147464 | tf_op jit(solution)/shard_map/ppermute | solution.py:282
  6.3 1.3 collective-permute-start.1
  7.6 0.8 pad_add_fusion.numbers
  8.4 0.7 reshape.45.gain
  9.1 2.7 %collective-permute-done.1.right = bf16[16,1536]{1,0:T(8,128)(2,1)S(1)} collective-permute-done((bf16[16,1536]{1,0:T(8,128)(2,1)S(1)}, bf16[16,1536]{1,0:T(8,128)(2,1)S(1)}, u32[]{:S(2)}, u32[]{:S(2)}) %collective-permute-start.1) | collective-permute-done | bytes 49184 | tf_op jit(solution)/shard_map/ppermute | solution.py:283
  11.8 1.1 copy-done.8
  12.8 1.1 copy-done.10
  13.9 0.9 copy-done.18
  14.8 5.7 %shard_map.136 = (bf16[32,32,1536]{2,1,0:T(8,128)(2,1)S(1)}, f32[192,1536]{1,0:T(8,128)S(1)}) custom-call(s32[96]{0:T(128)S(1)} %pad_add_fusion.numbers, bf16[16,1536]{1,0:T(8,128)(2,1)S(1)} %collective-permute-done.left, bf16[192,1536]{1,0:T(8,128)(2,1)S(1)} %bitcast.30, bf16[16,1536]{1,0:T(8,128)(2,1)S(1)} %collective-permute-done.1.right, ...), custom_call_target="tpu_custom_call" | custom-call | tf_op jit(solution)/shard_map/pallas_call | solution.py:24
  20.6 81.7 %all_to_all.46.got = bf16[32,32,1536]{2,1,0:T(8,128)(2,1)S(1)} all-to-all(bf16[32,32,1536]{2,1,0:T(8,128)(2,1)S(1)} %get-tuple-element.32), channel_id=1, replica_groups=mesh['dp'=16,'ctx'=32] {'ctx'}, dimensions={0} | all-to-all | bytes 6291456 | tf_op jit(solution)/shard_map/all_to_all | solution.py:296
  102.3 1.4 shard_map.137
  103.7 1.1 copy-done.3
  104.9 8.3 %all-to-all-start.1 = ((bf16[32,16,1536]{2,1,0:T(8,128)(2,1)}), bf16[32,16,1536]{2,1,0:T(8,128)(2,1)}, u32[]{:S(2)}, u32[]{:S(2)}) async-start(bf16[32,16,1536]{2,1,0:T(8,128)(2,1)} %bitcast.28), calls=%async_computation.1 | async-start | bytes 3145728 | tf_op jit(solution)/shard_map/all_to_all | solution.py:296
  113.2 1.1 copy-done.1
  114.3 1.1 copy-done.7
  115.5 2.5 %shard_map.138 = (f32[8,192,256]{2,1,0:T(8,128)S(1)}, bf16[8,192,256]{2,1,0:T(8,128)(2,1)S(1)}, bf16[512,256]{1,0:T(8,128)(2,1)S(1)}) custom-call(s32[1]{0:T(128)} %bitcast.8.place, bf16[32,32,1536]{2,1,0:T(8,128)(2,1)S(1)} %all_to_all.46.got, bf16[2,1536,128]{2,1,0:T(8,128)(2,1)S(1)} %copy-done.7, bf16[2,128,1536]{2,1,0:T(8,128)(2,1)S(1)} %copy-done.1), custom_call_target="tpu_custom_call" | custom-call | tf_op jit(solution)/shard_map/pallas_call | solution.py:24
  118.0 4.0 %collective-permute-start.2 = (bf16[8,192,256]{2,1,0:T(8,128)(2,1)S(1)}, bf16[8,192,256]{2,1,0:T(8,128)(2,1)S(1)}, u32[]{:S(2)}, u32[]{:S(2)}) collective-permute-start(bf16[8,192,256]{2,1,0:T(8,128)(2,1)S(1)} %get-tuple-element.34), channel_id=1, source_target_pairs={{0,32},{32,0},{64,96},{96,64},{128,160},{160,128},{192,224},{224,1... | collective-permute-start | bytes 2359304 | tf_op jit(solution)/shard_map/ppermute | solution.py:290
  121.9 1.9 collective-permute-done.2.got
  124.0 3.3 %collective-permute-start.3 = (bf16[2,192,256]{2,1,0:T(8,128)(2,1)S(1)}, bf16[2,192,256]{2,1,0:T(8,128)(2,1)S(1)}, u32[]{:S(2)}, u32[]{:S(2)}) collective-permute-start(bf16[2,192,256]{2,1,0:T(8,128)(2,1)S(1)} %get-tuple-element.36), channel_id=1, source_target_pairs={{0,64},{32,96},{64,0},{96,32},{128,192},{160,224},{192,128},{224,1... | collective-permute-start | bytes 589832 | tf_op jit(solution)/shard_map/ppermute | solution.py:290
  127.3 4.2 %collective-permute-start.4 = (bf16[2,192,256]{2,1,0:T(8,128)(2,1)S(1)}, bf16[2,192,256]{2,1,0:T(8,128)(2,1)S(1)}, u32[]{:S(2)}, u32[]{:S(2)}) collective-permute-start(bf16[2,192,256]{2,1,0:T(8,128)(2,1)S(1)} %get-tuple-element.37), channel_id=1, source_target_pairs={{0,128},{32,160},{64,192},{96,224},{128,0},{160,32},{192,64},{224,... | collective-permute-start | bytes 589832 | tf_op jit(solution)/shard_map/ppermute | solution.py:290
  131.6 1.9 collective-permute-start.5
  133.5 11.0 %collective-permute-done.4.second = bf16[2,192,256]{2,1,0:T(8,128)(2,1)S(1)} collective-permute-done((bf16[2,192,256]{2,1,0:T(8,128)(2,1)S(1)}, bf16[2,192,256]{2,1,0:T(8,128)(2,1)S(1)}, u32[]{:S(2)}, u32[]{:S(2)}) %collective-permute-start.4) | collective-permute-done | bytes 196640 | tf_op jit(solution)/shard_map/ppermute | solution.py:290
  144.7 0.7 copy-done.20
  145.3 4.6 %all-to-all-done.1 = bf16[32,16,1536]{2,1,0:T(8,128)(2,1)} async-done(((bf16[32,16,1536]{2,1,0:T(8,128)(2,1)}), bf16[32,16,1536]{2,1,0:T(8,128)(2,1)}, u32[]{:S(2)}, u32[]{:S(2)}) %all-to-all-start.1) | async-done | bytes 1572896 | tf_op jit(solution)/shard_map/all_to_all | solution.py:296
  150.0 0.9 copy-done.15
  150.9 8.1 %shard_map.141 = (f32[192,1536]{1,0:T(8,128)S(1)}, bf16[256,1536]{1,0:T(8,128)(2,1)S(1)}) custom-call(s32[96]{0:T(128)S(1)} %pad_add_fusion.numbers, bf16[512,1536]{1,0:T(8,128)(2,1)} %bitcast.7.back, bf16[192,1536]{1,0:T(8,128)(2,1)S(1)} %bitcast.33, f32[192,1536]{1,0:T(8,128)S(1)} %copy-done.5, f32[1,1536]{1,0:T(1,128)S(1)} %reshape.45.gain, ...), custom_call_target="tpu_custom_call" | custom-call | tf_op jit(solution)/shard_map/pallas_call | solution.py:24
  159.0 1.0 copy-done.12
  160.1 0.9 copy-done.17
  160.9 7.6 %all-to-all-start.2 = ((bf16[32,8,1536]{2,1,0:T(8,128)(2,1)}), bf16[32,8,1536]{2,1,0:T(8,128)(2,1)S(1)}, u32[]{:S(2)}, u32[]{:S(2)}) async-start(bf16[32,8,1536]{2,1,0:T(8,128)(2,1)} %bitcast.34), calls=%async_computation.2 | async-start | bytes 1572864 | tf_op jit(solution)/shard_map/all_to_all | solution.py:296
  168.5 7.5 %collective-permute-start.6 = (bf16[192,256]{1,0:T(8,128)(2,1)S(1)}, bf16[192,256]{1,0:T(8,128)(2,1)S(1)}, u32[]{:S(2)}, u32[]{:S(2)}) collective-permute-start(bf16[192,256]{1,0:T(8,128)(2,1)S(1)} %get-tuple-element.46), channel_id=1, source_target_pairs={{0,256},{32,288},{64,320},{96,352},{128,384},{160,416},{192,448},{... | collective-permute-start | bytes 294920 | tf_op jit(solution)/shard_map/ppermute | solution.py:290
  176.0 1.0 fusion
  177.0 3.1 %collective-permute-start.7 = (f32[16,1536]{1,0:T(8,128)S(1)}, f32[16,1536]{1,0:T(8,128)S(1)}, u32[]{:S(2)}, u32[]{:S(2)}) collective-permute-start(f32[16,1536]{1,0:T(8,128)S(1)} %get-tuple-element.59), channel_id=1, source_target_pairs={{0,1},{1,2},{2,3},{3,4},{4,5},{5,6},{6,7},{7,8},{8,9},{9,10},{10,1... | collective-permute-start | bytes 294920 | tf_op jit(solution)/shard_map/ppermute | solution.py:282
  180.1 1.3 collective-permute-start.8
  181.4 1.5 shard_map.142
  182.9 0.7 shard_map.143
  183.6 0.5 collective-permute-done.7.left
  184.0 4.8 %collective-permute-done.8.right = f32[16,1536]{1,0:T(8,128)S(1)} collective-permute-done((f32[16,1536]{1,0:T(8,128)S(1)}, f32[16,1536]{1,0:T(8,128)S(1)}, u32[]{:S(2)}, u32[]{:S(2)}) %collective-permute-start.8) | collective-permute-done | bytes 98336 | tf_op jit(solution)/shard_map/ppermute | solution.py:283
  188.9 8.8 %all-to-all-start.3 = ((bf16[32,8,1536]{2,1,0:T(8,128)(2,1)}), bf16[32,8,1536]{2,1,0:T(8,128)(2,1)S(1)}, u32[]{:S(2)}, u32[]{:S(2)}) async-start(bf16[32,8,1536]{2,1,0:T(8,128)(2,1)} %bitcast.12), calls=%async_computation.3 | async-start | bytes 1572864 | tf_op jit(solution)/shard_map/all_to_all | solution.py:296
  197.8 19.3 %all-gather = f32[16,1,1536]{2,1,0:T(1,128)S(1)} all-gather(f32[1,1,1536]{2,1,0:T(1,128)S(1)} %slice_bitcast_fusion.2), channel_id=1, replica_groups=mesh['dp'=16,'ctx'=32] {'dp'}, dimensions={0}, use_global_device_ids=true | all-gather | bytes 104448 | tf_op jit(solution)/shard_map/all_gather | solution.py:369
  217.4 0.8 broadcast_in_dim.15
  218.2 9.2 %all-to-all-start.4 = ((f32[32,1,1536]{2,1,0:T(1,128)}), f32[32,1,1536]{2,1,0:T(1,128)S(1)}, u32[]{:S(2)}, u32[]{:S(2)}) async-start(f32[32,1,1536]{2,1,0:T(1,128)} %broadcast_in_dim.15), calls=%async_computation.4 | async-start | bytes 393216 | tf_op jit(solution)/shard_map/all_to_all | solution.py:296
  227.5 1.3 copy-done.13
  228.7 4.4 %shard_map.146 = bf16[192,1536]{1,0:T(8,128)(2,1)} custom-call(f32[16,1536]{1,0:T(8,128)S(1)} %collective-permute-done.7.left, f32[192,1536]{1,0:T(8,128)S(1)} %copy-done.13, f32[16,1536]{1,0:T(8,128)S(1)} %collective-permute-done.8.right, f32[31,1536]{1,0:T(8,128)S(1)} %copy-done.19), custom_call_target="tpu_custom_call" | custom-call | tf_op jit(solution)/shard_map/pallas_call | solution.py:24
  233.1 2.4 %shard_map.145 = bf16[192,1536]{1,0:T(8,128)(2,1)} custom-call(s32[96]{0:T(128)S(1)} %pad_add_fusion.numbers, bf16[256,1536]{1,0:T(8,128)(2,1)S(1)} %bitcast.29, bf16[256,1536]{1,0:T(8,128)(2,1)S(1)} %bitcast.27, f32[192,1536]{1,0:T(8,128)S(1)} %copy-done.5), custom_call_target="tpu_custom_call" | custom-call | tf_op jit(solution)/shard_map/pallas_call | solution.py:24
  235.5 1.3 all-to-all-done.4
  236.9 0.7 copy.19
  237.6 0.6 slice_reduce_fusion
  (47 shorter events, 0.9 us)
Async XLA Ops:
  1.5 7.6 %collective-permute-start = (bf16[16,1536]{1,0:T(8,128)(2,1)S(1)}, bf16[16,1536]{1,0:T(8,128)(2,1)S(1)}, u32[]{:S(2)}, u32[]{:S(2)}) collective-permute-start(bf16[16,1536]{1,0:T(8,128)(2,1)S(1)} %get-tuple-element.61), channel_id=1, source_target_pairs={{0,1},{1,2},{2,3},{3,4},{4,5},{5,6},{6,7},{7,8},{8,9},{9,10},{10,1... | collective-permute-start | bytes 147464 | tf_op jit(solution)/shard_map/ppermute | solution.py:282
  6.3 5.5 %collective-permute-start.1 = (bf16[16,1536]{1,0:T(8,128)(2,1)S(1)}, bf16[16,1536]{1,0:T(8,128)(2,1)S(1)}, u32[]{:S(2)}, u32[]{:S(2)}) collective-permute-start(bf16[16,1536]{1,0:T(8,128)(2,1)S(1)} %get-tuple-element.60), channel_id=1, source_target_pairs={{1,0},{2,1},{3,2},{4,3},{5,4},{6,5},{7,6},{8,7},{9,8},{10,9},{11,1... | collective-permute-start | bytes 147464 | tf_op jit(solution)/shard_map/ppermute | solution.py:283
  11.8 1.1 copy-start.8
  12.8 1.1 copy-start.10
  13.9 0.9 copy-start.18
  20.5 81.7 %copy-start.4 = (f32[192,1536]{1,0:T(8,128)}, f32[192,1536]{1,0:T(8,128)S(1)}, u32[]{:S(2)}) copy-start(f32[192,1536]{1,0:T(8,128)S(1)} %get-tuple-element.42.summed) | copy-start | bytes 3538948
  20.6 81.7 %copy-start = (bf16[2,128,1536]{2,1,0:T(8,128)(2,1)S(1)}, bf16[2,128,1536]{2,1,0:T(8,128)(2,1)}, u32[]{:S(2)}) copy-start(bf16[2,128,1536]{2,1,0:T(8,128)(2,1)} %up.5) | copy-start | bytes 2359300
  20.6 81.7 %copy-start.6 = (bf16[2,1536,128]{2,1,0:T(8,128)(2,1)S(1)}, bf16[2,1536,128]{2,1,0:T(8,128)(2,1)}, u32[]{:S(2)}) copy-start(bf16[2,1536,128]{2,1,0:T(8,128)(2,1)} %down_w.1) | copy-start | bytes 2359300
  103.7 1.2 copy-start.3
  104.9 45.1 %all-to-all-start.1 = ((bf16[32,16,1536]{2,1,0:T(8,128)(2,1)}), bf16[32,16,1536]{2,1,0:T(8,128)(2,1)}, u32[]{:S(2)}, u32[]{:S(2)}) async-start(bf16[32,16,1536]{2,1,0:T(8,128)(2,1)} %bitcast.28), calls=%async_computation.1 | async-start | bytes 3145728 | tf_op jit(solution)/shard_map/all_to_all | solution.py:296
  113.2 1.1 copy-start.1
  114.3 1.1 copy-start.7
  117.9 6.0 %copy-start.14 = (bf16[512,256]{1,0:T(8,128)(2,1)}, bf16[512,256]{1,0:T(8,128)(2,1)S(1)}, u32[]{:S(2)}) copy-start(bf16[512,256]{1,0:T(8,128)(2,1)S(1)} %get-tuple-element.43.act) | copy-start | bytes 786436
  118.0 5.9 %collective-permute-start.2 = (bf16[8,192,256]{2,1,0:T(8,128)(2,1)S(1)}, bf16[8,192,256]{2,1,0:T(8,128)(2,1)S(1)}, u32[]{:S(2)}, u32[]{:S(2)}) collective-permute-start(bf16[8,192,256]{2,1,0:T(8,128)(2,1)S(1)} %get-tuple-element.34), channel_id=1, source_target_pairs={{0,32},{32,0},{64,96},{96,64},{128,160},{160,128},{192,224},{224,1... | collective-permute-start | bytes 2359304 | tf_op jit(solution)/shard_map/ppermute | solution.py:290
  123.8 26.1 %copy-start.2 = (bf16[2,128,1536]{2,1,0:T(8,128)(2,1)S(1)}, bf16[2,128,1536]{2,1,0:T(8,128)(2,1)}, u32[]{:S(2)}) copy-start(bf16[2,128,1536]{2,1,0:T(8,128)(2,1)} %up.5) | copy-start | bytes 2359300
  123.8 26.1 %copy-start.5 = (f32[192,1536]{1,0:T(8,128)S(1)}, f32[192,1536]{1,0:T(8,128)}, u32[]{:S(2)}) copy-start(f32[192,1536]{1,0:T(8,128)} %copy-done.4) | copy-start | bytes 3538948
  123.8 26.1 %copy-start.9 = (bf16[1,192,1536]{2,1,0:T(8,128)(2,1)S(1)}, bf16[1,192,1536]{2,1,0:T(8,128)(2,1)}, u32[]{:S(2)}) copy-start(bf16[1,192,1536]{2,1,0:T(8,128)(2,1)} %param.9) | copy-start | bytes 1769476
  123.8 26.1 %copy-start.11 = (bf16[1,192,1536]{2,1,0:T(8,128)(2,1)S(1)}, bf16[1,192,1536]{2,1,0:T(8,128)(2,1)}, u32[]{:S(2)}) copy-start(bf16[1,192,1536]{2,1,0:T(8,128)(2,1)} %param.10) | copy-start | bytes 1769476
  124.0 9.5 %collective-permute-start.3 = (bf16[2,192,256]{2,1,0:T(8,128)(2,1)S(1)}, bf16[2,192,256]{2,1,0:T(8,128)(2,1)S(1)}, u32[]{:S(2)}, u32[]{:S(2)}) collective-permute-start(bf16[2,192,256]{2,1,0:T(8,128)(2,1)S(1)} %get-tuple-element.36), channel_id=1, source_target_pairs={{0,64},{32,96},{64,0},{96,32},{128,192},{160,224},{192,128},{224,1... | collective-permute-start | bytes 589832 | tf_op jit(solution)/shard_map/ppermute | solution.py:290
  127.3 17.2 %collective-permute-start.4 = (bf16[2,192,256]{2,1,0:T(8,128)(2,1)S(1)}, bf16[2,192,256]{2,1,0:T(8,128)(2,1)S(1)}, u32[]{:S(2)}, u32[]{:S(2)}) collective-permute-start(bf16[2,192,256]{2,1,0:T(8,128)(2,1)S(1)} %get-tuple-element.37), channel_id=1, source_target_pairs={{0,128},{32,160},{64,192},{96,224},{128,0},{160,32},{192,64},{224,... | collective-permute-start | bytes 589832 | tf_op jit(solution)/shard_map/ppermute | solution.py:290
  131.6 13.0 %collective-permute-start.5 = (bf16[2,192,256]{2,1,0:T(8,128)(2,1)S(1)}, bf16[2,192,256]{2,1,0:T(8,128)(2,1)S(1)}, u32[]{:S(2)}, u32[]{:S(2)}) collective-permute-start(bf16[2,192,256]{2,1,0:T(8,128)(2,1)S(1)} %get-tuple-element.38), channel_id=1, source_target_pairs={{0,192},{32,224},{64,128},{96,160},{128,64},{160,96},{192,0},{224,... | collective-permute-start | bytes 589832 | tf_op jit(solution)/shard_map/ppermute | solution.py:290
  144.7 0.7 copy-start.20
  150.0 1.0 copy-start.15
  159.0 1.0 copy-start.12
  160.1 0.9 copy-start.17
  160.1 21.3 %copy-start.16 = (bf16[512,256]{1,0:T(8,128)(2,1)S(1)}, bf16[512,256]{1,0:T(8,128)(2,1)}, u32[]{:S(2)}) copy-start(bf16[512,256]{1,0:T(8,128)(2,1)} %copy-done.14) | copy-start | bytes 786436
  160.9 21.9 %copy-start.21 = (f32[192,256]{1,0:T(8,128)S(1)}, f32[192,256]{1,0:T(8,128)}, u32[]{:S(2)}) copy-start(f32[192,256]{1,0:T(8,128)} %copy-done.20) | copy-start | bytes 589828
  160.9 27.9 %all-to-all-start.2 = ((bf16[32,8,1536]{2,1,0:T(8,128)(2,1)}), bf16[32,8,1536]{2,1,0:T(8,128)(2,1)S(1)}, u32[]{:S(2)}, u32[]{:S(2)}) async-start(bf16[32,8,1536]{2,1,0:T(8,128)(2,1)} %bitcast.34), calls=%async_computation.2 | async-start | bytes 1572864 | tf_op jit(solution)/shard_map/all_to_all | solution.py:296
  168.5 14.3 %collective-permute-start.6 = (bf16[192,256]{1,0:T(8,128)(2,1)S(1)}, bf16[192,256]{1,0:T(8,128)(2,1)S(1)}, u32[]{:S(2)}, u32[]{:S(2)}) collective-permute-start(bf16[192,256]{1,0:T(8,128)(2,1)S(1)} %get-tuple-element.46), channel_id=1, source_target_pairs={{0,256},{32,288},{64,320},{96,352},{128,384},{160,416},{192,448},{... | collective-permute-start | bytes 294920 | tf_op jit(solution)/shard_map/ppermute | solution.py:290
  177.0 7.1 %collective-permute-start.7 = (f32[16,1536]{1,0:T(8,128)S(1)}, f32[16,1536]{1,0:T(8,128)S(1)}, u32[]{:S(2)}, u32[]{:S(2)}) collective-permute-start(f32[16,1536]{1,0:T(8,128)S(1)} %get-tuple-element.59), channel_id=1, source_target_pairs={{0,1},{1,2},{2,3},{3,4},{4,5},{5,6},{6,7},{7,8},{8,9},{9,10},{10,1... | collective-permute-start | bytes 294920 | tf_op jit(solution)/shard_map/ppermute | solution.py:282
  180.1 8.8 %collective-permute-start.8 = (f32[16,1536]{1,0:T(8,128)S(1)}, f32[16,1536]{1,0:T(8,128)S(1)}, u32[]{:S(2)}, u32[]{:S(2)}) collective-permute-start(f32[16,1536]{1,0:T(8,128)S(1)} %get-tuple-element.58), channel_id=1, source_target_pairs={{1,0},{2,1},{3,2},{4,3},{5,4},{6,5},{7,6},{8,7},{9,8},{10,9},{11,1... | collective-permute-start | bytes 294920 | tf_op jit(solution)/shard_map/ppermute | solution.py:283
  188.9 38.6 %copy-start.19 = (f32[31,1536]{1,0:T(8,128)S(1)}, f32[31,1536]{1,0:T(8,128)}, u32[]{:S(2)}) copy-start(f32[31,1536]{1,0:T(8,128)} %taps.3) | copy-start | bytes 571396
  188.9 28.5 %all-to-all-start.3 = ((bf16[32,8,1536]{2,1,0:T(8,128)(2,1)}), bf16[32,8,1536]{2,1,0:T(8,128)(2,1)S(1)}, u32[]{:S(2)}, u32[]{:S(2)}) async-start(bf16[32,8,1536]{2,1,0:T(8,128)(2,1)} %bitcast.12), calls=%async_computation.3 | async-start | bytes 1572864 | tf_op jit(solution)/shard_map/all_to_all | solution.py:296
  218.2 18.6 %all-to-all-start.4 = ((f32[32,1,1536]{2,1,0:T(1,128)}), f32[32,1,1536]{2,1,0:T(1,128)S(1)}, u32[]{:S(2)}, u32[]{:S(2)}) async-start(f32[32,1,1536]{2,1,0:T(1,128)} %broadcast_in_dim.15), calls=%async_computation.4 | async-start | bytes 393216 | tf_op jit(solution)/shard_map/all_to_all | solution.py:296
  227.5 1.3 copy-start.13
